TPU v7x, 32 devices: a whole 2x2x4 slice. The times are simulated.
32 devices in a mesh: fsdp: 8 (over z, y), mem: 4 (over x, core).
Axes of the slice: x: 2, y: 2, z: 4, core: 2. Of those that a mesh axis runs over, the one named last changes fastest.
Arguments:
- suffix: bfloat16 [256, 32, 768], P('fsdp'), may hold values from -6 to 6
- memory: bfloat16 [256, 256, 768], P('fsdp', 'mem'), may hold values from -6 to 6
- counts: int32 [256], P('fsdp'), may hold values from 0 to 256, as said below
- cotangent: bfloat16 [256, 32, 768], P('fsdp'), may hold values from -6 to 6
- self_norm_gain: bfloat16 [768], P('fsdp'), may hold values from 0.5 to 1.5
- self_norm_bias: bfloat16 [768], P('fsdp'), may hold values from -1.5 to 1.5
- self_query: bfloat16 [768, 768], P('fsdp'), may hold values from -0.21875 to 0.21875
- self_key: bfloat16 [768, 768], P('fsdp'), may hold values from -0.21875 to 0.21875
- self_value: bfloat16 [768, 768], P('fsdp'), may hold values from -0.21875 to 0.21875
- self_output: bfloat16 [768, 768], P('fsdp'), may hold values from -0.4375 to 0.4375
- cross_norm_gain: bfloat16 [768], P('fsdp'), may hold values from 0.5 to 1.5
- cross_norm_bias: bfloat16 [768], P('fsdp'), may hold values from -1.5 to 1.5
- cross_query: bfloat16 [768, 768], P('fsdp'), may hold values from -0.21875 to 0.21875
- cross_key: bfloat16 [768, 768], P('fsdp'), may hold values from -0.21875 to 0.21875
- cross_value: bfloat16 [768, 768], P('fsdp'), may hold values from -0.21875 to 0.21875
- cross_output: bfloat16 [768, 768], P('fsdp'), may hold values from -1.25 to 1.25
- dense_norm_gain: bfloat16 [768], P('fsdp'), may hold values from 0.5 to 1.5
- dense_norm_bias: bfloat16 [768], P('fsdp'), may hold values from -1.5 to 1.5
- dense_in: bfloat16 [768, 3072], P('fsdp'), may hold values from -0.21875 to 0.21875
- dense_in_bias: bfloat16 [3072], P('fsdp'), may hold values from -2.5 to 2.5
- dense_out: bfloat16 [3072, 768], P('fsdp'), may hold values from -0.109375 to 0.109375
- dense_out_bias: bfloat16 [768], P('fsdp'), may hold values from -2.5 to 2.5
Outputs:
- block_output: bfloat16 [256, 32, 768], P('fsdp')
- suffix_grad: bfloat16 [256, 32, 768], P('fsdp')
- memory_grad: bfloat16 [256, 256, 768], P('fsdp', 'mem')
- self_norm_gain_grad: float32 [768], P('fsdp')
- self_norm_bias_grad: float32 [768], P('fsdp')
- self_query_grad: float32 [768, 768], P('fsdp')
- self_key_grad: float32 [768, 768], P('fsdp')
- self_value_grad: float32 [768, 768], P('fsdp')
- self_output_grad: float32 [768, 768], P('fsdp')
- cross_norm_gain_grad: float32 [768], P('fsdp')
- cross_norm_bias_grad: float32 [768], P('fsdp')
- cross_query_grad: float32 [768, 768], P('fsdp')
- cross_key_grad: float32 [768, 768], P('fsdp')
- cross_value_grad: float32 [768, 768], P('fsdp')
- cross_output_grad: float32 [768, 768], P('fsdp')
- dense_norm_gain_grad: float32 [768], P('fsdp')
- dense_norm_bias_grad: float32 [768], P('fsdp')
- dense_in_grad: float32 [768, 3072], P('fsdp')
- dense_in_bias_grad: float32 [3072], P('fsdp')
- dense_out_grad: float32 [3072, 768], P('fsdp')
- dense_out_bias_grad: float32 [768], P('fsdp')
Inputs may be any that keep to these rules, and one draw needn't show every extreme that they name: memory slots that an example may read are its first counts ones; in every aligned group of 32 examples one example has 256 and another has none.
All inputs are finite; a program needn't handle non-finite values.
Results may differ from a plain program's by a relative error of at most 0.019.
Values may be sent and summed in bfloat16 or wider, within the bound.
No kernel may reach another device: no remote copies, remote signals or barrier semaphores. Data moves between devices by JAX's collectives and lax.ppermute only.
A program may use at most 256 MiB of HBM per device.

v0:
```python
import functools

import jax
import jax.numpy as jnp
from jax import lax
from jax.experimental import pallas as pl
from jax.experimental.pallas import tpu as pltpu
from jax.sharding import PartitionSpec as P

HEADS = 12
HEAD = 64
TOGETHER = 4
GROUPS = HEADS // TOGETHER
LANES = TOGETHER * HEAD
SCALE = HEAD ** (-0.5)
BF = jnp.bfloat16
F32 = jnp.float32
ANY = pl.BlockSpec(memory_space=pl.ANY)
SMEM = pl.BlockSpec(memory_space=pltpu.SMEM)
VMEM = pl.BlockSpec(memory_space=pltpu.VMEM)


def swap(value, axis, distance):
    size = lax.axis_size(axis)
    return lax.ppermute(value, axis, [(i, i ^ distance) for i in range(size)])


def after(value, *others):
    return lax.optimization_barrier((value, *others))[0] if others else value


def fsdp_split(size):
    slow = 4 if size % 4 == 0 else 1
    return slow, size // slow


def dot(left, right):
    return jnp.dot(left, right, preferred_element_type=F32)


def dot_nt(left, right):
    return lax.dot_general(left, right, (((1,), (1,)), ((), ())), preferred_element_type=F32)


def dot_tn(left, right):
    return lax.dot_general(left, right, (((0,), (0,)), ((), ())), preferred_element_type=F32)


def rows_of(start, size):
    return pl.ds(pl.multiple_of(start, 16), size)


def block(ref, by_rows, shard, which):
    if by_rows:
        return ref.at[shard, pl.ds(which * 2, 2)]
    rows = ref.shape[1] // SHARDS[0]
    return ref.at[pl.ds(which * 2, 2), rows_of(shard * rows, rows)]


SHARDS = [0]


class Copies:
    def __init__(self, sems):
        self.sems = sems
        self.next = 0

    def start(self, source, target):
        copy = pltpu.make_async_copy(source, target, self.sems.at[self.next])
        self.next += 1
        copy.start()
        return copy


def wait_all(copies):
    for copy in copies:
        copy.wait()


def load_weight(where, whole, weights, copies, by_rows=False):
    z, y, c = where[0], where[1], where[2]
    rows = whole.shape[2] if by_rows else whole.shape[1] // SHARDS[0]
    started = []
    for which, pieces in ((c, weights[0]), (1 - c, weights[1])):
        fast = len(pieces)
        for b, piece in enumerate(pieces):
            for k in range(piece.shape[0]):
                shard = (z ^ k) * fast + (y ^ b)
                for i in range(2):
                    source = piece.at[k, pl.ds(i * rows, rows)]
                    if by_rows:
                        target = whole.at[shard, 2 * which + i]
                    else:
                        target = whole.at[2 * which + i, rows_of(shard * rows, rows)]
                    started.append(copies.start(source, target))
    return started


def store_grad(where, whole, near, far, theirs, copies, by_rows=False):
    y, c = where[1], where[2]
    slow, cut = near.shape[0], near.shape[0] // 2
    fast = (len(theirs) + 1) // 2
    started = []
    for b in range(fast):
        for k in range(slow):
            shard = k * fast + (y ^ b)
            mine = far.at[b - 1, k] if b else near.at[k]
            other = theirs[2 * b - 1 + k // cut].at[k % cut] if b else theirs[0].at[k]
            started.append(copies.start(block(whole, by_rows, shard, 1 - c), other))
            started.append(copies.start(block(whole, by_rows, shard, c), mine))
    return started


def my_examples(where, source, target, copies):
    count = target.shape[0]
    return copies.start(source.at[pl.ds(where[3] * count, count)], target)


def normalise(values):
    centred = values - jnp.mean(values, axis=-1, keepdims=True)
    scale = lax.rsqrt(jnp.mean(centred * centred, axis=-1, keepdims=True) + 1e-06)
    return centred * scale, scale


def norm_back(grad, gain, hat, scale):
    inner = grad * gain
    mean = jnp.mean(inner, axis=-1, keepdims=True)
    along = jnp.mean(inner * hat, axis=-1, keepdims=True)
    return (
        scale * (inner - mean - hat * along),
        jnp.sum(grad * hat, axis=0, keepdims=True),
        jnp.sum(grad, axis=0, keepdims=True),
    )


def head_mask(rows):
    shape = (TOGETHER * rows, LANES)
    row = lax.broadcasted_iota(jnp.int32, shape, 0) // rows
    lane = lax.broadcasted_iota(jnp.int32, shape, 1) // HEAD
    return (row == lane).astype(F32)


def stack_heads(value, mask):
    return (jnp.concatenate([value] * TOGETHER, axis=0).astype(F32) * mask).astype(BF)


def merge_heads(value, mask):
    rows = value.shape[0] // TOGETHER
    value = value * mask
    total = value[:rows]
    for h in range(1, TOGETHER):
        total = total + value[h * rows : (h + 1) * rows]
    return total


def columns(j, width):
    return slice(j * width, (j + 1) * width)


def self_forward(
    group, where, suffix, weights, x1, a1, qkv, p1, o1, vec, weight, start, small, sems
):
    rows, width = x1.shape
    copies = Copies(sems)
    first = my_examples(where, suffix, start, copies)
    fast, slow = len(weights[0]), weights[0][0].shape[0]
    part = width // (fast * slow)
    vectors = []
    for b, piece in enumerate(weights[0]):
        for k in range(slow):
            source = piece.at[k, pl.ds(2 * part, 16), pl.ds(0, 128)]
            vectors.append(copies.start(source, small.at[b * slow + k]))
    loads = load_weight(where, weight, weights, copies)
    wait_all(vectors)
    lane = lax.broadcasted_iota(jnp.int32, (128, width), 0)
    place = lax.broadcasted_iota(jnp.int32, (128, width), 1) - lane
    together = jnp.zeros(vec.shape, F32)
    for i in range(fast * slow):
        shard = (where[0] ^ (i % slow)) * fast + (where[1] ^ (i // slow))
        chosen = ((place == shard * part) & (lane < part)).astype(F32).astype(BF)
        together = together + dot(small[i], chosen)
    vec[...] = together
    first.wait()
    values = start[...].reshape(rows, width).astype(F32)
    hat, _ = normalise(values)
    a1[...] = (hat * vec[0:1, :] + vec[1:2, :]).astype(BF)
    wait_all(loads)
    for j in range(3):
        qkv[:, columns(j, width)] = dot(a1[...], weight[j]).astype(BF)
    mask = head_mask(group)
    length = suffix.shape[1]
    shape = (TOGETHER * group, group)
    row = lax.broadcasted_iota(jnp.int32, shape, 0) % group
    col = lax.broadcasted_iota(jnp.int32, shape, 1)
    seen = (row // length == col // length) & (row >= col)
    for r in range(rows // group):
        here = columns(r, group)
        for g in range(GROUPS):
            lanes = [slice(i * width + g * LANES, i * width + (g + 1) * LANES) for i in range(3)]
            queries = stack_heads(qkv[here, lanes[0]], mask)
            scores = dot_nt(queries, qkv[here, lanes[1]]) * SCALE
            scores = jnp.where(seen, scores, -1e30)
            powers = jnp.exp(scores - jnp.max(scores, axis=-1, keepdims=True))
            probs = (powers / jnp.sum(powers, axis=-1, keepdims=True)).astype(BF)
            p1[r * GROUPS + g] = probs
            found = dot(probs, qkv[here, lanes[2]])
            o1[here, lanes[0]] = merge_heads(found, mask).astype(BF)
    x1[...] = values + dot(o1[...], weight[3])


def cross_forward(
    where, counts, x1, vec, memory, weights, x2, a2, q2, kv, p2, o2, weight, sems
):
    rows, width = x1.shape
    per = kv.shape[0]
    step = pl.program_id(0)
    total = kv.shape[1]
    length = p2.shape[2] // TOGETHER

    @pl.when(step == 0)
    def _():
        loads = load_weight(where, weight, weights, Copies(sems))
        hat, _ = normalise(x1[...])
        a2[...] = (hat * vec[2:3, :] + vec[3:4, :]).astype(BF)
        wait_all(loads)
        q2[...] = dot(a2[...], weight[0]).astype(BF)

    for i in range(per):
        tokens = memory[:, i].reshape(total, width)
        for j in range(2):
            kv[i, :, columns(j, width)] = dot(tokens, weight[1 + j]).astype(BF)
    mask = head_mask(length)
    position = lax.broadcasted_iota(jnp.int32, (1, total), 1)
    probs = {}
    for i in range(per):
        e = step * per + i
        valid = position < counts[where[3] * (pl.num_programs(0) * per) + e]
        here = rows_of(e * length, length)
        for g in range(GROUPS):
            lanes = columns(g, LANES)
            queries = stack_heads(q2[here, lanes], mask)
            scores = dot_nt(queries, kv[i, :, lanes]) * SCALE
            scores = jnp.where(valid, scores, -1e30)
            top = jnp.maximum(jnp.max(scores, axis=-1, keepdims=True), 0.0)
            powers = jnp.exp(scores - top)
            weight_sum = jnp.sum(powers, axis=-1, keepdims=True) + jnp.exp(-top)
            probs[i, g] = (powers / weight_sum).astype(BF)
    for i in range(per):
        here = rows_of((step * per + i) * length, length)
        for g in range(GROUPS):
            p2[i, g] = probs[i, g]
            found = dot(probs[i, g], kv[i, :, width + g * LANES : width + (g + 1) * LANES])
            o2[here, columns(g, LANES)] = merge_heads(found, mask).astype(BF)

    @pl.when(step == pl.num_programs(0) - 1)
    def _():
        x2[...] = x1[...] + dot(o2[...], weight[3])


def dense_inner(
    where, x2, vec, bias, cotangent, weights, a3, h, slope, near, far, theirs,
    weight, grad, cot, sems,
):
    rows, width = x2.shape
    copies = Copies(sems)
    cot_copy = my_examples(where, cotangent, cot, copies)
    loads = load_weight(where, weight, weights, copies)
    hat, _ = normalise(x2[...])
    a3[...] = (hat * vec[4:5, :] + vec[5:6, :]).astype(BF)
    cot_copy.wait()
    gy = cot[...].reshape(rows, width)
    wait_all(loads)
    flat = grad.shape[0] * grad.shape[1] * grad.shape[2]
    step = flat // grad.shape[0]
    for j in range(4):
        for half in range(2):
            cols = slice(j * width + half * 384, j * width + (half + 1) * 384)
            u = dot(a3[...], weight[j, :, half * 384 : (half + 1) * 384]) + bias[:, cols]
            square = u * u
            t = jnp.tanh(0.7978845608 * u * (1.0 + 0.044715 * square))
            h[:, cols] = (0.5 * u * (1.0 + t)).astype(BF)
            slope[:, cols] = (
                0.5 * (1.0 + t)
                + (0.5 * 0.7978845608) * u * (1.0 - t * t) * (1.0 + (3.0 * 0.044715) * square)
            ).astype(BF)
            part = dot_tn(h[:, cols], gy).astype(BF)
            per = 384 // step
            grad[cols.start // step : cols.start // step + per] = part.reshape(
                (per,) + grad.shape[1:]
            )
    wait_all(store_grad(where, grad, near, far, theirs, Copies(sems), True))


def dense_outer(
    where, x2, vec, a3, h, slope, cotangent, weights, y, du, vecs, bias_grad, near, far, theirs,
    weight, grad, cot, sems,
):
    rows, width = x2.shape
    copies = Copies(sems)
    cot_copy = my_examples(where, cotangent, cot, copies)
    wait_all(load_weight(where, weight, weights, copies, True))
    cot_copy.wait()
    gy = cot[...].reshape(rows, width)
    shards = weight.shape[0]
    step = weight.shape[1] * weight.shape[2]
    whole = weight[...].reshape(shards * step, width)
    for j in range(4):
        cols = columns(j, width)
        low = (dot_nt(gy, whole[cols]) * slope[:, cols].astype(F32)).astype(BF)
        du[:, cols] = low
        bias_grad[:, cols] = jnp.sum(low.astype(F32), axis=0, keepdims=True)
        grad[j] = dot_tn(a3[...], low).astype(BF)
    started = store_grad(where, grad, near, far, theirs, Copies(sems))
    result = x2[...] + dot(h[...], whole) + vec[6:7, :]
    y[...] = result.astype(BF).reshape(y.shape)
    vecs[...] = jnp.sum(gy.astype(F32), axis=0, keepdims=True)
    wait_all(started)


def dense_back(where, x2, vec, du, cotangent, weights, gx2, vecs, weight, cot, sems):
    rows, width = x2.shape
    copies = Copies(sems)
    cot_copy = my_examples(where, cotangent, cot, copies)
    loads = load_weight(where, weight, weights, copies)
    hat, scale = normalise(x2[...])
    cot_copy.wait()
    wait_all(loads)
    da3 = dot_nt(du[:, columns(0, width)], weight[0])
    for j in range(1, 4):
        da3 = da3 + dot_nt(du[:, columns(j, width)], weight[j])
    back, gain_grad, shift_grad = norm_back(da3, vec[4:5, :], hat, scale)
    gx2[...] = cot[...].reshape(rows, width).astype(F32) + back
    vecs[0:1, :] = gain_grad
    vecs[1:2, :] = shift_grad


def cross_backward(
    where, x1, vec, gx2, q2, kv, p2, weights, gx1, vecs, dkv, dq2, out_mem, weight, do2, moved, sems
):
    rows, width = x1.shape
    per, total = kv.shape[0], kv.shape[1]
    step = pl.program_id(0)
    length = p2.shape[2] // TOGETHER

    @pl.when(step == 0)
    def _():
        wait_all(load_weight(where, weight, weights, Copies(sems)))
        do2[...] = dot_nt(gx2[...].astype(BF), weight[3]).astype(BF)

    mask = head_mask(length)
    pairs = [(i, g) for i in range(per) for g in range(GROUPS)]
    queries, grads, dz = {}, {}, {}
    for i, g in pairs:
        here = rows_of((step * per + i) * length, length)
        lanes = columns(g, LANES)
        queries[i, g] = stack_heads(q2[here, lanes], mask)
        grads[i, g] = stack_heads(do2[here, lanes], mask)
        dp = dot_nt(grads[i, g], kv[i, :, width + g * LANES : width + (g + 1) * LANES])
        wide = p2[i, g].astype(F32)
        row_sum = jnp.sum(wide * dp, axis=-1, keepdims=True)
        dz[i, g] = (wide * (dp - row_sum)).astype(BF)
    for i, g in pairs:
        here = rows_of((step * per + i) * length, length)
        lanes = columns(g, LANES)
        value_lanes = slice(width + g * LANES, width + (g + 1) * LANES)
        dkv[i, :, value_lanes] = dot_tn(p2[i, g], grads[i, g]).astype(BF)
        dkv[i, :, lanes] = (dot_tn(dz[i, g], queries[i, g]) * SCALE).astype(BF)
        dq = merge_heads(dot(dz[i, g], kv[i, :, lanes]), mask) * SCALE
        dq2[here, lanes] = dq.astype(BF)
    for i in range(per):
        back = dot_nt(dkv[i, :, :width], weight[1]) + dot_nt(dkv[i, :, width:], weight[2])
        moved[i] = back.astype(BF)
        for d, out in enumerate(out_mem):
            slots = out.shape[1]
            out[i] = moved[i, rows_of((where[3] ^ d) * slots, slots), :]

    @pl.when(step == pl.num_programs(0) - 1)
    def _():
        hat, scale = normalise(x1[...])
        back, gain_grad, shift_grad = norm_back(
            dot_nt(dq2[...], weight[0]), vec[2:3, :], hat, scale
        )
        gx1[...] = gx2[...] + back
        vecs[0:1, :] = gain_grad
        vecs[1:2, :] = shift_grad


def cross_grads(
    where, gx2, a2, o2, dq2, dkv, all_memory, near, far, theirs, grad, turned, memory, sems
):
    rows, width = gx2.shape
    mem, examples, slots, _ = all_memory.shape
    half = pl.program_id(0)
    tokens = mem * examples * slots

    @pl.when(half == 0)
    def _():
        copies = Copies(sems)
        loads = [
            copies.start(all_memory.at[d], memory.at[:, d * slots : (d + 1) * slots, :])
            for d in range(mem)
        ]
        grad[0] = dot_tn(a2[...], dq2[...]).astype(BF)
        grad[3] = dot_tn(o2[...], gx2[...].astype(BF)).astype(BF)
        wait_all(loads)
        turned[...] = memory[...].reshape(tokens, width).T

    grad[1 + half] = dot(turned[...], dkv[...].reshape(tokens, width)).astype(BF)

    @pl.when(half == 1)
    def _():
        wait_all(store_grad(where, grad, near, far, theirs, Copies(sems)))


def self_backward(
    group, where, suffix, vec, gx1, a1, qkv, p1, o1, parts, weights, suffix_grad, vecs,
    near, far, theirs, weight, start, grad, dqkv, do1, sems,
):
    rows, width = gx1.shape
    copies = Copies(sems)
    start_copy = my_examples(where, suffix, start, copies)
    loads = load_weight(where, weight, weights, copies)
    gs = gx1[...].astype(BF)
    grad[3] = dot_tn(o1[...], gs).astype(BF)
    wait_all(loads)
    do1[...] = dot_nt(gs, weight[3]).astype(BF)
    mask = head_mask(group)
    for r in range(rows // group):
        here = columns(r, group)
        for g in range(GROUPS):
            lanes = [slice(i * width + g * LANES, i * width + (g + 1) * LANES) for i in range(3)]
            queries = stack_heads(qkv[here, lanes[0]], mask)
            grads = stack_heads(do1[here, lanes[0]], mask)
            probs = p1[r * GROUPS + g]
            dp = dot_nt(grads, qkv[here, lanes[2]])
            wide = probs.astype(F32)
            row_sum = jnp.sum(wide * dp, axis=-1, keepdims=True)
            dz = (wide * (dp - row_sum)).astype(BF)
            dqkv[here, lanes[2]] = dot_tn(probs, grads).astype(BF)
            dqkv[here, lanes[1]] = (dot_tn(dz, queries) * SCALE).astype(BF)
            dq = merge_heads(dot(dz, qkv[here, lanes[1]]), mask) * SCALE
            dqkv[here, lanes[0]] = dq.astype(BF)
    for j in range(3):
        grad[j] = dot_tn(a1[...], dqkv[:, columns(j, width)]).astype(BF)
    start_copy.wait()
    started = store_grad(where, grad, near, far, theirs, Copies(sems))
    da1 = dot_nt(dqkv[:, columns(0, width)], weight[0])
    for j in range(1, 3):
        da1 = da1 + dot_nt(dqkv[:, columns(j, width)], weight[j])
    hat, scale = normalise(start[...].reshape(rows, width).astype(F32))
    back, gain_grad, shift_grad = norm_back(da1, vec[0:1, :], hat, scale)
    suffix_grad[...] = (gx1[...] + back).astype(BF).reshape(suffix_grad.shape)
    found = [gain_grad, shift_grad]
    for ref in parts:
        for r in range(ref.shape[0]):
            found += [ref[r : r + 1, columns(j, width)] for j in range(ref.shape[1] // width)]
    found.append(jnp.zeros((vecs.shape[0] - len(found), width), F32))
    vecs[...] = jnp.concatenate(found, axis=0).astype(BF)
    wait_all(started)


def run(kernel, inputs, outputs, scratch, copies, grid=()):
    def leaf(x):
        return isinstance(x, tuple) and len(x) == 2 and isinstance(x[0], pl.BlockSpec)

    flat_in, tree_in = jax.tree.flatten(inputs, is_leaf=leaf)
    flat_out, tree_out = jax.tree.flatten(outputs, is_leaf=leaf)

    def body(*refs):
        first, second = len(flat_in), len(flat_in) + len(flat_out)
        given = jax.tree.unflatten(tree_in, refs[:first])
        taken = jax.tree.unflatten(tree_out, refs[first:second])
        kernel(*given, *taken, *refs[second:])

    found = pl.pallas_call(
        body,
        grid=grid,
        in_specs=[spec for spec, _ in flat_in],
        out_specs=[spec for spec, _ in flat_out],
        out_shape=[shape for _, shape in flat_out],
        scratch_shapes=scratch + [pltpu.SemaphoreType.DMA((copies,))],
        compiler_params=pltpu.CompilerParams(vmem_limit_bytes=56 * 1024 * 1024),
        cost_estimate=pl.CostEstimate(
            flops=0, bytes_accessed=0, transcendentals=0
        ),
    )(*[x for _, x in flat_in])
    return jax.tree.unflatten(tree_out, found)


def shape_of(dims, dtype):
    return jax.ShapeDtypeStruct(tuple(dims), dtype)


def over_slow(value, slow, fast):
    groups = [[k * fast + b for k in range(slow)] for b in range(fast)]
    return lax.all_to_all(value, "fsdp", 0, 0, axis_index_groups=groups, tiled=True)


class Gather:
    def __init__(self, half, slow, fast):
        self.half, self.slow, self.fast = half, slow, fast

    def send_slow(self, *others):
        half = after(self.half, *others)
        self.came = [half] + [swap(half, "fsdp", k * self.fast) for k in range(1, self.slow)]

    def send_fast(self, *others):
        self.near = jnp.stack([after(piece, *others) for piece in self.came])
        self.near_other = swap(self.near, "mem", 1)
        self.far = [swap(self.near, "fsdp", b) for b in range(1, self.fast)]

    def whole(self):
        mine = [self.near] + self.far
        theirs = [self.near_other] + [swap(piece, "mem", 1) for piece in self.far]
        return mine, theirs

    @staticmethod
    def refs(weights):
        return [[(ANY, x) for x in some] for some in weights]


class Scatter:
    def __init__(self, grads, slow, fast, *others, vectors=None):
        self.near, self.far, theirs = grads
        self.slow, self.fast, self.vectors = slow, fast, vectors
        theirs = [after(part, *others) for part in theirs]
        far = [swap(part, "mem", 1) for part in theirs[1:]]
        far = [jnp.concatenate(far[2 * b : 2 * b + 2]) for b in range(fast - 1)]
        self.sent = [swap(theirs[0], "mem", 1)] + far
        if vectors is not None:
            self.vectors = vectors.astype(F32) + swap(vectors, "mem", 1).astype(F32)

    def add_cores(self):
        self.out = [
            (self.far[b].astype(F32) + self.sent[b + 1].astype(F32)).astype(BF)
            for b in range(self.fast - 1)
        ]
        return self.out

    def send_fast(self):
        self.came = [swap(part, "fsdp", b + 1) for b, part in enumerate(self.out)]
        if self.vectors is not None:
            low = self.vectors.astype(BF)
            self.vectors = [low] + [swap(low, "fsdp", b) for b in range(1, self.fast)]

    def add_fast(self, *others):
        if self.vectors is not None:
            self.vectors, self.came = lax.optimization_barrier((self.vectors, self.came))
            self.vectors = sum(part.astype(F32) for part in self.vectors)
        total = after(self.near, *others).astype(F32) + self.sent[0].astype(F32)
        for part in self.came:
            total = total + part.astype(F32)
        self.total = total.astype(BF).reshape(self.slow, -1, total.shape[-1])
        if self.vectors is not None:
            low = self.vectors.astype(BF)
            low = jnp.broadcast_to(low, (self.slow,) + low.shape)
            self.total = jnp.concatenate([self.total, low], axis=1)
        return self.total

    def send_slow(self):
        self.came = over_slow(self.total, self.slow, self.fast)

    def add_slow(self, *others):
        return jnp.sum(after(self.came, *others).astype(F32), axis=0)


class Replicas:
    def __init__(self, value, rows, across):
        self.rows = rows
        k = 1
        while 2 * k < across:
            low = value.astype(BF)
            value = low.astype(F32) + swap(low, "mem", 2 * k).astype(F32)
            k *= 2
        low = value.astype(BF)
        self.halves = [low, swap(low, "mem", 2 * k)] if across > 1 else [low]

    def swap_cores(self, *others):
        halves, _ = lax.optimization_barrier((self.halves, others))
        self.others = [swap(half[: 2 * self.rows], "mem", 1) for half in halves]

    def combine(self, c):
        rows = self.rows
        other = sum(half.astype(F32) for half in self.others)
        mine = sum(half.astype(F32) for half in self.halves)
        vectors, mine = mine[2 * rows :], mine[: 2 * rows]
        first = jnp.where(c == 0, mine, other)
        second = jnp.where(c == 0, other, mine)
        return [first[:rows], first[rows:], second[:rows], second[rows:]], vectors


def place_rows(where, blocks, outs, scratch, sems):
    copies = Copies(sems)
    loads = []
    for i, (even, odd) in enumerate(blocks):
        for d, piece in enumerate(even):
            loads.append((copies.start(piece, scratch.at[i, 2 * d]), i, 2 * d))
            loads.append((copies.start(odd.at[d], scratch.at[i, 2 * d + 1]), i, 2 * d + 1))
    examples = scratch.shape[2]
    stores = []
    for load, i, d in loads:
        load.wait()
        target = outs[i].at[pl.ds((where[3] ^ d) * examples, examples)]
        stores.append(copies.start(scratch.at[i, d], target))
    wait_all(stores)


def place_memory(where, pieces, out, scratch, sems):
    examples = pieces[0].shape[0]
    copies = Copies(sems)
    loads = [copies.start(piece, scratch.at[d]) for d, piece in enumerate(pieces)]
    stores = []
    for d, load in enumerate(loads):
        load.wait()
        target = out.at[pl.ds((where[3] ^ d) * examples, examples)]
        stores.append(copies.start(scratch.at[d], target))
    wait_all(stores)


def spread_across(value, mem):
    return [value] + [swap(value, "mem", d) for d in range(2, mem, 2)]


def per_device(
    suffix,
    memory,
    counts,
    cotangent,
    self_norm_gain,
    self_norm_bias,
    self_query,
    self_key,
    self_value,
    self_output,
    cross_norm_gain,
    cross_norm_bias,
    cross_query,
    cross_key,
    cross_value,
    cross_output,
    dense_norm_gain,
    dense_norm_bias,
    dense_in,
    dense_in_bias,
    dense_out,
    dense_out_bias,
):
    f = lax.axis_index("fsdp")
    m = lax.axis_index("mem")
    c = m % 2
    fsdp = lax.axis_size("fsdp")
    mem = lax.axis_size("mem")
    across = mem // 2
    slow, fast = fsdp_split(fsdp)
    SHARDS[0] = fsdp
    where = jnp.stack([f // fast, f % fast, c, m]).astype(jnp.int32)
    examples = suffix.shape[0] // mem
    length = suffix.shape[1]
    width = suffix.shape[2]
    slots = memory.shape[1]
    total = mem * slots
    rows = examples * length
    inner = dense_in.shape[1]
    part = width // fsdp
    group = min(128, rows)
    blocks = 4 * fsdp

    def gather(matrices, *others):
        halves = [jnp.concatenate(matrices[:2]), jnp.concatenate(matrices[2:])]
        half = jnp.concatenate([jnp.where(c == 0, *halves), *others])
        return Gather(half, slow, fast)

    cross_gather = gather([cross_query, cross_key, cross_value, cross_output])
    in_gather = gather([dense_in[:, columns(j, width)] for j in range(4)])
    out_gather = gather([dense_out[columns(j, part)] for j in range(4)])
    small = [
        self_norm_gain,
        self_norm_bias,
        cross_norm_gain,
        cross_norm_bias,
        dense_norm_gain,
        dense_norm_bias,
        dense_out_bias,
    ]
    small += [dense_in_bias[columns(j, part)] for j in range(4)]
    small = sum(
        jnp.pad(value[None], ((i, 15 - i), (0, width - part))) for i, value in enumerate(small)
    )
    self_gather = gather([self_query, self_key, self_value, self_output], small)

    def exchange(value):
        blocks = value.reshape((mem, examples) + value.shape[1:])
        return lax.all_to_all(blocks, "mem", 0, 0, tiled=True)

    all_memory = exchange(memory)
    self_gather.send_slow()
    sent = self_gather.came
    self_gather.send_fast(*sent)
    cross_gather.send_slow(*sent)
    sent = [*self_gather.far, *cross_gather.came, all_memory]
    self_gather.far = [after(piece, *sent) for piece in self_gather.far]
    self_weights = self_gather.whole()
    cross_gather.send_fast(*self_gather.far)
    in_gather.send_slow(*self_gather.far)

    half = (2, part, width)
    grads_like = [
        (ANY, shape_of((slow,) + half, BF)),
        (ANY, shape_of((fast - 1, slow) + half, BF)),
        [(ANY, shape_of((slow,) + half, BF))]
        + [(ANY, shape_of((slow // 2,) + half, BF))] * (2 * fast - 2),
    ]

    def flat(dims, dtype):
        return (VMEM, shape_of(dims, dtype))

    per = 2 if examples % 2 == 0 else 1

    def per_example(value):
        dims = value.shape[1:]
        spec = pl.BlockSpec((per,) + dims, lambda e: (e,) + (0,) * len(dims))
        return (spec, value)

    def slots_of_example(value):
        spec = pl.BlockSpec((mem, per, slots, width), lambda e: (0, e, 0, 0))
        return (spec, value)

    def scratch(*dims):
        return pltpu.VMEM(dims, BF)

    def scatter(grads, *others, vectors=None):
        return Scatter(grads, slow, fast, *others, vectors=vectors)

    wide = (rows, width)
    square = scratch(4, width, width)
    own_rows = scratch(examples, length, width)
    x1, a1, qkv, p1, o1, vec = run(
        functools.partial(self_forward, group),
        [(SMEM, where), (ANY, suffix), Gather.refs(self_weights)],
        [
            flat(wide, F32),
            flat(wide, BF),
            flat((rows, 3 * width), BF),
            flat((rows // group * GROUPS, TOGETHER * group, group), BF),
            flat(wide, BF),
            flat((16, width), F32),
        ],
        [square, own_rows, scratch(fsdp, 16, 128)],
        1 + fsdp + blocks,
    )
    cross_gather.far = [after(piece, x1, *in_gather.came) for piece in cross_gather.far]
    cross_weights = Gather.refs(cross_gather.whole())
    in_gather.send_fast(*cross_gather.far)
    out_gather.send_slow(*cross_gather.far)
    x2, a2, q2, kv, p2, o2 = run(
        cross_forward,
        [(SMEM, where), (SMEM, counts), (VMEM, x1), (VMEM, vec)]
        + [slots_of_example(all_memory), cross_weights],
        [
            flat(wide, F32),
            flat(wide, BF),
            flat(wide, BF),
            per_example(shape_of((examples, total, 2 * width), BF)),
            per_example(shape_of((examples, GROUPS, TOGETHER * length, total), BF)),
            flat(wide, BF),
        ],
        [square],
        blocks,
        (examples // per,),
    )
    small = [after(piece, x1)[:, 2 * part + 7 : 2 * part + 11, :part] for piece in self_weights[0]]
    order = jnp.arange(fsdp) ^ f
    bias_in = jnp.take(jnp.concatenate(small), order % fast * slow + order // fast, axis=0)
    bias_in = bias_in.astype(F32).reshape(1, inner)
    in_gather.far = [after(piece, x2, *out_gather.came) for piece in in_gather.far]
    in_weights = Gather.refs(in_gather.whole())
    out_gather.send_fast(*in_gather.far)
    a3, h, slope, *grads = run(
        dense_inner,
        [(SMEM, where), (VMEM, x2), (VMEM, vec), (VMEM, bias_in), (ANY, cotangent), in_weights],
        [flat(wide, BF), flat((rows, inner), BF), flat((rows, inner), BF)] + grads_like,
        [square, scratch(fsdp, 4, part, width), own_rows],
        1 + blocks,
    )
    out_gather.far = [after(piece, a3) for piece in out_gather.far]
    out_weights = Gather.refs(out_gather.whole())
    out_scatter = scatter(grads, *out_gather.far)
    out_sum = out_scatter.add_cores()
    out_scatter.send_fast()
    y, du, vecs_y, bias_grad, *grads = run(
        dense_outer,
        [(SMEM, where), (VMEM, after(x2, *out_sum)), (VMEM, vec), (VMEM, a3), (VMEM, h)]
        + [(VMEM, slope), (ANY, cotangent), out_weights],
        [
            flat((examples, length, width), BF),
            flat((rows, inner), BF),
            flat((1, width), F32),
            flat((1, inner), F32),
        ]
        + grads_like,
        [scratch(fsdp, 4, part, width), square, own_rows],
        1 + blocks,
    )
    in_grads = grads
    gx2, vecs_dense = run(
        dense_back,
        [(SMEM, where), (VMEM, x2), (VMEM, vec), (VMEM, du), (ANY, cotangent), in_weights],
        [flat(wide, F32), flat((2, width), F32)],
        [square, own_rows],
        1 + blocks,
    )
    in_scatter = scatter(in_grads, gx2)
    in_sum = in_scatter.add_cores()
    in_scatter.send_fast()
    gx1, vecs_cross, dkv, dq2, grad_memory = run(
        cross_backward,
        [(SMEM, where), (VMEM, x1), (VMEM, vec), (VMEM, after(gx2, *in_sum, *out_scatter.came)), (VMEM, q2)]
        + [per_example(kv), per_example(p2), cross_weights],
        [
            flat(wide, F32),
            flat((2, width), F32),
            per_example(shape_of((examples, total, 2 * width), BF)),
            flat(wide, BF),
            [per_example(shape_of((examples, slots, width), BF))] * mem,
        ],
        [square, scratch(*wide), scratch(per, total, width)],
        blocks,
        (examples // per,),
    )
    in_scatter.came, _ = lax.optimization_barrier((in_scatter.came, gx1))
    out_total = out_scatter.add_fast(gx1)
    out_scatter.send_slow()
    mem_pieces = grad_memory[:1] + [swap(grad_memory[d], "mem", d) for d in range(1, mem)]
    grads = run(
        cross_grads,
        [(SMEM, where), (VMEM, after(gx2, out_total, *in_scatter.came)), (VMEM, a2), (VMEM, o2), (VMEM, dq2)]
        + [(pl.BlockSpec((examples, total, width), lambda j: (0, 0, j)), dkv), (ANY, all_memory)],
        grads_like,
        [square, scratch(width, examples * total), scratch(examples, total, width)],
        max(mem, blocks),
        (2,),
    )
    out_final = out_scatter.add_slow()
    in_scatter.add_fast(out_final)
    in_scatter.send_slow()
    cross_scatter = scatter(grads, out_final)
    cross_sum = cross_scatter.add_cores()
    cross_scatter.send_fast()
    gx1 = after(gx1, *cross_sum)
    suffix_part, vecs_self, *grads = run(
        functools.partial(self_backward, group),
        [(SMEM, where), (ANY, suffix), (VMEM, vec), (VMEM, gx1), (VMEM, a1)]
        + [(VMEM, qkv), (VMEM, p1), (VMEM, o1)]
        + [[(VMEM, x) for x in (vecs_cross, vecs_dense, vecs_y, bias_grad)], Gather.refs(self_weights)],
        [flat((examples, length, width), BF), flat((16, width), BF)] + grads_like,
        [square, own_rows, square, scratch(rows, 3 * width), scratch(*wide)],
        1 + blocks,
    )
    self_scatter = scatter(grads, *mem_pieces[1:3], vectors=vecs_self)
    self_sum = self_scatter.add_cores()
    self_scatter.send_fast()
    cross_scatter.add_fast(*self_sum)
    cross_scatter.send_slow()
    in_final = in_scatter.add_slow(*self_sum)
    dense_sum = jnp.concatenate([out_final, in_final])
    dense_sum = Replicas(dense_sum, 2 * part, across)
    self_total = self_scatter.add_fast(*dense_sum.halves, *mem_pieces[3:])
    self_scatter.send_slow()
    cross_sum = Replicas(cross_scatter.add_slow(self_total), part, across)
    suffix_rows = spread_across(after(suffix_part, self_total), mem)
    y_rows = spread_across(after(y, self_total), mem)
    dense_sum.swap_cores(self_total)
    mem_pieces = [after(value, self_total) for value in mem_pieces]
    (memory_grad,) = run(
        place_memory,
        [(SMEM, where), [(ANY, value) for value in mem_pieces]],
        [(ANY, shape_of(memory.shape, BF))],
        [scratch(mem, examples, slots, width)],
        2 * mem,
    )
    (out_low, in_low, out_high, in_high), _ = dense_sum.combine(c)
    grad_in = jnp.concatenate([in_low[:part], in_low[part:], in_high[:part], in_high[part:]], axis=1)
    grad_out = jnp.concatenate([out_low, out_high])
    done = [*cross_sum.halves, *suffix_rows, *y_rows, grad_in, grad_out, memory_grad]
    self_final = Replicas(self_scatter.add_slow(*done), part, across)
    cross_sum.swap_cores(self_final.halves[0])
    y_rows = [after(value, self_final.halves[0]) for value in y_rows]
    y_far = swap(jnp.stack(y_rows), "mem", 1)
    suffix_rows = [after(value, self_final.halves[0]) for value in suffix_rows]
    suffix_far = swap(jnp.stack(suffix_rows), "mem", 1)
    blocks = [([(ANY, x) for x in y_rows], (ANY, y_far))]
    blocks += [([(ANY, x) for x in suffix_rows], (ANY, suffix_far))]
    ((block_output, suffix_grad),) = run(
        place_rows,
        [(SMEM, where), blocks],
        [[(ANY, shape_of(suffix.shape, BF))] * 2],
        [scratch(2, mem, examples, length, width)],
        4 * mem,
    )
    grad_cross, _ = cross_sum.combine(c)
    self_final.swap_cores(block_output)
    grad_self, vectors = self_final.combine(c)

    def vector(i):
        return lax.dynamic_slice(vectors, (i, f * part), (1, part)).reshape(part)

    return (
        block_output,
        suffix_grad,
        memory_grad,
        vector(0),
        vector(1),
        *grad_self,
        vector(2),
        vector(3),
        *grad_cross,
        vector(4),
        vector(5),
        grad_in,
        lax.dynamic_slice_in_dim(vectors[7:11].reshape(-1), f * (inner // fsdp), inner // fsdp, 0),
        grad_out,
        vector(6),
    )


def solution(mesh):
    rows = P("fsdp", None, None)
    matrix = P("fsdp", None)
    vector = P("fsdp")
    attention = (vector, vector, matrix, matrix, matrix, matrix)
    params = attention + attention + (vector, vector, matrix, vector, matrix, vector)
    return jax.shard_map(
        per_device,
        mesh=mesh,
        in_specs=(rows, P("fsdp", "mem", None), vector, rows) + params,
        out_specs=(rows, rows, P("fsdp", "mem", None)) + params,
        check_vma=False,
    )
```

profile of v0, /device:TPU:0, one launch (start us, length us, event | category | flops | bytes accessed | tf_op | source)
XLA Modules:
  0.0 402.8 jit_solution(1853033850776488829)
XLA Ops:
  0.8 4.4 %all-to-all-start = ((bf16[4,8,64,768]{3,2,1,0:T(8,128)(2,1)}), bf16[4,8,64,768]{3,2,1,0:T(8,128)(2,1)S(1)}, u32[]{:S(2)}, u32[]{:S(2)}) async-start(bf16[4,8,64,768]{3,2,1,0:T(8,128)(2,1)} %bitcast.73), calls=%async_computation | async-start | bytes 6291456 | tf_op jit(solution)/shard_map/all_to_all | solution.py:693
  6.4 2.6 collective-permute-start
  9.0 2.6 collective-permute-start.1
  11.6 12.0 %collective-permute-done = bf16[208,768]{1,0:T(8,128)(2,1)S(1)} collective-permute-done((bf16[208,768]{1,0:T(8,128)(2,1)S(1)}, bf16[208,768]{1,0:T(8,128)(2,1)S(1)}, u32[]{:S(2)}, u32[]{:S(2)}) %collective-permute-start) | collective-permute-done | bytes 319520 | tf_op jit(solution)/shard_map/ppermute | solution.py:25
  23.5 10.5 %collective-permute-done.1 = bf16[208,768]{1,0:T(8,128)(2,1)S(1)} collective-permute-done((bf16[208,768]{1,0:T(8,128)(2,1)S(1)}, bf16[208,768]{1,0:T(8,128)(2,1)S(1)}, u32[]{:S(2)}, u32[]{:S(2)}) %collective-permute-start.1) | collective-permute-done | bytes 319520 | tf_op jit(solution)/shard_map/ppermute | solution.py:25
  34.0 1.2 pad_maximum_fusion.refs_2_.refs_12_
  35.3 1.6 collective-permute-start.3
  37.8 6.6 %collective-permute-start.4 = (bf16[192,768]{1,0:T(8,128)(2,1)}, bf16[192,768]{1,0:T(8,128)(2,1)S(1)}, u32[]{:S(2)}, u32[]{:S(2)}) collective-permute-start(bf16[192,768]{1,0:T(8,128)(2,1)} %get-tuple-element.150), channel_id=1, source_target_pairs={{0,8},{4,12},{8,0},{12,4},{16,24},{20,28},{24,16},{28,20},{1,9},{5... | collective-permute-start | bytes 884744 | tf_op jit(solution)/shard_map/ppermute | solution.py:25
  45.4 1.5 collective-permute-start.6
  46.9 9.1 %collective-permute-done.4 = bf16[192,768]{1,0:T(8,128)(2,1)S(1)} collective-permute-done((bf16[192,768]{1,0:T(8,128)(2,1)}, bf16[192,768]{1,0:T(8,128)(2,1)S(1)}, u32[]{:S(2)}, u32[]{:S(2)}) %collective-permute-start.4) | collective-permute-done | bytes 294944 | tf_op jit(solution)/shard_map/ppermute | solution.py:25
  56.0 12.1 %collective-permute-done.5 = bf16[192,768]{1,0:T(8,128)(2,1)S(1)} collective-permute-done((bf16[192,768]{1,0:T(8,128)(2,1)}, bf16[192,768]{1,0:T(8,128)(2,1)S(1)}, u32[]{:S(2)}, u32[]{:S(2)}) %collective-permute-start.5) | collective-permute-done | bytes 294944 | tf_op jit(solution)/shard_map/ppermute | solution.py:25
  69.6 3.3 pad_maximum_fusion.2.refs_5_.refs_7_
  73.9 4.2 %collective-permute-start.10 = (bf16[192,768]{1,0:T(8,128)(2,1)S(1)}, bf16[192,768]{1,0:T(8,128)(2,1)}, u32[]{:S(2)}, u32[]{:S(2)}) collective-permute-start(bf16[192,768]{1,0:T(8,128)(2,1)S(1)} %get-tuple-element.159), channel_id=1, source_target_pairs={{0,8},{4,12},{8,0},{12,4},{16,24},{20,28},{24,16},{28,20},{1,9},{5... | collective-permute-start | bytes 884744 | tf_op jit(solution)/shard_map/ppermute | solution.py:25
  79.1 1.5 collective-permute-start.12
  81.2 7.6 %shard_map.373 = (f32[256,768]{1,0:T(8,128)}, bf16[256,768]{1,0:T(8,128)(2,1)}, bf16[256,2304]{1,0:T(8,128)(2,1)}, bf16[6,512,128]{2,1,0:T(8,128)(2,1)}, bf16[256,768]{1,0:T(8,128)(2,1)}, /*index=5*/f32[16,768]{1,0:T(8,128)}) custom-call(s32[4]{0:T(128)} %pad_add_fusion.1.refs_0_, bf16[32,32,768]{2,1,0:T(8,128)(2,1)} %refs_1_.5, ...), custom_call_target="tpu_custom_call" | custom-call | tf_op jit(solution)/shard_map/pallas_call | solution.py:475
  90.0 11.7 %collective-permute-done.11 = bf16[192,768]{1,0:T(8,128)(2,1)} collective-permute-done((bf16[192,768]{1,0:T(8,128)(2,1)S(1)}, bf16[192,768]{1,0:T(8,128)(2,1)}, u32[]{:S(2)}, u32[]{:S(2)}) %collective-permute-start.11) | collective-permute-done | bytes 294944 | tf_op jit(solution)/shard_map/ppermute | solution.py:25
  101.7 1.4 pad_maximum_fusion.3.refs_5_
  104.0 5.0 %collective-permute-start.16 = (bf16[192,768]{1,0:T(8,128)(2,1)S(1)}, bf16[192,768]{1,0:T(8,128)(2,1)S(1)}, u32[]{:S(2)}, u32[]{:S(2)}) collective-permute-start(bf16[192,768]{1,0:T(8,128)(2,1)S(1)} %slice_select_fusion), channel_id=1, source_target_pairs={{0,8},{4,12},{8,0},{12,4},{16,24},{20,28},{24,16},{28,20},{1,9},{5... | collective-permute-start | bytes 884744 | tf_op jit(solution)/shard_map/ppermute | solution.py:25
  110.1 1.4 collective-permute-start.18
  112.5 15.1 %shard_map.374 = (f32[256,768]{1,0:T(8,128)}, bf16[256,768]{1,0:T(8,128)(2,1)}, bf16[256,768]{1,0:T(8,128)(2,1)}, bf16[8,256,1536]{2,1,0:T(8,128)(2,1)}, bf16[8,...) custom-call(s32[4]{0:T(128)} %pad_add_fusion.1.refs_0_, s32[32]{0:T(128)} %refs_1_.4, ...), custom_call_target="tpu_custom_call" | custom-call | tf_op jit(solution)/shard_map/pallas_call | solution.py:475
  127.6 4.8 %collective-permute-done.17 = bf16[192,768]{1,0:T(8,128)(2,1)S(1)} collective-permute-done((bf16[192,768]{1,0:T(8,128)(2,1)S(1)}, bf16[192,768]{1,0:T(8,128)(2,1)S(1)}, u32[]{:S(2)}, u32[]{:S(2)}) %collective-permute-start.17) | collective-permute-done | bytes 294944 | tf_op jit(solution)/shard_map/ppermute | solution.py:25
  132.5 1.4 pad_maximum_fusion.4.refs_7_
  133.9 1.3 collective-permute-start.21
  140.9 13.6 %shard_map.375 = (bf16[256,768]{1,0:T(8,128)(2,1)}, bf16[256,3072]{1,0:T(8,128)(2,1)}, bf16[256,3072]{1,0:T(8,128)(2,1)}, bf16[4,2,96,768]{3,2,1,0:T(8,128)(2,1)...) custom-call(s32[4]{0:T(128)} %pad_add_fusion.1.refs_0_, ...), custom_call_target="tpu_custom_call" | custom-call | tf_op jit(solution)/shard_map/pallas_call | solution.py:475
  154.5 7.9 %collective-permute-done.21.refs_8_ = bf16[4,192,768]{2,1,0:T(8,128)(2,1)} collective-permute-done((bf16[4,192,768]{2,1,0:T(8,128)(2,1)}, bf16[4,192,768]{2,1,0:T(8,128)(2,1)}, u32[]{:S(2)}, u32[]{:S(2)}) %collective-permute-start.21) | collective-permute-done | bytes 1179680 | tf_op jit(solution)/shard_map/ppermute | solution.py:25
  162.9 3.4 collective-permute-done.22
  167.2 1.6 fusion.3
  168.8 1.3 collective-permute-start.28
  171.5 11.7 %shard_map.376 = (bf16[8,32,768]{2,1,0:T(8,128)(2,1)}, bf16[256,3072]{1,0:T(8,128)(2,1)}, f32[1,768]{1,0:T(1,128)}, f32[1,3072]{1,0:T(1,128)}, bf16[4,2,96,768]{...) custom-call(s32[4]{0:T(128)} %pad_add_fusion.1.refs_0_, ...), custom_call_target="tpu_custom_call" | custom-call | tf_op jit(solution)/shard_map/pallas_call | solution.py:475
  183.3 7.4 %shard_map.377 = (f32[256,768]{1,0:T(8,128)}, f32[2,768]{1,0:T(2,128)}) custom-call(s32[4]{0:T(128)} %pad_add_fusion.1.refs_0_, f32[256,768]{1,0:T(8,128)} %get-tuple-element.176.refs_1_, f32[16,768]{1,0:T(8,128)} %get-tuple-element.149.refs_3_.refs_2_, bf16[256,3072]{1,0:T(8,128)(2,1)} %get-tuple-element.180.refs_3_, bf16[32,32,768]{2,1,0:T(8,128)(2,1)} %refs_4_.3, ...), custom_call_target="tpu_custom_call" | custom-call | tf_op jit(solution)/shard_map/pallas_call | solution.py:475
  191.3 1.5 collective-permute-done.26
  194.0 2.9 collective-permute-done.28
  196.9 17.7 %shard_map.378 = (f32[256,768]{1,0:T(8,128)}, f32[2,768]{1,0:T(2,128)}, bf16[8,256,1536]{2,1,0:T(8,128)(2,1)}, bf16[256,768]{1,0:T(8,128)(2,1)}, bf16[8,64,768]{...) custom-call(s32[4]{0:T(128)} %pad_add_fusion.1.refs_0_, ...), custom_call_target="tpu_custom_call" | custom-call | tf_op jit(solution)/shard_map/pallas_call | solution.py:475
  214.7 1.5 add_convert_fusion.3
  216.1 8.1 %all-to-all-start.1 = ((bf16[4,192,768]{2,1,0:T(8,128)(2,1)}), bf16[4,192,768]{2,1,0:T(8,128)(2,1)S(1)}, u32[]{:S(2)}, u32[]{:S(2)}) async-start(bf16[4,192,768]{2,1,0:T(8,128)(2,1)} %bitcast.35), calls=%async_computation.1 | async-start | bytes 2359296 | tf_op jit(solution)/shard_map/all_to_all | solution.py:496
  224.2 1.2 collective-permute-start.30
  225.5 25.7 %collective-permute-done.30 = bf16[4,2,96,768]{3,2,1,0:T(8,128)(2,1)S(1)} collective-permute-done((bf16[4,2,96,768]{3,2,1,0:T(8,128)(2,1)S(1)}, bf16[4,2,96,768]{3,2,1,0:T(8,128)(2,1)S(1)}, u32[]{:S(2)}, u32[]{:S(2)}) %collective-permute-start.30) | collective-permute-done | bytes 1179680 | tf_op jit(solution)/shard_map/ppermute | solution.py:25
  252.2 13.1 %shard_map.379 = (bf16[4,2,96,768]{3,2,1,0:T(8,128)(2,1)}, bf16[1,4,2,96,768]{4,3,2,1,0:T(8,128)(2,1)}, bf16[4,2,96,768]{3,2,1,0:T(8,128)(2,1)}, bf16[2,2,96,768]{3,2,1,0:T(8,128)(2,1)}, bf16[2,2,96,768]{3,2,1,0:T(8,128)(2,1)}) custom-call(s32[4]{0:T(128)} %pad_add_fusion.1.refs_0_, f32[256,768]{1,0:T(8,128)} %get-tuple-element.197.refs_3_.refs_1_, ...), custom_call_target="tpu_custom_call" | custom-call | tf_op jit(solution)/shard_map/pallas_call | solution.py:475
  266.1 1.4 collective-permute-start.35
  267.5 3.1 add_convert_fusion.2
  270.6 5.2 %all-to-all-start.2 = ((bf16[4,192,768]{2,1,0:T(8,128)(2,1)}), bf16[4,192,768]{2,1,0:T(8,128)(2,1)S(1)}, u32[]{:S(2)}, u32[]{:S(2)}) async-start(bf16[4,192,768]{2,1,0:T(8,128)(2,1)} %bitcast.37), calls=%async_computation.2 | async-start | bytes 2359296 | tf_op jit(solution)/shard_map/all_to_all | solution.py:496
  275.9 1.5 fusion.1
  277.4 1.3 collective-permute-start.45
  278.7 11.7 %shard_map.380 = (bf16[8,32,768]{2,1,0:T(8,128)(2,1)}, bf16[16,768]{1,0:T(8,128)(2,1)}, bf16[4,2,96,768]{3,2,1,0:T(8,128)(2,1)}, bf16[1,4,2,96,768]{4,3,2,1,0:T(...) custom-call(s32[4]{0:T(128)} %pad_add_fusion.1.refs_0_, ...), custom_call_target="tpu_custom_call" | custom-call | tf_op jit(solution)/shard_map/pallas_call | solution.py:475
  291.0 1.7 collective-permute-done.36
  293.6 2.7 fusion
  297.0 9.2 %collective-permute-done.45 = bf16[4,2,96,768]{3,2,1,0:T(8,128)(2,1)S(1)} collective-permute-done((bf16[4,2,96,768]{3,2,1,0:T(8,128)(2,1)S(1)}, bf16[4,2,96,768]{3,2,1,0:T(8,128)(2,1)S(1)}, u32[]{:S(2)}, u32[]{:S(2)}) %collective-permute-start.45) | collective-permute-done | bytes 1179680 | tf_op jit(solution)/shard_map/ppermute | solution.py:25
  306.3 1.5 add_convert_fusion
  307.7 5.1 %all-to-all-start.4 = ((bf16[4,192,768]{2,1,0:T(8,128)(2,1)}), bf16[4,192,768]{2,1,0:T(8,128)(2,1)S(1)}, u32[]{:S(2)}, u32[]{:S(2)}) async-start(bf16[4,192,768]{2,1,0:T(8,128)(2,1)} %bitcast.40), calls=%async_computation.4 | async-start | bytes 2359296 | tf_op jit(solution)/shard_map/all_to_all | solution.py:496
  314.7 1.4 collective-permute-start.38
  317.3 1.3 collective-permute-start.42
  318.6 13.8 %collective-permute-done.39.refs_4_ = bf16[8,64,768]{2,1,0:T(8,128)(2,1)} collective-permute-done((bf16[8,64,768]{2,1,0:T(8,128)(2,1)}, bf16[8,64,768]{2,1,0:T(8,128)(2,1)}, u32[]{:S(2)}, u32[]{:S(2)}) %collective-permute-start.39) | collective-permute-done | bytes 786464 | tf_op jit(solution)/shard_map/ppermute | solution.py:25
  332.5 13.2 %collective-permute-done.38 = bf16[384,768]{1,0:T(8,128)(2,1)} collective-permute-done((bf16[384,768]{1,0:T(8,128)(2,1)}, bf16[384,768]{1,0:T(8,128)(2,1)}, u32[]{:S(2)}, u32[]{:S(2)}) %collective-permute-start.38) | collective-permute-done | bytes 589856 | tf_op jit(solution)/shard_map/ppermute | solution.py:25
  345.7 2.1 add_convert_fusion.1
  349.5 5.0 %all-to-all-start.3 = ((bf16[4,208,768]{2,1,0:T(8,128)(2,1)}), bf16[4,208,768]{2,1,0:T(8,128)(2,1)S(1)}, u32[]{:S(2)}, u32[]{:S(2)}) async-start(bf16[4,208,768]{2,1,0:T(8,128)(2,1)} %pad_maximum_fusion.1), calls=%async_computation.3 | async-start | bytes 2555904 | tf_op jit(solution)/shard_map/all_to_all | solution.py:496
  355.1 1.4 collective-permute-start.48
  356.5 3.5 shard_map.381
  360.1 1.7 fusion.5
  365.5 2.2 pad_maximum_fusion.5
  367.6 7.6 %collective-permute-done.48.refs_2_ = bf16[8,32,768]{2,1,0:T(8,128)(2,1)} collective-permute-done((bf16[8,32,768]{2,1,0:T(8,128)(2,1)S(1)}, bf16[8,32,768]{2,1,0:T(8,128)(2,1)}, u32[]{:S(2)}, u32[]{:S(2)}) %collective-permute-start.48) | collective-permute-done | bytes 393248 | tf_op jit(solution)/shard_map/ppermute | solution.py:25
  375.2 5.0 %collective-permute-done.46 = bf16[192,768]{1,0:T(8,128)(2,1)} collective-permute-done((bf16[192,768]{1,0:T(8,128)(2,1)}, bf16[192,768]{1,0:T(8,128)(2,1)}, u32[]{:S(2)}, u32[]{:S(2)}) %collective-permute-start.46) | collective-permute-done | bytes 294944 | tf_op jit(solution)/shard_map/ppermute | solution.py:25
  380.3 5.0 %all-to-all-done.3 = bf16[4,208,768]{2,1,0:T(8,128)(2,1)S(1)} async-done(((bf16[4,208,768]{2,1,0:T(8,128)(2,1)}), bf16[4,208,768]{2,1,0:T(8,128)(2,1)S(1)}, u32[]{:S(2)}, u32[]{:S(2)}) %all-to-all-start.3) | async-done | bytes 1277984 | tf_op jit(solution)/shard_map/all_to_all | solution.py:496
  389.6 1.4 fusion.8
  394.5 3.4 shard_map.382
  (217 shorter events, 47.2 us)
Async XLA Ops:
  0.8 68.8 %all-to-all-start = ((bf16[4,8,64,768]{3,2,1,0:T(8,128)(2,1)}), bf16[4,8,64,768]{3,2,1,0:T(8,128)(2,1)S(1)}, u32[]{:S(2)}, u32[]{:S(2)}) async-start(bf16[4,8,64,768]{3,2,1,0:T(8,128)(2,1)} %bitcast.73), calls=%async_computation | async-start | bytes 6291456 | tf_op jit(solution)/shard_map/all_to_all | solution.py:693
  6.4 17.2 %collective-permute-start = (bf16[208,768]{1,0:T(8,128)(2,1)S(1)}, bf16[208,768]{1,0:T(8,128)(2,1)S(1)}, u32[]{:S(2)}, u32[]{:S(2)}) collective-permute-start(bf16[208,768]{1,0:T(8,128)(2,1)S(1)} %pad_maximum_fusion.10), channel_id=1, source_target_pairs={{0,8},{4,12},{8,0},{12,4},{16,24},{20,28},{24,16},{28,20},{1,9},{5... | collective-permute-start | bytes 958472 | tf_op jit(solution)/shard_map/ppermute | solution.py:25
  9.0 25.0 %collective-permute-start.1 = (bf16[208,768]{1,0:T(8,128)(2,1)S(1)}, bf16[208,768]{1,0:T(8,128)(2,1)S(1)}, u32[]{:S(2)}, u32[]{:S(2)}) collective-permute-start(bf16[208,768]{1,0:T(8,128)(2,1)S(1)} %pad_maximum_fusion.10), channel_id=1, source_target_pairs={{0,16},{4,20},{8,24},{12,28},{16,0},{20,4},{24,8},{28,12},{1,17},{... | collective-permute-start | bytes 958472 | tf_op jit(solution)/shard_map/ppermute | solution.py:25
  11.6 22.4 %collective-permute-start.2 = (bf16[208,768]{1,0:T(8,128)(2,1)S(1)}, bf16[208,768]{1,0:T(8,128)(2,1)S(1)}, u32[]{:S(2)}, u32[]{:S(2)}) collective-permute-start(bf16[208,768]{1,0:T(8,128)(2,1)S(1)} %pad_maximum_fusion.10), channel_id=1, source_target_pairs={{0,24},{4,28},{8,16},{12,20},{16,8},{20,12},{24,0},{28,4},{1,25},{... | collective-permute-start | bytes 958472 | tf_op jit(solution)/shard_map/ppermute | solution.py:25
  35.3 34.3 %collective-permute-start.3 = (bf16[4,208,768]{2,1,0:T(8,128)(2,1)}, bf16[4,208,768]{2,1,0:T(8,128)(2,1)}, u32[]{:S(2)}, u32[]{:S(2)}) collective-permute-start(bf16[4,208,768]{2,1,0:T(8,128)(2,1)} %pad_maximum_fusion.refs_2_.refs_12_), channel_id=1, source_target_pairs={{0,4},{4,0},{8,12},{12,8},{16,20},{20,16},{24,28},{28,24},{1,5},{5... | collective-permute-start | bytes 3833864 | tf_op jit(solution)/shard_map/ppermute | solution.py:25
  37.8 18.2 %collective-permute-start.4 = (bf16[192,768]{1,0:T(8,128)(2,1)}, bf16[192,768]{1,0:T(8,128)(2,1)S(1)}, u32[]{:S(2)}, u32[]{:S(2)}) collective-permute-start(bf16[192,768]{1,0:T(8,128)(2,1)} %get-tuple-element.150), channel_id=1, source_target_pairs={{0,8},{4,12},{8,0},{12,4},{16,24},{20,28},{24,16},{28,20},{1,9},{5... | collective-permute-start | bytes 884744 | tf_op jit(solution)/shard_map/ppermute | solution.py:25
  44.4 23.7 %collective-permute-start.5 = (bf16[192,768]{1,0:T(8,128)(2,1)}, bf16[192,768]{1,0:T(8,128)(2,1)S(1)}, u32[]{:S(2)}, u32[]{:S(2)}) collective-permute-start(bf16[192,768]{1,0:T(8,128)(2,1)} %get-tuple-element.150), channel_id=1, source_target_pairs={{0,16},{4,20},{8,24},{12,28},{16,0},{20,4},{24,8},{28,12},{1,17},{... | collective-permute-start | bytes 884744 | tf_op jit(solution)/shard_map/ppermute | solution.py:25
  45.4 22.7 %collective-permute-start.6 = (bf16[192,768]{1,0:T(8,128)(2,1)}, bf16[192,768]{1,0:T(8,128)(2,1)S(1)}, u32[]{:S(2)}, u32[]{:S(2)}) collective-permute-start(bf16[192,768]{1,0:T(8,128)(2,1)} %get-tuple-element.150), channel_id=1, source_target_pairs={{0,24},{4,28},{8,16},{12,20},{16,8},{20,12},{24,0},{28,4},{1,25},{... | collective-permute-start | bytes 884744 | tf_op jit(solution)/shard_map/ppermute | solution.py:25
  46.9 32.2 %collective-permute-start.7 = (bf16[4,208,768]{2,1,0:T(8,128)(2,1)}, bf16[4,208,768]{2,1,0:T(8,128)(2,1)}, u32[]{:S(2)}, u32[]{:S(2)}) collective-permute-start(bf16[4,208,768]{2,1,0:T(8,128)(2,1)} %pad_maximum_fusion.refs_2_.refs_12_), channel_id=1, source_target_pairs={{0,1},{1,0},{2,3},{3,2},{4,5},{5,4},{6,7},{7,6},{8,9},{9,8},{10,11... | collective-permute-start | bytes 3833864 | tf_op jit(solution)/shard_map/ppermute | solution.py:25
  69.6 11.1 %collective-permute-start.8 = (bf16[4,208,768]{2,1,0:T(8,128)(2,1)}, bf16[4,208,768]{2,1,0:T(8,128)(2,1)}, u32[]{:S(2)}, u32[]{:S(2)}) collective-permute-start(bf16[4,208,768]{2,1,0:T(8,128)(2,1)} %collective-permute-done.3.refs_3_.refs_13_), channel_id=1, source_target_pairs={{0,1},{1,0},{2,3},{3,2},{4,5},{5,4},{6,7},{7,6},{8,9},{9,8},{10,11... | collective-permute-start | bytes 3833864 | tf_op jit(solution)/shard_map/ppermute | solution.py:25
  72.9 28.8 %collective-permute-start.9 = (bf16[4,192,768]{2,1,0:T(8,128)(2,1)}, bf16[4,192,768]{2,1,0:T(8,128)(2,1)}, u32[]{:S(2)}, u32[]{:S(2)}) collective-permute-start(bf16[4,192,768]{2,1,0:T(8,128)(2,1)} %pad_maximum_fusion.2.refs_5_.refs_7_), channel_id=1, source_target_pairs={{0,4},{4,0},{8,12},{12,8},{16,20},{20,16},{24,28},{28,24},{1,5},{5... | collective-permute-start | bytes 3538952 | tf_op jit(solution)/shard_map/ppermute | solution.py:25
  73.9 16.1 %collective-permute-start.10 = (bf16[192,768]{1,0:T(8,128)(2,1)S(1)}, bf16[192,768]{1,0:T(8,128)(2,1)}, u32[]{:S(2)}, u32[]{:S(2)}) collective-permute-start(bf16[192,768]{1,0:T(8,128)(2,1)S(1)} %get-tuple-element.159), channel_id=1, source_target_pairs={{0,8},{4,12},{8,0},{12,4},{16,24},{20,28},{24,16},{28,20},{1,9},{5... | collective-permute-start | bytes 884744 | tf_op jit(solution)/shard_map/ppermute | solution.py:25
  78.1 23.6 %collective-permute-start.11 = (bf16[192,768]{1,0:T(8,128)(2,1)S(1)}, bf16[192,768]{1,0:T(8,128)(2,1)}, u32[]{:S(2)}, u32[]{:S(2)}) collective-permute-start(bf16[192,768]{1,0:T(8,128)(2,1)S(1)} %get-tuple-element.159), channel_id=1, source_target_pairs={{0,16},{4,20},{8,24},{12,28},{16,0},{20,4},{24,8},{28,12},{1,17},{... | collective-permute-start | bytes 884744 | tf_op jit(solution)/shard_map/ppermute | solution.py:25
  79.1 22.6 %collective-permute-start.12 = (bf16[192,768]{1,0:T(8,128)(2,1)S(1)}, bf16[192,768]{1,0:T(8,128)(2,1)}, u32[]{:S(2)}, u32[]{:S(2)}) collective-permute-start(bf16[192,768]{1,0:T(8,128)(2,1)S(1)} %get-tuple-element.159), channel_id=1, source_target_pairs={{0,24},{4,28},{8,16},{12,20},{16,8},{20,12},{24,0},{28,4},{1,25},{... | collective-permute-start | bytes 884744 | tf_op jit(solution)/shard_map/ppermute | solution.py:25
  80.6 29.5 %collective-permute-start.13 = (bf16[4,192,768]{2,1,0:T(8,128)(2,1)}, bf16[4,192,768]{2,1,0:T(8,128)(2,1)}, u32[]{:S(2)}, u32[]{:S(2)}) collective-permute-start(bf16[4,192,768]{2,1,0:T(8,128)(2,1)} %pad_maximum_fusion.2.refs_5_.refs_7_), channel_id=1, source_target_pairs={{0,1},{1,0},{2,3},{3,2},{4,5},{5,4},{6,7},{7,6},{8,9},{9,8},{10,11... | collective-permute-start | bytes 3538952 | tf_op jit(solution)/shard_map/ppermute | solution.py:25
  101.7 9.7 %collective-permute-start.14 = (bf16[4,192,768]{2,1,0:T(8,128)(2,1)}, bf16[4,192,768]{2,1,0:T(8,128)(2,1)S(1)}, u32[]{:S(2)}, u32[]{:S(2)}) collective-permute-start(bf16[4,192,768]{2,1,0:T(8,128)(2,1)} %collective-permute-done.9.refs_6_.refs_8_), channel_id=1, source_target_pairs={{0,1},{1,0},{2,3},{3,2},{4,5},{5,4},{6,7},{7,6},{8,9},{9,8},{10,11... | collective-permute-start | bytes 3538952 | tf_op jit(solution)/shard_map/ppermute | solution.py:25
  103.1 29.3 %collective-permute-start.15 = (bf16[4,192,768]{2,1,0:T(8,128)(2,1)S(1)}, bf16[4,192,768]{2,1,0:T(8,128)(2,1)S(1)}, u32[]{:S(2)}, u32[]{:S(2)}) collective-permute-start(bf16[4,192,768]{2,1,0:T(8,128)(2,1)S(1)} %pad_maximum_fusion.3.refs_5_), channel_id=1, source_target_pairs={{0,4},{4,0},{8,12},{12,8},{16,20},{20,16},{24,28},{28,24},{1,5},{5... | collective-permute-start | bytes 3538952 | tf_op jit(solution)/shard_map/ppermute | solution.py:25
  104.0 23.6 %collective-permute-start.16 = (bf16[192,768]{1,0:T(8,128)(2,1)S(1)}, bf16[192,768]{1,0:T(8,128)(2,1)S(1)}, u32[]{:S(2)}, u32[]{:S(2)}) collective-permute-start(bf16[192,768]{1,0:T(8,128)(2,1)S(1)} %slice_select_fusion), channel_id=1, source_target_pairs={{0,8},{4,12},{8,0},{12,4},{16,24},{20,28},{24,16},{28,20},{1,9},{5... | collective-permute-start | bytes 884744 | tf_op jit(solution)/shard_map/ppermute | solution.py:25
  109.0 23.4 %collective-permute-start.17 = (bf16[192,768]{1,0:T(8,128)(2,1)S(1)}, bf16[192,768]{1,0:T(8,128)(2,1)S(1)}, u32[]{:S(2)}, u32[]{:S(2)}) collective-permute-start(bf16[192,768]{1,0:T(8,128)(2,1)S(1)} %slice_select_fusion), channel_id=1, source_target_pairs={{0,16},{4,20},{8,24},{12,28},{16,0},{20,4},{24,8},{28,12},{1,17},{... | collective-permute-start | bytes 884744 | tf_op jit(solution)/shard_map/ppermute | solution.py:25
  110.1 22.3 %collective-permute-start.18 = (bf16[192,768]{1,0:T(8,128)(2,1)S(1)}, bf16[192,768]{1,0:T(8,128)(2,1)S(1)}, u32[]{:S(2)}, u32[]{:S(2)}) collective-permute-start(bf16[192,768]{1,0:T(8,128)(2,1)S(1)} %slice_select_fusion), channel_id=1, source_target_pairs={{0,24},{4,28},{8,16},{12,20},{16,8},{20,12},{24,0},{28,4},{1,25},{... | collective-permute-start | bytes 884744 | tf_op jit(solution)/shard_map/ppermute | solution.py:25
  111.5 28.4 %collective-permute-start.19 = (bf16[4,192,768]{2,1,0:T(8,128)(2,1)S(1)}, bf16[4,192,768]{2,1,0:T(8,128)(2,1)}, u32[]{:S(2)}, u32[]{:S(2)}) collective-permute-start(bf16[4,192,768]{2,1,0:T(8,128)(2,1)S(1)} %pad_maximum_fusion.3.refs_5_), channel_id=1, source_target_pairs={{0,1},{1,0},{2,3},{3,2},{4,5},{5,4},{6,7},{7,6},{8,9},{9,8},{10,11... | collective-permute-start | bytes 3538952 | tf_op jit(solution)/shard_map/ppermute | solution.py:25
  132.4 7.4 %collective-permute-start.20 = (bf16[4,192,768]{2,1,0:T(8,128)(2,1)S(1)}, bf16[4,192,768]{2,1,0:T(8,128)(2,1)S(1)}, u32[]{:S(2)}, u32[]{:S(2)}) collective-permute-start(bf16[4,192,768]{2,1,0:T(8,128)(2,1)S(1)} %collective-permute-done.15.refs_6_), channel_id=1, source_target_pairs={{0,1},{1,0},{2,3},{3,2},{4,5},{5,4},{6,7},{7,6},{8,9},{9,8},{10,11... | collective-permute-start | bytes 3538952 | tf_op jit(solution)/shard_map/ppermute | solution.py:25
  133.9 28.5 %collective-permute-start.21 = (bf16[4,192,768]{2,1,0:T(8,128)(2,1)}, bf16[4,192,768]{2,1,0:T(8,128)(2,1)}, u32[]{:S(2)}, u32[]{:S(2)}) collective-permute-start(bf16[4,192,768]{2,1,0:T(8,128)(2,1)} %pad_maximum_fusion.4.refs_7_), channel_id=1, source_target_pairs={{0,4},{4,0},{8,12},{12,8},{16,20},{20,16},{24,28},{28,24},{1,5},{5... | collective-permute-start | bytes 3538952 | tf_op jit(solution)/shard_map/ppermute | solution.py:25
  139.8 30.3 %collective-permute-start.24 = (bf16[4,192,768]{2,1,0:T(8,128)(2,1)}, bf16[4,192,768]{2,1,0:T(8,128)(2,1)S(1)}, u32[]{:S(2)}, u32[]{:S(2)}) collective-permute-start(bf16[4,192,768]{2,1,0:T(8,128)(2,1)} %pad_maximum_fusion.4.refs_7_), channel_id=1, source_target_pairs={{0,1},{1,0},{2,3},{3,2},{4,5},{5,4},{6,7},{7,6},{8,9},{9,8},{10,11... | collective-permute-start | bytes 3538952 | tf_op jit(solution)/shard_map/ppermute | solution.py:25
  162.4 7.7 %collective-permute-start.25 = (bf16[4,192,768]{2,1,0:T(8,128)(2,1)}, bf16[4,192,768]{2,1,0:T(8,128)(2,1)S(1)}, u32[]{:S(2)}, u32[]{:S(2)}) collective-permute-start(bf16[4,192,768]{2,1,0:T(8,128)(2,1)} %collective-permute-done.21.refs_8_), channel_id=1, source_target_pairs={{0,1},{1,0},{2,3},{3,2},{4,5},{5,4},{6,7},{7,6},{8,9},{9,8},{10,11... | collective-permute-start | bytes 3538952 | tf_op jit(solution)/shard_map/ppermute | solution.py:25
  162.4 3.9 collective-permute-start.22
  162.9 4.2 %collective-permute-start.23 = (bf16[2,2,96,768]{3,2,1,0:T(8,128)(2,1)}, bf16[2,2,96,768]{3,2,1,0:T(8,128)(2,1)S(1)}, u32[]{:S(2)}, u32[]{:S(2)}) collective-permute-start(bf16[2,2,96,768]{3,2,1,0:T(8,128)(2,1)} %get-tuple-element.175), channel_id=1, source_target_pairs={{0,1},{1,0},{2,3},{3,2},{4,5},{5,4},{6,7},{7,6},{8,9},{9,8},{10,11... | collective-permute-start | bytes 1769480 | tf_op jit(solution)/shard_map/ppermute | solution.py:25
  168.8 28.1 %collective-permute-start.28 = (bf16[4,2,96,768]{3,2,1,0:T(8,128)(2,1)S(1)}, bf16[4,2,96,768]{3,2,1,0:T(8,128)(2,1)S(1)}, u32[]{:S(2)}, u32[]{:S(2)}) collective-permute-start(bf16[4,2,96,768]{3,2,1,0:T(8,128)(2,1)S(1)} %fusion.3), channel_id=1, source_target_pairs={{0,4},{4,0},{8,12},{12,8},{16,20},{20,16},{24,28},{28,24},{1,5},{5... | collective-permute-start | bytes 3538952 | tf_op jit(solution)/shard_map/ppermute | solution.py:25
  170.1 44.5 %collective-permute-start.29 = (bf16[4,2,96,768]{3,2,1,0:T(8,128)(2,1)S(1)}, bf16[4,2,96,768]{3,2,1,0:T(8,128)(2,1)S(1)}, u32[]{:S(2)}, u32[]{:S(2)}) collective-permute-start(bf16[4,2,96,768]{3,2,1,0:T(8,128)(2,1)S(1)} %copy-done.39), channel_id=1, source_target_pairs={{0,1},{1,0},{2,3},{3,2},{4,5},{5,4},{6,7},{7,6},{8,9},{9,8},{10,11... | collective-permute-start | bytes 3538952 | tf_op jit(solution)/shard_map/ppermute | solution.py:25
  190.6 2.2 collective-permute-start.26
  191.2 2.5 collective-permute-start.27
  216.1 49.2 %all-to-all-start.1 = ((bf16[4,192,768]{2,1,0:T(8,128)(2,1)}), bf16[4,192,768]{2,1,0:T(8,128)(2,1)S(1)}, u32[]{:S(2)}, u32[]{:S(2)}) async-start(bf16[4,192,768]{2,1,0:T(8,128)(2,1)} %bitcast.35), calls=%async_computation.1 | async-start | bytes 2359296 | tf_op jit(solution)/shard_map/all_to_all | solution.py:496
  224.2 26.9 %collective-permute-start.30 = (bf16[4,2,96,768]{3,2,1,0:T(8,128)(2,1)S(1)}, bf16[4,2,96,768]{3,2,1,0:T(8,128)(2,1)S(1)}, u32[]{:S(2)}, u32[]{:S(2)}) collective-permute-start(bf16[4,2,96,768]{3,2,1,0:T(8,128)(2,1)S(1)} %fusion.2), channel_id=1, source_target_pairs={{0,4},{4,0},{8,12},{12,8},{16,20},{20,16},{24,28},{28,24},{1,5},{5... | collective-permute-start | bytes 3538952 | tf_op jit(solution)/shard_map/ppermute | solution.py:25
  225.5 42.0 %collective-permute-start.33 = (bf16[4,2,96,768]{3,2,1,0:T(8,128)(2,1)}, bf16[4,2,96,768]{3,2,1,0:T(8,128)(2,1)}, u32[]{:S(2)}, u32[]{:S(2)}) collective-permute-start(bf16[4,2,96,768]{3,2,1,0:T(8,128)(2,1)} %get-tuple-element.220), channel_id=1, source_target_pairs={{0,1},{1,0},{2,3},{3,2},{4,5},{5,4},{6,7},{7,6},{8,9},{9,8},{10,11... | collective-permute-start | bytes 3538952 | tf_op jit(solution)/shard_map/ppermute | solution.py:25
  265.5 10.4 %collective-permute-start.31 = (bf16[2,2,96,768]{3,2,1,0:T(8,128)(2,1)}, bf16[2,2,96,768]{3,2,1,0:T(8,128)(2,1)}, u32[]{:S(2)}, u32[]{:S(2)}) collective-permute-start(bf16[2,2,96,768]{3,2,1,0:T(8,128)(2,1)} %get-tuple-element.204), channel_id=1, source_target_pairs={{0,1},{1,0},{2,3},{3,2},{4,5},{5,4},{6,7},{7,6},{8,9},{9,8},{10,11... | collective-permute-start | bytes 1769480 | tf_op jit(solution)/shard_map/ppermute | solution.py:25
  265.5 10.3 %collective-permute-start.32 = (bf16[2,2,96,768]{3,2,1,0:T(8,128)(2,1)}, bf16[2,2,96,768]{3,2,1,0:T(8,128)(2,1)}, u32[]{:S(2)}, u32[]{:S(2)}) collective-permute-start(bf16[2,2,96,768]{3,2,1,0:T(8,128)(2,1)} %get-tuple-element.206), channel_id=1, source_target_pairs={{0,1},{1,0},{2,3},{3,2},{4,5},{5,4},{6,7},{7,6},{8,9},{9,8},{10,11... | collective-permute-start | bytes 1769480 | tf_op jit(solution)/shard_map/ppermute | solution.py:25
  266.0 24.4 %collective-permute-start.34 = (bf16[8,64,768]{2,1,0:T(8,128)(2,1)}, bf16[8,64,768]{2,1,0:T(8,128)(2,1)S(1)}, u32[]{:S(2)}, u32[]{:S(2)}) collective-permute-start(bf16[8,64,768]{2,1,0:T(8,128)(2,1)} %get-tuple-element.223), channel_id=1, source_target_pairs={{0,1},{1,0},{2,3},{3,2},{4,5},{5,4},{6,7},{7,6},{8,9},{9,8},{10,11... | collective-permute-start | bytes 2359304 | tf_op jit(solution)/shard_map/ppermute | solution.py:25
  266.1 24.3 %collective-permute-start.35 = (bf16[8,64,768]{2,1,0:T(8,128)(2,1)}, bf16[8,64,768]{2,1,0:T(8,128)(2,1)}, u32[]{:S(2)}, u32[]{:S(2)}) collective-permute-start(bf16[8,64,768]{2,1,0:T(8,128)(2,1)} %get-tuple-element.224), channel_id=1, source_target_pairs={{0,2},{1,3},{2,0},{3,1},{4,6},{5,7},{6,4},{7,5},{8,10},{9,11},{10,... | collective-permute-start | bytes 2359304 | tf_op jit(solution)/shard_map/ppermute | solution.py:25
  270.6 37.1 %all-to-all-start.2 = ((bf16[4,192,768]{2,1,0:T(8,128)(2,1)}), bf16[4,192,768]{2,1,0:T(8,128)(2,1)S(1)}, u32[]{:S(2)}, u32[]{:S(2)}) async-start(bf16[4,192,768]{2,1,0:T(8,128)(2,1)} %bitcast.37), calls=%async_computation.2 | async-start | bytes 2359296 | tf_op jit(solution)/shard_map/all_to_all | solution.py:496
  275.8 21.2 %collective-permute-start.44 = (bf16[4,2,96,768]{3,2,1,0:T(8,128)(2,1)}, bf16[4,2,96,768]{3,2,1,0:T(8,128)(2,1)S(1)}, u32[]{:S(2)}, u32[]{:S(2)}) collective-permute-start(bf16[4,2,96,768]{3,2,1,0:T(8,128)(2,1)} %get-tuple-element.241), channel_id=1, source_target_pairs={{0,1},{1,0},{2,3},{3,2},{4,5},{5,4},{6,7},{7,6},{8,9},{9,8},{10,11... | collective-permute-start | bytes 3538952 | tf_op jit(solution)/shard_map/ppermute | solution.py:25
  277.4 28.8 %collective-permute-start.45 = (bf16[4,2,96,768]{3,2,1,0:T(8,128)(2,1)S(1)}, bf16[4,2,96,768]{3,2,1,0:T(8,128)(2,1)S(1)}, u32[]{:S(2)}, u32[]{:S(2)}) collective-permute-start(bf16[4,2,96,768]{3,2,1,0:T(8,128)(2,1)S(1)} %fusion.1), channel_id=1, source_target_pairs={{0,4},{4,0},{8,12},{12,8},{16,20},{20,16},{24,28},{28,24},{1,5},{5... | collective-permute-start | bytes 3538952 | tf_op jit(solution)/shard_map/ppermute | solution.py:25
  290.4 2.3 collective-permute-start.36
  290.7 2.9 collective-permute-start.37
  296.2 49.4 %collective-permute-start.43 = (bf16[4,2,96,768]{3,2,1,0:T(8,128)(2,1)}, bf16[4,2,96,768]{3,2,1,0:T(8,128)(2,1)}, u32[]{:S(2)}, u32[]{:S(2)}) collective-permute-start(bf16[4,2,96,768]{3,2,1,0:T(8,128)(2,1)} %fusion), channel_id=1, source_target_pairs={{0,4},{4,0},{8,12},{12,8},{16,20},{20,16},{24,28},{28,24},{1,5},{5... | collective-permute-start | bytes 3538952 | tf_op jit(solution)/shard_map/ppermute | solution.py:25
  307.7 41.7 %all-to-all-start.4 = ((bf16[4,192,768]{2,1,0:T(8,128)(2,1)}), bf16[4,192,768]{2,1,0:T(8,128)(2,1)S(1)}, u32[]{:S(2)}, u32[]{:S(2)}) async-start(bf16[4,192,768]{2,1,0:T(8,128)(2,1)} %bitcast.40), calls=%async_computation.4 | async-start | bytes 2359296 | tf_op jit(solution)/shard_map/all_to_all | solution.py:496
  312.8 32.9 %collective-permute-start.40 = (bf16[4,2,96,768]{3,2,1,0:T(8,128)(2,1)}, bf16[4,2,96,768]{3,2,1,0:T(8,128)(2,1)}, u32[]{:S(2)}, u32[]{:S(2)}) collective-permute-start(bf16[4,2,96,768]{3,2,1,0:T(8,128)(2,1)} %get-tuple-element.232), channel_id=1, source_target_pairs={{0,1},{1,0},{2,3},{3,2},{4,5},{5,4},{6,7},{7,6},{8,9},{9,8},{10,11... | collective-permute-start | bytes 3538952 | tf_op jit(solution)/shard_map/ppermute | solution.py:25
  312.8 19.6 %collective-permute-start.39 = (bf16[8,64,768]{2,1,0:T(8,128)(2,1)}, bf16[8,64,768]{2,1,0:T(8,128)(2,1)}, u32[]{:S(2)}, u32[]{:S(2)}) collective-permute-start(bf16[8,64,768]{2,1,0:T(8,128)(2,1)} %get-tuple-element.229), channel_id=1, source_target_pairs={{0,3},{1,2},{2,1},{3,0},{4,7},{5,6},{6,5},{7,4},{8,11},{9,10},{10,... | collective-permute-start | bytes 2359304 | tf_op jit(solution)/shard_map/ppermute | solution.py:25
  313.9 31.9 %copy-start.11 = (bf16[4,2,96,768]{3,2,1,0:T(8,128)(2,1)S(1)}, bf16[4,2,96,768]{3,2,1,0:T(8,128)(2,1)}, u32[]{:S(2)}) copy-start(bf16[4,2,96,768]{3,2,1,0:T(8,128)(2,1)} %get-tuple-element.230) | copy-start | bytes 3538948
  314.7 30.9 %collective-permute-start.38 = (bf16[384,768]{1,0:T(8,128)(2,1)}, bf16[384,768]{1,0:T(8,128)(2,1)}, u32[]{:S(2)}, u32[]{:S(2)}) collective-permute-start(bf16[384,768]{1,0:T(8,128)(2,1)} %pad_maximum_fusion.9), channel_id=1, source_target_pairs={{0,2},{1,3},{2,0},{3,1},{4,6},{5,7},{6,4},{7,5},{8,10},{9,11},{10,... | collective-permute-start | bytes 1769480 | tf_op jit(solution)/shard_map/ppermute | solution.py:25
  316.1 1.2 collective-permute-start.41
  317.3 28.3 %collective-permute-start.42 = (bf16[16,768]{1,0:T(8,128)(2,1)S(1)}, bf16[16,768]{1,0:T(8,128)(2,1)S(1)}, u32[]{:S(2)}, u32[]{:S(2)}) collective-permute-start(bf16[16,768]{1,0:T(8,128)(2,1)S(1)} %add_convert_fusion.5), channel_id=1, source_target_pairs={{0,4},{4,0},{8,12},{12,8},{16,20},{20,16},{24,28},{28,24},{1,5},{5... | collective-permute-start | bytes 73736 | tf_op jit(solution)/shard_map/ppermute | solution.py:25
  348.9 11.1 %collective-permute-start.49 = (bf16[384,768]{1,0:T(8,128)(2,1)}, bf16[384,768]{1,0:T(8,128)(2,1)}, u32[]{:S(2)}, u32[]{:S(2)}) collective-permute-start(bf16[384,768]{1,0:T(8,128)(2,1)} %pad_maximum_fusion.9), channel_id=1, source_target_pairs={{0,1},{1,0},{2,3},{3,2},{4,5},{5,4},{6,7},{7,6},{8,9},{9,8},{10,11... | collective-permute-start | bytes 1769480 | tf_op jit(solution)/shard_map/ppermute | solution.py:25
  348.9 11.1 %collective-permute-start.50 = (bf16[384,768]{1,0:T(8,128)(2,1)}, bf16[384,768]{1,0:T(8,128)(2,1)}, u32[]{:S(2)}, u32[]{:S(2)}) collective-permute-start(bf16[384,768]{1,0:T(8,128)(2,1)} %collective-permute-done.38), channel_id=1, source_target_pairs={{0,1},{1,0},{2,3},{3,2},{4,5},{5,4},{6,7},{7,6},{8,9},{9,8},{10,11... | collective-permute-start | bytes 1769480 | tf_op jit(solution)/shard_map/ppermute | solution.py:25
  349.5 35.8 %all-to-all-start.3 = ((bf16[4,208,768]{2,1,0:T(8,128)(2,1)}), bf16[4,208,768]{2,1,0:T(8,128)(2,1)S(1)}, u32[]{:S(2)}, u32[]{:S(2)}) async-start(bf16[4,208,768]{2,1,0:T(8,128)(2,1)} %pad_maximum_fusion.1), calls=%async_computation.3 | async-start | bytes 2555904 | tf_op jit(solution)/shard_map/all_to_all | solution.py:496
  354.5 13.1 %collective-permute-start.47 = (bf16[8,32,768]{2,1,0:T(8,128)(2,1)}, bf16[8,32,768]{2,1,0:T(8,128)(2,1)}, u32[]{:S(2)}, u32[]{:S(2)}) collective-permute-start(bf16[8,32,768]{2,1,0:T(8,128)(2,1)} %get-tuple-element.255.refs_4_), channel_id=1, source_target_pairs={{0,2},{1,3},{2,0},{3,1},{4,6},{5,7},{6,4},{7,5},{8,10},{9,11},{10,... | collective-permute-start | bytes 1179656 | tf_op jit(solution)/shard_map/ppermute | solution.py:25
  355.1 20.1 %collective-permute-start.48 = (bf16[8,32,768]{2,1,0:T(8,128)(2,1)S(1)}, bf16[8,32,768]{2,1,0:T(8,128)(2,1)}, u32[]{:S(2)}, u32[]{:S(2)}) collective-permute-start(bf16[8,32,768]{2,1,0:T(8,128)(2,1)S(1)} %copy-done.5), channel_id=1, source_target_pairs={{0,2},{1,3},{2,0},{3,1},{4,6},{5,7},{6,4},{7,5},{8,10},{9,11},{10,... | collective-permute-start | bytes 1179656 | tf_op jit(solution)/shard_map/ppermute | solution.py:25
  364.8 15.5 %collective-permute-start.46 = (bf16[192,768]{1,0:T(8,128)(2,1)}, bf16[192,768]{1,0:T(8,128)(2,1)}, u32[]{:S(2)}, u32[]{:S(2)}) collective-permute-start(bf16[192,768]{1,0:T(8,128)(2,1)} %reduce_sum.44), channel_id=1, source_target_pairs={{0,2},{1,3},{2,0},{3,1},{4,6},{5,7},{6,4},{7,5},{8,10},{9,11},{10,... | collective-permute-start | bytes 884744 | tf_op jit(solution)/shard_map/ppermute | solution.py:25
  385.6 4.0 collective-permute-start.56
  385.7 3.9 collective-permute-start.57
  387.3 5.5 %collective-permute-start.52 = (bf16[2,8,32,768]{3,2,1,0:T(8,128)(2,1)S(1)}, bf16[2,8,32,768]{3,2,1,0:T(8,128)(2,1)S(1)}, u32[]{:S(2)}, u32[]{:S(2)}) collective-permute-start(bf16[2,8,32,768]{3,2,1,0:T(8,128)(2,1)S(1)} %pad_maximum_fusion.8), channel_id=1, source_target_pairs={{0,1},{1,0},{2,3},{3,2},{4,5},{5,4},{6,7},{7,6},{8,9},{9,8},{10,11... | collective-permute-start | bytes 2359304 | tf_op jit(solution)/shard_map/ppermute | solution.py:25
  388.5 4.2 %collective-permute-start.51 = (bf16[2,8,32,768]{3,2,1,0:T(8,128)(2,1)S(1)}, bf16[2,8,32,768]{3,2,1,0:T(8,128)(2,1)S(1)}, u32[]{:S(2)}, u32[]{:S(2)}) collective-permute-start(bf16[2,8,32,768]{3,2,1,0:T(8,128)(2,1)S(1)} %pad_maximum_fusion.7), channel_id=1, source_target_pairs={{0,1},{1,0},{2,3},{3,2},{4,5},{5,4},{6,7},{7,6},{8,9},{9,8},{10,11... | collective-permute-start | bytes 2359304 | tf_op jit(solution)/shard_map/ppermute | solution.py:25
  389.0 9.5 %collective-permute-start.53 = (bf16[208,768]{1,0:T(8,128)(2,1)S(1)}, bf16[208,768]{1,0:T(8,128)(2,1)S(1)}, u32[]{:S(2)}, u32[]{:S(2)}) collective-permute-start(bf16[208,768]{1,0:T(8,128)(2,1)S(1)} %reduce_sum.45), channel_id=1, source_target_pairs={{0,2},{1,3},{2,0},{3,1},{4,6},{5,7},{6,4},{7,5},{8,10},{9,11},{10,... | collective-permute-start | bytes 958472 | tf_op jit(solution)/shard_map/ppermute | solution.py:25
  398.5 2.0 collective-permute-start.54
  398.6 2.0 collective-permute-start.55
  (41 other events, 223.4 us)
where the time goes:
time: 411 us; the launch traced here: 403 us
  waiting for transfers between devices  163 us (40%)
  Pallas kernels  105 us (26%)
  starting transfers between devices  78.7 us (19%)
  other arithmetic  37.7 us (9%)
  local copies, waits for them, and re-layouts  16.9 us (4%)
    ppermute x58, waiting for transfers between devices, swap(): return lax.ppermute(value, axis, [(i, i ^ distance) for i in range(size)])  158 us
    pallas_call x10, Pallas kernels, run(): pl.pallas_call(body, grid=grid, in_specs=[spec for spec, _ in flat_in], o...  105 us
    ppermute x58, starting transfers between devices, swap(): return lax.ppermute(value, axis, [(i, i ^ distance) for i in range(size)])  50.9 us
    all_to_all x4, starting transfers between devices, over_slow(): lax.all_to_all(value, 'fsdp', 0, 0, axis_index_groups=groups, tiled=True)  23.4 us
  transfers between devices with their start and end apart: 63, of which 24 were waited for; matrix products, arithmetic and copies ran while one was open for 11% of the time, Pallas kernels for 26%

commit v1 on v0

--- a/solution.py
+++ b/solution.py
@@ -459,7 +459,7 @@
     wait_all(started)
 
 
-def run(kernel, inputs, outputs, scratch, copies, grid=()):
+def run(kernel, inputs, outputs, scratch, copies, grid=(), moved=0):
     def leaf(x):
         return isinstance(x, tuple) and len(x) == 2 and isinstance(x[0], pl.BlockSpec)
 
@@ -481,7 +481,7 @@
         scratch_shapes=scratch + [pltpu.SemaphoreType.DMA((copies,))],
         compiler_params=pltpu.CompilerParams(vmem_limit_bytes=56 * 1024 * 1024),
         cost_estimate=pl.CostEstimate(
-            flops=0, bytes_accessed=0, transcendentals=0
+            flops=0, bytes_accessed=moved, transcendentals=0
         ),
     )(*[x for _, x in flat_in])
     return jax.tree.unflatten(tree_out, found)
@@ -530,9 +530,10 @@
         if vectors is not None:
             self.vectors = vectors.astype(F32) + swap(vectors, "mem", 1).astype(F32)
 
-    def add_cores(self):
+    def add_cores(self, *others):
+        far = after(self.far, *others)
         self.out = [
-            (self.far[b].astype(F32) + self.sent[b + 1].astype(F32)).astype(BF)
+            (far[b].astype(F32) + self.sent[b + 1].astype(F32)).astype(BF)
             for b in range(self.fast - 1)
         ]
         return self.out
@@ -810,11 +811,11 @@
         1 + blocks,
     )
     in_scatter = scatter(in_grads, gx2)
-    in_sum = in_scatter.add_cores()
+    in_sum = in_scatter.add_cores(*out_scatter.came)
     in_scatter.send_fast()
     gx1, vecs_cross, dkv, dq2, grad_memory = run(
         cross_backward,
-        [(SMEM, where), (VMEM, x1), (VMEM, vec), (VMEM, after(gx2, *in_sum, *out_scatter.came)), (VMEM, q2)]
+        [(SMEM, where), (VMEM, x1), (VMEM, vec), (VMEM, after(gx2, *in_sum)), (VMEM, q2)]
         + [per_example(kv), per_example(p2), cross_weights],
         [
             flat(wide, F32),
@@ -826,9 +827,10 @@
         [square, scratch(*wide), scratch(per, total, width)],
         blocks,
         (examples // per,),
+        60_000_000,
     )
     in_scatter.came, _ = lax.optimization_barrier((in_scatter.came, gx1))
-    out_total = out_scatter.add_fast(gx1)
+    out_total = out_scatter.add_fast(*in_scatter.came)
     out_scatter.send_slow()
     mem_pieces = grad_memory[:1] + [swap(grad_memory[d], "mem", d) for d in range(1, mem)]
     grads = run(
@@ -839,11 +841,12 @@
         [square, scratch(width, examples * total), scratch(examples, total, width)],
         max(mem, blocks),
         (2,),
+        45_000_000,
     )
     out_final = out_scatter.add_slow()
     in_scatter.add_fast(out_final)
     in_scatter.send_slow()
-    cross_scatter = scatter(grads, out_final)
+    cross_scatter = scatter(grads, out_final, *mem_pieces[1:3])
     cross_sum = cross_scatter.add_cores()
     cross_scatter.send_fast()
     gx1 = after(gx1, *cross_sum)
@@ -855,8 +858,9 @@
         [flat((examples, length, width), BF), flat((16, width), BF)] + grads_like,
         [square, own_rows, square, scratch(rows, 3 * width), scratch(*wide)],
         1 + blocks,
-    )
-    self_scatter = scatter(grads, *mem_pieces[1:3], vectors=vecs_self)
+        moved=40_000_000,
+    )
+    self_scatter = scatter(grads, *mem_pieces[3:4], vectors=vecs_self)
     self_sum = self_scatter.add_cores()
     self_scatter.send_fast()
     cross_scatter.add_fast(*self_sum)
@@ -864,7 +868,7 @@
     in_final = in_scatter.add_slow(*self_sum)
     dense_sum = jnp.concatenate([out_final, in_final])
     dense_sum = Replicas(dense_sum, 2 * part, across)
-    self_total = self_scatter.add_fast(*dense_sum.halves, *mem_pieces[3:])
+    self_total = self_scatter.add_fast(*dense_sum.halves)
     self_scatter.send_slow()
     cross_sum = Replicas(cross_scatter.add_slow(self_total), part, across)
     suffix_rows = spread_across(after(suffix_part, self_total), mem)

time: 411 us -> 392 us (0.954)
  waiting for transfers between devices: 163 us -> 148 us
    ppermute x58, waiting for transfers between devices: 158 us -> 125 us  [swap(): return lax.ppermute(value, axis, [(i, i ^ distance) for i in range(size)])]
    all_to_all x4, waiting for transfers between devices: 5.01 us -> 22.2 us  [over_slow(): lax.all_to_all(value, 'fsdp', 0, 0, axis_index_groups=groups, tiled=True)]
  transfers between devices with their start and end apart: 63 -> 63, of which waited for: 24 -> 25; matrix products, arithmetic and copies ran while one was open for 11% -> 11% of each run, Pallas kernels for 26% -> 27%
where the time goes in v1:
time: 392 us; the launch traced here: 384 us
  waiting for transfers between devices  148 us (38%)
  Pallas kernels  105 us (27%)
  starting transfers between devices  76.7 us (20%)
  other arithmetic  37.6 us (10%)
  local copies, waits for them, and re-layouts  15.5 us (4%)
    ppermute x58, waiting for transfers between devices, swap(): return lax.ppermute(value, axis, [(i, i ^ distance) for i in range(size)])  125 us
    pallas_call x10, Pallas kernels, run(): pl.pallas_call(body, grid=grid, in_specs=[spec for spec, _ in flat_in], o...  105 us
    ppermute x58, starting transfers between devices, swap(): return lax.ppermute(value, axis, [(i, i ^ distance) for i in range(size)])  52.1 us
    all_to_all x4, waiting for transfers between devices, over_slow(): lax.all_to_all(value, 'fsdp', 0, 0, axis_index_groups=groups, tiled=True)  22.2 us
    all_to_all x4, starting transfers between devices, over_slow(): lax.all_to_all(value, 'fsdp', 0, 0, axis_index_groups=groups, tiled=True)  20.3 us
    convert_element_type x4, other arithmetic, add_fast(): self.total = total.astype(BF).reshape(self.slow, -1, total.shape[-1])  8.07 us
  transfers between devices with their start and end apart: 63, of which 25 were waited for; matrix products, arithmetic and copies ran while one was open for 11% of the time, Pallas kernels for 27%

profile of v1, /device:TPU:0, one launch (start us, length us, event | category | flops | bytes accessed | tf_op | source)
XLA Modules:
  0.0 384.1 jit_solution(3192811834729464462)
XLA Ops:
  0.8 4.4 %all-to-all-start = ((bf16[4,8,64,768]{3,2,1,0:T(8,128)(2,1)}), bf16[4,8,64,768]{3,2,1,0:T(8,128)(2,1)S(1)}, u32[]{:S(2)}, u32[]{:S(2)}) async-start(bf16[4,8,64,768]{3,2,1,0:T(8,128)(2,1)} %bitcast.73), calls=%async_computation | async-start | bytes 6291456 | tf_op jit(solution)/shard_map/all_to_all | solution.py:694
  6.4 2.6 collective-permute-start
  9.0 2.6 collective-permute-start.1
  11.6 12.0 %collective-permute-done = bf16[208,768]{1,0:T(8,128)(2,1)S(1)} collective-permute-done((bf16[208,768]{1,0:T(8,128)(2,1)S(1)}, bf16[208,768]{1,0:T(8,128)(2,1)S(1)}, u32[]{:S(2)}, u32[]{:S(2)}) %collective-permute-start) | collective-permute-done | bytes 319520 | tf_op jit(solution)/shard_map/ppermute | solution.py:25
  23.5 10.5 %collective-permute-done.1 = bf16[208,768]{1,0:T(8,128)(2,1)S(1)} collective-permute-done((bf16[208,768]{1,0:T(8,128)(2,1)S(1)}, bf16[208,768]{1,0:T(8,128)(2,1)S(1)}, u32[]{:S(2)}, u32[]{:S(2)}) %collective-permute-start.1) | collective-permute-done | bytes 319520 | tf_op jit(solution)/shard_map/ppermute | solution.py:25
  34.0 1.2 pad_maximum_fusion.refs_2_.refs_12_
  35.3 1.6 collective-permute-start.3
  37.8 6.6 %collective-permute-start.4 = (bf16[192,768]{1,0:T(8,128)(2,1)}, bf16[192,768]{1,0:T(8,128)(2,1)S(1)}, u32[]{:S(2)}, u32[]{:S(2)}) collective-permute-start(bf16[192,768]{1,0:T(8,128)(2,1)} %get-tuple-element.151), channel_id=1, source_target_pairs={{0,8},{4,12},{8,0},{12,4},{16,24},{20,28},{24,16},{28,20},{1,9},{5... | collective-permute-start | bytes 884744 | tf_op jit(solution)/shard_map/ppermute | solution.py:25
  45.4 1.5 collective-permute-start.6
  46.9 9.1 %collective-permute-done.4 = bf16[192,768]{1,0:T(8,128)(2,1)S(1)} collective-permute-done((bf16[192,768]{1,0:T(8,128)(2,1)}, bf16[192,768]{1,0:T(8,128)(2,1)S(1)}, u32[]{:S(2)}, u32[]{:S(2)}) %collective-permute-start.4) | collective-permute-done | bytes 294944 | tf_op jit(solution)/shard_map/ppermute | solution.py:25
  56.0 12.1 %collective-permute-done.5 = bf16[192,768]{1,0:T(8,128)(2,1)S(1)} collective-permute-done((bf16[192,768]{1,0:T(8,128)(2,1)}, bf16[192,768]{1,0:T(8,128)(2,1)S(1)}, u32[]{:S(2)}, u32[]{:S(2)}) %collective-permute-start.5) | collective-permute-done | bytes 294944 | tf_op jit(solution)/shard_map/ppermute | solution.py:25
  69.6 3.3 pad_maximum_fusion.2.refs_5_.refs_7_
  73.9 4.2 %collective-permute-start.10 = (bf16[192,768]{1,0:T(8,128)(2,1)S(1)}, bf16[192,768]{1,0:T(8,128)(2,1)}, u32[]{:S(2)}, u32[]{:S(2)}) collective-permute-start(bf16[192,768]{1,0:T(8,128)(2,1)S(1)} %get-tuple-element.160), channel_id=1, source_target_pairs={{0,8},{4,12},{8,0},{12,4},{16,24},{20,28},{24,16},{28,20},{1,9},{5... | collective-permute-start | bytes 884744 | tf_op jit(solution)/shard_map/ppermute | solution.py:25
  79.1 1.5 collective-permute-start.12
  81.2 7.7 %shard_map.373 = (f32[256,768]{1,0:T(8,128)}, bf16[256,768]{1,0:T(8,128)(2,1)}, bf16[256,2304]{1,0:T(8,128)(2,1)}, bf16[6,512,128]{2,1,0:T(8,128)(2,1)}, bf16[256,768]{1,0:T(8,128)(2,1)}, /*index=5*/f32[16,768]{1,0:T(8,128)}) custom-call(s32[4]{0:T(128)} %pad_add_fusion.1.refs_0_, bf16[32,32,768]{2,1,0:T(8,128)(2,1)} %refs_1_.5, ...), custom_call_target="tpu_custom_call" | custom-call | tf_op jit(solution)/shard_map/pallas_call | solution.py:475
  90.0 11.7 %collective-permute-done.11 = bf16[192,768]{1,0:T(8,128)(2,1)} collective-permute-done((bf16[192,768]{1,0:T(8,128)(2,1)S(1)}, bf16[192,768]{1,0:T(8,128)(2,1)}, u32[]{:S(2)}, u32[]{:S(2)}) %collective-permute-start.11) | collective-permute-done | bytes 294944 | tf_op jit(solution)/shard_map/ppermute | solution.py:25
  101.7 1.4 pad_maximum_fusion.3.refs_5_
  104.0 5.0 %collective-permute-start.16 = (bf16[192,768]{1,0:T(8,128)(2,1)S(1)}, bf16[192,768]{1,0:T(8,128)(2,1)S(1)}, u32[]{:S(2)}, u32[]{:S(2)}) collective-permute-start(bf16[192,768]{1,0:T(8,128)(2,1)S(1)} %slice_select_fusion), channel_id=1, source_target_pairs={{0,8},{4,12},{8,0},{12,4},{16,24},{20,28},{24,16},{28,20},{1,9},{5... | collective-permute-start | bytes 884744 | tf_op jit(solution)/shard_map/ppermute | solution.py:25
  110.1 1.4 collective-permute-start.18
  112.5 15.1 %shard_map.374 = (f32[256,768]{1,0:T(8,128)}, bf16[256,768]{1,0:T(8,128)(2,1)}, bf16[256,768]{1,0:T(8,128)(2,1)}, bf16[8,256,1536]{2,1,0:T(8,128)(2,1)}, bf16[8,...) custom-call(s32[4]{0:T(128)} %pad_add_fusion.1.refs_0_, s32[32]{0:T(128)} %refs_1_.4, ...), custom_call_target="tpu_custom_call" | custom-call | tf_op jit(solution)/shard_map/pallas_call | solution.py:475
  127.6 4.8 %collective-permute-done.17 = bf16[192,768]{1,0:T(8,128)(2,1)S(1)} collective-permute-done((bf16[192,768]{1,0:T(8,128)(2,1)S(1)}, bf16[192,768]{1,0:T(8,128)(2,1)S(1)}, u32[]{:S(2)}, u32[]{:S(2)}) %collective-permute-start.17) | collective-permute-done | bytes 294944 | tf_op jit(solution)/shard_map/ppermute | solution.py:25
  132.5 1.3 pad_maximum_fusion.4.refs_7_
  133.8 1.2 collective-permute-start.21
  140.7 13.6 %shard_map.375 = (bf16[256,768]{1,0:T(8,128)(2,1)}, bf16[256,3072]{1,0:T(8,128)(2,1)}, bf16[256,3072]{1,0:T(8,128)(2,1)}, bf16[4,2,96,768]{3,2,1,0:T(8,128)(2,1)...) custom-call(s32[4]{0:T(128)} %pad_add_fusion.1.refs_0_, ...), custom_call_target="tpu_custom_call" | custom-call | tf_op jit(solution)/shard_map/pallas_call | solution.py:475
  154.3 8.0 %collective-permute-done.21.refs_8_ = bf16[4,192,768]{2,1,0:T(8,128)(2,1)} collective-permute-done((bf16[4,192,768]{2,1,0:T(8,128)(2,1)}, bf16[4,192,768]{2,1,0:T(8,128)(2,1)}, u32[]{:S(2)}, u32[]{:S(2)}) %collective-permute-start.21) | collective-permute-done | bytes 1179680 | tf_op jit(solution)/shard_map/ppermute | solution.py:25
  163.4 1.2 collective-permute-done.22
  165.4 1.6 fusion.3
  167.0 1.3 collective-permute-start.26
  169.8 11.7 %shard_map.376 = (bf16[8,32,768]{2,1,0:T(8,128)(2,1)}, bf16[256,3072]{1,0:T(8,128)(2,1)}, f32[1,768]{1,0:T(1,128)}, f32[1,3072]{1,0:T(1,128)}, bf16[4,2,96,768]{...) custom-call(s32[4]{0:T(128)} %pad_add_fusion.1.refs_0_, ...), custom_call_target="tpu_custom_call" | custom-call | tf_op jit(solution)/shard_map/pallas_call | solution.py:475
  181.5 7.4 %shard_map.377 = (f32[256,768]{1,0:T(8,128)}, f32[2,768]{1,0:T(2,128)}) custom-call(s32[4]{0:T(128)} %pad_add_fusion.1.refs_0_, f32[256,768]{1,0:T(8,128)} %get-tuple-element.177.refs_1_, f32[16,768]{1,0:T(8,128)} %get-tuple-element.150.refs_3_.refs_2_, bf16[256,3072]{1,0:T(8,128)(2,1)} %get-tuple-element.181.refs_3_, bf16[32,32,768]{2,1,0:T(8,128)(2,1)} %refs_4_.3, ...), custom_call_target="tpu_custom_call" | custom-call | tf_op jit(solution)/shard_map/pallas_call | solution.py:475
  189.5 5.6 %collective-permute-done.26 = bf16[4,2,96,768]{3,2,1,0:T(8,128)(2,1)S(1)} collective-permute-done((bf16[4,2,96,768]{3,2,1,0:T(8,128)(2,1)S(1)}, bf16[4,2,96,768]{3,2,1,0:T(8,128)(2,1)S(1)}, u32[]{:S(2)}, u32[]{:S(2)}) %collective-permute-start.26) | collective-permute-done | bytes 1179680 | tf_op jit(solution)/shard_map/ppermute | solution.py:25
  195.4 1.3 collective-permute-start.29
  196.7 17.8 %shard_map.378 = (f32[256,768]{1,0:T(8,128)}, f32[2,768]{1,0:T(2,128)}, bf16[8,256,1536]{2,1,0:T(8,128)(2,1)}, bf16[256,768]{1,0:T(8,128)(2,1)}, bf16[8,64,768]{...) custom-call(s32[4]{0:T(128)} %pad_add_fusion.1.refs_0_, ...), custom_call_target="tpu_custom_call" | custom-call | bytes 60000000 | tf_op jit(solution)/shard_map/pallas_call | solution.py:475
  214.5 8.2 %collective-permute-done.29 = bf16[4,2,96,768]{3,2,1,0:T(8,128)(2,1)S(1)} collective-permute-done((bf16[4,2,96,768]{3,2,1,0:T(8,128)(2,1)S(1)}, bf16[4,2,96,768]{3,2,1,0:T(8,128)(2,1)S(1)}, u32[]{:S(2)}, u32[]{:S(2)}) %collective-permute-start.29) | collective-permute-done | bytes 1179680 | tf_op jit(solution)/shard_map/ppermute | solution.py:25
  222.6 1.5 add_convert_fusion.3
  224.1 8.1 %all-to-all-start.1 = ((bf16[4,192,768]{2,1,0:T(8,128)(2,1)}), bf16[4,192,768]{2,1,0:T(8,128)(2,1)S(1)}, u32[]{:S(2)}, u32[]{:S(2)}) async-start(bf16[4,192,768]{2,1,0:T(8,128)(2,1)} %bitcast.35), calls=%async_computation.1 | async-start | bytes 2359296 | tf_op jit(solution)/shard_map/all_to_all | solution.py:496
  232.7 1.4 collective-permute-start.32
  234.1 13.1 %shard_map.379 = (bf16[4,2,96,768]{3,2,1,0:T(8,128)(2,1)}, bf16[1,4,2,96,768]{4,3,2,1,0:T(8,128)(2,1)}, bf16[4,2,96,768]{3,2,1,0:T(8,128)(2,1)}, bf16[2,2,96,768]{3,2,1,0:T(8,128)(2,1)}, bf16[2,2,96,768]{3,2,1,0:T(8,128)(2,1)}) custom-call(s32[4]{0:T(128)} %pad_add_fusion.1.refs_0_, f32[256,768]{1,0:T(8,128)} %get-tuple-element.199.refs_3_.refs_1_, ...), custom_call_target="tpu_custom_call" | custom-call | bytes 45000000 | tf_op jit(solution)/shard_map/pallas_call | solution.py:475
  247.2 12.1 %all-to-all-done.1 = bf16[4,192,768]{2,1,0:T(8,128)(2,1)S(1)} async-done(((bf16[4,192,768]{2,1,0:T(8,128)(2,1)}), bf16[4,192,768]{2,1,0:T(8,128)(2,1)S(1)}, u32[]{:S(2)}, u32[]{:S(2)}) %all-to-all-start.1) | async-done | bytes 1179680 | tf_op jit(solution)/shard_map/all_to_all | solution.py:496
  261.1 3.1 add_convert_fusion.2
  264.2 3.9 %all-to-all-start.2 = ((bf16[4,192,768]{2,1,0:T(8,128)(2,1)}), bf16[4,192,768]{2,1,0:T(8,128)(2,1)S(1)}, u32[]{:S(2)}, u32[]{:S(2)}) async-start(bf16[4,192,768]{2,1,0:T(8,128)(2,1)} %bitcast.37), calls=%async_computation.2 | async-start | bytes 2359296 | tf_op jit(solution)/shard_map/all_to_all | solution.py:496
  268.6 1.5 fusion.1
  270.2 1.3 collective-permute-start.45
  271.5 11.7 %shard_map.380 = (bf16[8,32,768]{2,1,0:T(8,128)(2,1)}, bf16[16,768]{1,0:T(8,128)(2,1)}, bf16[4,2,96,768]{3,2,1,0:T(8,128)(2,1)}, bf16[1,4,2,96,768]{4,3,2,1,0:T(...) custom-call(s32[4]{0:T(128)} %pad_add_fusion.1.refs_0_, ...), custom_call_target="tpu_custom_call" | custom-call | bytes 40000000 | tf_op jit(solution)/shard_map/pallas_call | solution.py:475
  283.8 1.7 collective-permute-done.37
  286.3 2.7 fusion
  289.8 9.3 %collective-permute-done.45 = bf16[4,2,96,768]{3,2,1,0:T(8,128)(2,1)S(1)} collective-permute-done((bf16[4,2,96,768]{3,2,1,0:T(8,128)(2,1)S(1)}, bf16[4,2,96,768]{3,2,1,0:T(8,128)(2,1)S(1)}, u32[]{:S(2)}, u32[]{:S(2)}) %collective-permute-start.45) | collective-permute-done | bytes 1179680 | tf_op jit(solution)/shard_map/ppermute | solution.py:25
  299.1 1.5 add_convert_fusion
  300.5 4.8 %all-to-all-start.4 = ((bf16[4,192,768]{2,1,0:T(8,128)(2,1)}), bf16[4,192,768]{2,1,0:T(8,128)(2,1)S(1)}, u32[]{:S(2)}, u32[]{:S(2)}) async-start(bf16[4,192,768]{2,1,0:T(8,128)(2,1)} %bitcast.40), calls=%async_computation.4 | async-start | bytes 2359296 | tf_op jit(solution)/shard_map/all_to_all | solution.py:496
  308.3 1.3 collective-permute-start.42
  309.6 12.9 %collective-permute-done.39 = bf16[384,768]{1,0:T(8,128)(2,1)} collective-permute-done((bf16[384,768]{1,0:T(8,128)(2,1)}, bf16[384,768]{1,0:T(8,128)(2,1)}, u32[]{:S(2)}, u32[]{:S(2)}) %collective-permute-start.39) | collective-permute-done | bytes 589856 | tf_op jit(solution)/shard_map/ppermute | solution.py:25
  322.5 1.5 collective-permute-done.42
  324.0 2.1 add_convert_fusion.1
  327.8 5.2 %all-to-all-done.4 = bf16[4,192,768]{2,1,0:T(8,128)(2,1)S(1)} async-done(((bf16[4,192,768]{2,1,0:T(8,128)(2,1)}), bf16[4,192,768]{2,1,0:T(8,128)(2,1)S(1)}, u32[]{:S(2)}, u32[]{:S(2)}) %all-to-all-start.4) | async-done | bytes 1179680 | tf_op jit(solution)/shard_map/all_to_all | solution.py:496
  333.0 3.5 all-to-all-start.3
  337.2 1.4 collective-permute-start.48
  338.6 3.5 shard_map.381
  342.1 1.7 fusion.5
  347.6 2.2 pad_maximum_fusion.5
  349.7 7.6 %collective-permute-done.48.refs_2_ = bf16[8,32,768]{2,1,0:T(8,128)(2,1)} collective-permute-done((bf16[8,32,768]{2,1,0:T(8,128)(2,1)S(1)}, bf16[8,32,768]{2,1,0:T(8,128)(2,1)}, u32[]{:S(2)}, u32[]{:S(2)}) %collective-permute-start.48) | collective-permute-done | bytes 393248 | tf_op jit(solution)/shard_map/ppermute | solution.py:25
  357.4 4.3 %collective-permute-done.46 = bf16[192,768]{1,0:T(8,128)(2,1)} collective-permute-done((bf16[192,768]{1,0:T(8,128)(2,1)}, bf16[192,768]{1,0:T(8,128)(2,1)}, u32[]{:S(2)}, u32[]{:S(2)}) %collective-permute-start.46) | collective-permute-done | bytes 294944 | tf_op jit(solution)/shard_map/ppermute | solution.py:25
  361.7 4.9 %all-to-all-done.3 = bf16[4,208,768]{2,1,0:T(8,128)(2,1)S(1)} async-done(((bf16[4,208,768]{2,1,0:T(8,128)(2,1)}), bf16[4,208,768]{2,1,0:T(8,128)(2,1)S(1)}, u32[]{:S(2)}, u32[]{:S(2)}) %all-to-all-start.3) | async-done | bytes 1277984 | tf_op jit(solution)/shard_map/all_to_all | solution.py:496
  370.9 1.4 fusion.8
  375.8 3.4 shard_map.382
  (217 shorter events, 47.6 us)
Async XLA Ops:
  0.8 68.8 %all-to-all-start = ((bf16[4,8,64,768]{3,2,1,0:T(8,128)(2,1)}), bf16[4,8,64,768]{3,2,1,0:T(8,128)(2,1)S(1)}, u32[]{:S(2)}, u32[]{:S(2)}) async-start(bf16[4,8,64,768]{3,2,1,0:T(8,128)(2,1)} %bitcast.73), calls=%async_computation | async-start | bytes 6291456 | tf_op jit(solution)/shard_map/all_to_all | solution.py:694
  6.4 17.2 %collective-permute-start = (bf16[208,768]{1,0:T(8,128)(2,1)S(1)}, bf16[208,768]{1,0:T(8,128)(2,1)S(1)}, u32[]{:S(2)}, u32[]{:S(2)}) collective-permute-start(bf16[208,768]{1,0:T(8,128)(2,1)S(1)} %pad_maximum_fusion.10), channel_id=1, source_target_pairs={{0,8},{4,12},{8,0},{12,4},{16,24},{20,28},{24,16},{28,20},{1,9},{5... | collective-permute-start | bytes 958472 | tf_op jit(solution)/shard_map/ppermute | solution.py:25
  9.0 25.0 %collective-permute-start.1 = (bf16[208,768]{1,0:T(8,128)(2,1)S(1)}, bf16[208,768]{1,0:T(8,128)(2,1)S(1)}, u32[]{:S(2)}, u32[]{:S(2)}) collective-permute-start(bf16[208,768]{1,0:T(8,128)(2,1)S(1)} %pad_maximum_fusion.10), channel_id=1, source_target_pairs={{0,16},{4,20},{8,24},{12,28},{16,0},{20,4},{24,8},{28,12},{1,17},{... | collective-permute-start | bytes 958472 | tf_op jit(solution)/shard_map/ppermute | solution.py:25
  11.6 22.4 %collective-permute-start.2 = (bf16[208,768]{1,0:T(8,128)(2,1)S(1)}, bf16[208,768]{1,0:T(8,128)(2,1)S(1)}, u32[]{:S(2)}, u32[]{:S(2)}) collective-permute-start(bf16[208,768]{1,0:T(8,128)(2,1)S(1)} %pad_maximum_fusion.10), channel_id=1, source_target_pairs={{0,24},{4,28},{8,16},{12,20},{16,8},{20,12},{24,0},{28,4},{1,25},{... | collective-permute-start | bytes 958472 | tf_op jit(solution)/shard_map/ppermute | solution.py:25
  35.3 34.3 %collective-permute-start.3 = (bf16[4,208,768]{2,1,0:T(8,128)(2,1)}, bf16[4,208,768]{2,1,0:T(8,128)(2,1)}, u32[]{:S(2)}, u32[]{:S(2)}) collective-permute-start(bf16[4,208,768]{2,1,0:T(8,128)(2,1)} %pad_maximum_fusion.refs_2_.refs_12_), channel_id=1, source_target_pairs={{0,4},{4,0},{8,12},{12,8},{16,20},{20,16},{24,28},{28,24},{1,5},{5... | collective-permute-start | bytes 3833864 | tf_op jit(solution)/shard_map/ppermute | solution.py:25
  37.8 18.2 %collective-permute-start.4 = (bf16[192,768]{1,0:T(8,128)(2,1)}, bf16[192,768]{1,0:T(8,128)(2,1)S(1)}, u32[]{:S(2)}, u32[]{:S(2)}) collective-permute-start(bf16[192,768]{1,0:T(8,128)(2,1)} %get-tuple-element.151), channel_id=1, source_target_pairs={{0,8},{4,12},{8,0},{12,4},{16,24},{20,28},{24,16},{28,20},{1,9},{5... | collective-permute-start | bytes 884744 | tf_op jit(solution)/shard_map/ppermute | solution.py:25
  44.4 23.7 %collective-permute-start.5 = (bf16[192,768]{1,0:T(8,128)(2,1)}, bf16[192,768]{1,0:T(8,128)(2,1)S(1)}, u32[]{:S(2)}, u32[]{:S(2)}) collective-permute-start(bf16[192,768]{1,0:T(8,128)(2,1)} %get-tuple-element.151), channel_id=1, source_target_pairs={{0,16},{4,20},{8,24},{12,28},{16,0},{20,4},{24,8},{28,12},{1,17},{... | collective-permute-start | bytes 884744 | tf_op jit(solution)/shard_map/ppermute | solution.py:25
  45.4 22.7 %collective-permute-start.6 = (bf16[192,768]{1,0:T(8,128)(2,1)}, bf16[192,768]{1,0:T(8,128)(2,1)S(1)}, u32[]{:S(2)}, u32[]{:S(2)}) collective-permute-start(bf16[192,768]{1,0:T(8,128)(2,1)} %get-tuple-element.151), channel_id=1, source_target_pairs={{0,24},{4,28},{8,16},{12,20},{16,8},{20,12},{24,0},{28,4},{1,25},{... | collective-permute-start | bytes 884744 | tf_op jit(solution)/shard_map/ppermute | solution.py:25
  46.9 32.2 %collective-permute-start.7 = (bf16[4,208,768]{2,1,0:T(8,128)(2,1)}, bf16[4,208,768]{2,1,0:T(8,128)(2,1)}, u32[]{:S(2)}, u32[]{:S(2)}) collective-permute-start(bf16[4,208,768]{2,1,0:T(8,128)(2,1)} %pad_maximum_fusion.refs_2_.refs_12_), channel_id=1, source_target_pairs={{0,1},{1,0},{2,3},{3,2},{4,5},{5,4},{6,7},{7,6},{8,9},{9,8},{10,11... | collective-permute-start | bytes 3833864 | tf_op jit(solution)/shard_map/ppermute | solution.py:25
  69.6 11.1 %collective-permute-start.8 = (bf16[4,208,768]{2,1,0:T(8,128)(2,1)}, bf16[4,208,768]{2,1,0:T(8,128)(2,1)}, u32[]{:S(2)}, u32[]{:S(2)}) collective-permute-start(bf16[4,208,768]{2,1,0:T(8,128)(2,1)} %collective-permute-done.3.refs_3_.refs_13_), channel_id=1, source_target_pairs={{0,1},{1,0},{2,3},{3,2},{4,5},{5,4},{6,7},{7,6},{8,9},{9,8},{10,11... | collective-permute-start | bytes 3833864 | tf_op jit(solution)/shard_map/ppermute | solution.py:25
  72.9 28.8 %collective-permute-start.9 = (bf16[4,192,768]{2,1,0:T(8,128)(2,1)}, bf16[4,192,768]{2,1,0:T(8,128)(2,1)}, u32[]{:S(2)}, u32[]{:S(2)}) collective-permute-start(bf16[4,192,768]{2,1,0:T(8,128)(2,1)} %pad_maximum_fusion.2.refs_5_.refs_7_), channel_id=1, source_target_pairs={{0,4},{4,0},{8,12},{12,8},{16,20},{20,16},{24,28},{28,24},{1,5},{5... | collective-permute-start | bytes 3538952 | tf_op jit(solution)/shard_map/ppermute | solution.py:25
  73.9 16.1 %collective-permute-start.10 = (bf16[192,768]{1,0:T(8,128)(2,1)S(1)}, bf16[192,768]{1,0:T(8,128)(2,1)}, u32[]{:S(2)}, u32[]{:S(2)}) collective-permute-start(bf16[192,768]{1,0:T(8,128)(2,1)S(1)} %get-tuple-element.160), channel_id=1, source_target_pairs={{0,8},{4,12},{8,0},{12,4},{16,24},{20,28},{24,16},{28,20},{1,9},{5... | collective-permute-start | bytes 884744 | tf_op jit(solution)/shard_map/ppermute | solution.py:25
  78.1 23.6 %collective-permute-start.11 = (bf16[192,768]{1,0:T(8,128)(2,1)S(1)}, bf16[192,768]{1,0:T(8,128)(2,1)}, u32[]{:S(2)}, u32[]{:S(2)}) collective-permute-start(bf16[192,768]{1,0:T(8,128)(2,1)S(1)} %get-tuple-element.160), channel_id=1, source_target_pairs={{0,16},{4,20},{8,24},{12,28},{16,0},{20,4},{24,8},{28,12},{1,17},{... | collective-permute-start | bytes 884744 | tf_op jit(solution)/shard_map/ppermute | solution.py:25
  79.1 22.6 %collective-permute-start.12 = (bf16[192,768]{1,0:T(8,128)(2,1)S(1)}, bf16[192,768]{1,0:T(8,128)(2,1)}, u32[]{:S(2)}, u32[]{:S(2)}) collective-permute-start(bf16[192,768]{1,0:T(8,128)(2,1)S(1)} %get-tuple-element.160), channel_id=1, source_target_pairs={{0,24},{4,28},{8,16},{12,20},{16,8},{20,12},{24,0},{28,4},{1,25},{... | collective-permute-start | bytes 884744 | tf_op jit(solution)/shard_map/ppermute | solution.py:25
  80.6 29.5 %collective-permute-start.13 = (bf16[4,192,768]{2,1,0:T(8,128)(2,1)}, bf16[4,192,768]{2,1,0:T(8,128)(2,1)}, u32[]{:S(2)}, u32[]{:S(2)}) collective-permute-start(bf16[4,192,768]{2,1,0:T(8,128)(2,1)} %pad_maximum_fusion.2.refs_5_.refs_7_), channel_id=1, source_target_pairs={{0,1},{1,0},{2,3},{3,2},{4,5},{5,4},{6,7},{7,6},{8,9},{9,8},{10,11... | collective-permute-start | bytes 3538952 | tf_op jit(solution)/shard_map/ppermute | solution.py:25
  101.7 9.7 %collective-permute-start.14 = (bf16[4,192,768]{2,1,0:T(8,128)(2,1)}, bf16[4,192,768]{2,1,0:T(8,128)(2,1)S(1)}, u32[]{:S(2)}, u32[]{:S(2)}) collective-permute-start(bf16[4,192,768]{2,1,0:T(8,128)(2,1)} %collective-permute-done.9.refs_6_.refs_8_), channel_id=1, source_target_pairs={{0,1},{1,0},{2,3},{3,2},{4,5},{5,4},{6,7},{7,6},{8,9},{9,8},{10,11... | collective-permute-start | bytes 3538952 | tf_op jit(solution)/shard_map/ppermute | solution.py:25
  103.1 29.3 %collective-permute-start.15 = (bf16[4,192,768]{2,1,0:T(8,128)(2,1)S(1)}, bf16[4,192,768]{2,1,0:T(8,128)(2,1)S(1)}, u32[]{:S(2)}, u32[]{:S(2)}) collective-permute-start(bf16[4,192,768]{2,1,0:T(8,128)(2,1)S(1)} %pad_maximum_fusion.3.refs_5_), channel_id=1, source_target_pairs={{0,4},{4,0},{8,12},{12,8},{16,20},{20,16},{24,28},{28,24},{1,5},{5... | collective-permute-start | bytes 3538952 | tf_op jit(solution)/shard_map/ppermute | solution.py:25
  104.0 23.6 %collective-permute-start.16 = (bf16[192,768]{1,0:T(8,128)(2,1)S(1)}, bf16[192,768]{1,0:T(8,128)(2,1)S(1)}, u32[]{:S(2)}, u32[]{:S(2)}) collective-permute-start(bf16[192,768]{1,0:T(8,128)(2,1)S(1)} %slice_select_fusion), channel_id=1, source_target_pairs={{0,8},{4,12},{8,0},{12,4},{16,24},{20,28},{24,16},{28,20},{1,9},{5... | collective-permute-start | bytes 884744 | tf_op jit(solution)/shard_map/ppermute | solution.py:25
  109.0 23.4 %collective-permute-start.17 = (bf16[192,768]{1,0:T(8,128)(2,1)S(1)}, bf16[192,768]{1,0:T(8,128)(2,1)S(1)}, u32[]{:S(2)}, u32[]{:S(2)}) collective-permute-start(bf16[192,768]{1,0:T(8,128)(2,1)S(1)} %slice_select_fusion), channel_id=1, source_target_pairs={{0,16},{4,20},{8,24},{12,28},{16,0},{20,4},{24,8},{28,12},{1,17},{... | collective-permute-start | bytes 884744 | tf_op jit(solution)/shard_map/ppermute | solution.py:25
  110.1 22.3 %collective-permute-start.18 = (bf16[192,768]{1,0:T(8,128)(2,1)S(1)}, bf16[192,768]{1,0:T(8,128)(2,1)S(1)}, u32[]{:S(2)}, u32[]{:S(2)}) collective-permute-start(bf16[192,768]{1,0:T(8,128)(2,1)S(1)} %slice_select_fusion), channel_id=1, source_target_pairs={{0,24},{4,28},{8,16},{12,20},{16,8},{20,12},{24,0},{28,4},{1,25},{... | collective-permute-start | bytes 884744 | tf_op jit(solution)/shard_map/ppermute | solution.py:25
  111.5 28.3 %collective-permute-start.19 = (bf16[4,192,768]{2,1,0:T(8,128)(2,1)S(1)}, bf16[4,192,768]{2,1,0:T(8,128)(2,1)}, u32[]{:S(2)}, u32[]{:S(2)}) collective-permute-start(bf16[4,192,768]{2,1,0:T(8,128)(2,1)S(1)} %pad_maximum_fusion.3.refs_5_), channel_id=1, source_target_pairs={{0,1},{1,0},{2,3},{3,2},{4,5},{5,4},{6,7},{7,6},{8,9},{9,8},{10,11... | collective-permute-start | bytes 3538952 | tf_op jit(solution)/shard_map/ppermute | solution.py:25
  132.4 7.3 %collective-permute-start.20 = (bf16[4,192,768]{2,1,0:T(8,128)(2,1)S(1)}, bf16[4,192,768]{2,1,0:T(8,128)(2,1)S(1)}, u32[]{:S(2)}, u32[]{:S(2)}) collective-permute-start(bf16[4,192,768]{2,1,0:T(8,128)(2,1)S(1)} %collective-permute-done.15.refs_6_), channel_id=1, source_target_pairs={{0,1},{1,0},{2,3},{3,2},{4,5},{5,4},{6,7},{7,6},{8,9},{9,8},{10,11... | collective-permute-start | bytes 3538952 | tf_op jit(solution)/shard_map/ppermute | solution.py:25
  133.8 28.5 %collective-permute-start.21 = (bf16[4,192,768]{2,1,0:T(8,128)(2,1)}, bf16[4,192,768]{2,1,0:T(8,128)(2,1)}, u32[]{:S(2)}, u32[]{:S(2)}) collective-permute-start(bf16[4,192,768]{2,1,0:T(8,128)(2,1)} %pad_maximum_fusion.4.refs_7_), channel_id=1, source_target_pairs={{0,4},{4,0},{8,12},{12,8},{16,20},{20,16},{24,28},{28,24},{1,5},{5... | collective-permute-start | bytes 3538952 | tf_op jit(solution)/shard_map/ppermute | solution.py:25
  162.3 2.2 collective-permute-start.22
  162.3 3.1 collective-permute-start.23
  162.9 5.4 %collective-permute-start.24 = (bf16[4,192,768]{2,1,0:T(8,128)(2,1)}, bf16[4,192,768]{2,1,0:T(8,128)(2,1)S(1)}, u32[]{:S(2)}, u32[]{:S(2)}) collective-permute-start(bf16[4,192,768]{2,1,0:T(8,128)(2,1)} %pad_maximum_fusion.4.refs_7_), channel_id=1, source_target_pairs={{0,1},{1,0},{2,3},{3,2},{4,5},{5,4},{6,7},{7,6},{8,9},{9,8},{10,11... | collective-permute-start | bytes 3538952 | tf_op jit(solution)/shard_map/ppermute | solution.py:25
  162.9 5.9 %collective-permute-start.25 = (bf16[4,192,768]{2,1,0:T(8,128)(2,1)}, bf16[4,192,768]{2,1,0:T(8,128)(2,1)S(1)}, u32[]{:S(2)}, u32[]{:S(2)}) collective-permute-start(bf16[4,192,768]{2,1,0:T(8,128)(2,1)} %collective-permute-done.21.refs_8_), channel_id=1, source_target_pairs={{0,1},{1,0},{2,3},{3,2},{4,5},{5,4},{6,7},{7,6},{8,9},{9,8},{10,11... | collective-permute-start | bytes 3538952 | tf_op jit(solution)/shard_map/ppermute | solution.py:25
  167.0 28.1 %collective-permute-start.26 = (bf16[4,2,96,768]{3,2,1,0:T(8,128)(2,1)S(1)}, bf16[4,2,96,768]{3,2,1,0:T(8,128)(2,1)S(1)}, u32[]{:S(2)}, u32[]{:S(2)}) collective-permute-start(bf16[4,2,96,768]{3,2,1,0:T(8,128)(2,1)S(1)} %fusion.3), channel_id=1, source_target_pairs={{0,4},{4,0},{8,12},{12,8},{16,20},{20,16},{24,28},{28,24},{1,5},{5... | collective-permute-start | bytes 3538952 | tf_op jit(solution)/shard_map/ppermute | solution.py:25
  188.9 6.2 %collective-permute-start.27 = (bf16[2,2,96,768]{3,2,1,0:T(8,128)(2,1)S(1)}, bf16[2,2,96,768]{3,2,1,0:T(8,128)(2,1)S(1)}, u32[]{:S(2)}, u32[]{:S(2)}) collective-permute-start(bf16[2,2,96,768]{3,2,1,0:T(8,128)(2,1)S(1)} %copy-done.41), channel_id=1, source_target_pairs={{0,1},{1,0},{2,3},{3,2},{4,5},{5,4},{6,7},{7,6},{8,9},{9,8},{10,11... | collective-permute-start | bytes 1769480 | tf_op jit(solution)/shard_map/ppermute | solution.py:25
  189.1 6.0 %collective-permute-start.28 = (bf16[2,2,96,768]{3,2,1,0:T(8,128)(2,1)S(1)}, bf16[2,2,96,768]{3,2,1,0:T(8,128)(2,1)S(1)}, u32[]{:S(2)}, u32[]{:S(2)}) collective-permute-start(bf16[2,2,96,768]{3,2,1,0:T(8,128)(2,1)S(1)} %copy-done.40), channel_id=1, source_target_pairs={{0,1},{1,0},{2,3},{3,2},{4,5},{5,4},{6,7},{7,6},{8,9},{9,8},{10,11... | collective-permute-start | bytes 1769480 | tf_op jit(solution)/shard_map/ppermute | solution.py:25
  195.4 27.2 %collective-permute-start.29 = (bf16[4,2,96,768]{3,2,1,0:T(8,128)(2,1)S(1)}, bf16[4,2,96,768]{3,2,1,0:T(8,128)(2,1)S(1)}, u32[]{:S(2)}, u32[]{:S(2)}) collective-permute-start(bf16[4,2,96,768]{3,2,1,0:T(8,128)(2,1)S(1)} %fusion.2), channel_id=1, source_target_pairs={{0,4},{4,0},{8,12},{12,8},{16,20},{20,16},{24,28},{28,24},{1,5},{5... | collective-permute-start | bytes 3538952 | tf_op jit(solution)/shard_map/ppermute | solution.py:25
  196.7 25.9 %collective-permute-start.30 = (bf16[4,2,96,768]{3,2,1,0:T(8,128)(2,1)S(1)}, bf16[4,2,96,768]{3,2,1,0:T(8,128)(2,1)S(1)}, u32[]{:S(2)}, u32[]{:S(2)}) collective-permute-start(bf16[4,2,96,768]{3,2,1,0:T(8,128)(2,1)S(1)} %copy-done.39), channel_id=1, source_target_pairs={{0,1},{1,0},{2,3},{3,2},{4,5},{5,4},{6,7},{7,6},{8,9},{9,8},{10,11... | collective-permute-start | bytes 3538952 | tf_op jit(solution)/shard_map/ppermute | solution.py:25
  196.7 25.9 %copy-start.11 = (bf16[4,2,96,768]{3,2,1,0:T(8,128)(2,1)S(1)}, bf16[4,2,96,768]{3,2,1,0:T(8,128)(2,1)}, u32[]{:S(2)}) copy-start(bf16[4,2,96,768]{3,2,1,0:T(8,128)(2,1)} %get-tuple-element.196) | copy-start | bytes 3538948
  224.1 35.2 %all-to-all-start.1 = ((bf16[4,192,768]{2,1,0:T(8,128)(2,1)}), bf16[4,192,768]{2,1,0:T(8,128)(2,1)S(1)}, u32[]{:S(2)}, u32[]{:S(2)}) async-start(bf16[4,192,768]{2,1,0:T(8,128)(2,1)} %bitcast.35), calls=%async_computation.1 | async-start | bytes 2359296 | tf_op jit(solution)/shard_map/all_to_all | solution.py:496
  232.2 28.9 %collective-permute-start.35 = (bf16[4,2,96,768]{3,2,1,0:T(8,128)(2,1)}, bf16[4,2,96,768]{3,2,1,0:T(8,128)(2,1)}, u32[]{:S(2)}, u32[]{:S(2)}) collective-permute-start(bf16[4,2,96,768]{3,2,1,0:T(8,128)(2,1)} %get-tuple-element.224), channel_id=1, source_target_pairs={{0,1},{1,0},{2,3},{3,2},{4,5},{5,4},{6,7},{7,6},{8,9},{9,8},{10,11... | collective-permute-start | bytes 3538952 | tf_op jit(solution)/shard_map/ppermute | solution.py:25
  232.2 27.2 %collective-permute-start.31 = (bf16[8,64,768]{2,1,0:T(8,128)(2,1)}, bf16[8,64,768]{2,1,0:T(8,128)(2,1)S(1)}, u32[]{:S(2)}, u32[]{:S(2)}) collective-permute-start(bf16[8,64,768]{2,1,0:T(8,128)(2,1)} %get-tuple-element.206), channel_id=1, source_target_pairs={{0,1},{1,0},{2,3},{3,2},{4,5},{5,4},{6,7},{7,6},{8,9},{9,8},{10,11... | collective-permute-start | bytes 2359304 | tf_op jit(solution)/shard_map/ppermute | solution.py:25
  232.7 26.8 %collective-permute-start.32 = (bf16[8,64,768]{2,1,0:T(8,128)(2,1)}, bf16[8,64,768]{2,1,0:T(8,128)(2,1)}, u32[]{:S(2)}, u32[]{:S(2)}) collective-permute-start(bf16[8,64,768]{2,1,0:T(8,128)(2,1)} %get-tuple-element.207), channel_id=1, source_target_pairs={{0,2},{1,3},{2,0},{3,1},{4,6},{5,7},{6,4},{7,5},{8,10},{9,11},{10,... | collective-permute-start | bytes 2359304 | tf_op jit(solution)/shard_map/ppermute | solution.py:25
  259.5 9.2 %collective-permute-start.33 = (bf16[2,2,96,768]{3,2,1,0:T(8,128)(2,1)}, bf16[2,2,96,768]{3,2,1,0:T(8,128)(2,1)}, u32[]{:S(2)}, u32[]{:S(2)}) collective-permute-start(bf16[2,2,96,768]{3,2,1,0:T(8,128)(2,1)} %get-tuple-element.208), channel_id=1, source_target_pairs={{0,1},{1,0},{2,3},{3,2},{4,5},{5,4},{6,7},{7,6},{8,9},{9,8},{10,11... | collective-permute-start | bytes 1769480 | tf_op jit(solution)/shard_map/ppermute | solution.py:25
  259.6 9.1 %collective-permute-start.34 = (bf16[2,2,96,768]{3,2,1,0:T(8,128)(2,1)}, bf16[2,2,96,768]{3,2,1,0:T(8,128)(2,1)}, u32[]{:S(2)}, u32[]{:S(2)}) collective-permute-start(bf16[2,2,96,768]{3,2,1,0:T(8,128)(2,1)} %get-tuple-element.210), channel_id=1, source_target_pairs={{0,1},{1,0},{2,3},{3,2},{4,5},{5,4},{6,7},{7,6},{8,9},{9,8},{10,11... | collective-permute-start | bytes 1769480 | tf_op jit(solution)/shard_map/ppermute | solution.py:25
  260.1 23.1 %collective-permute-start.36 = (bf16[8,64,768]{2,1,0:T(8,128)(2,1)}, bf16[8,64,768]{2,1,0:T(8,128)(2,1)}, u32[]{:S(2)}, u32[]{:S(2)}) collective-permute-start(bf16[8,64,768]{2,1,0:T(8,128)(2,1)} %get-tuple-element.227), channel_id=1, source_target_pairs={{0,3},{1,2},{2,1},{3,0},{4,7},{5,6},{6,5},{7,4},{8,11},{9,10},{10,... | collective-permute-start | bytes 2359304 | tf_op jit(solution)/shard_map/ppermute | solution.py:25
  264.2 36.3 %all-to-all-start.2 = ((bf16[4,192,768]{2,1,0:T(8,128)(2,1)}), bf16[4,192,768]{2,1,0:T(8,128)(2,1)S(1)}, u32[]{:S(2)}, u32[]{:S(2)}) async-start(bf16[4,192,768]{2,1,0:T(8,128)(2,1)} %bitcast.37), calls=%async_computation.2 | async-start | bytes 2359296 | tf_op jit(solution)/shard_map/all_to_all | solution.py:496
  268.1 21.6 %collective-permute-start.44 = (bf16[4,2,96,768]{3,2,1,0:T(8,128)(2,1)}, bf16[4,2,96,768]{3,2,1,0:T(8,128)(2,1)S(1)}, u32[]{:S(2)}, u32[]{:S(2)}) collective-permute-start(bf16[4,2,96,768]{3,2,1,0:T(8,128)(2,1)} %get-tuple-element.243), channel_id=1, source_target_pairs={{0,1},{1,0},{2,3},{3,2},{4,5},{5,4},{6,7},{7,6},{8,9},{9,8},{10,11... | collective-permute-start | bytes 3538952 | tf_op jit(solution)/shard_map/ppermute | solution.py:25
  270.2 28.9 %collective-permute-start.45 = (bf16[4,2,96,768]{3,2,1,0:T(8,128)(2,1)S(1)}, bf16[4,2,96,768]{3,2,1,0:T(8,128)(2,1)S(1)}, u32[]{:S(2)}, u32[]{:S(2)}) collective-permute-start(bf16[4,2,96,768]{3,2,1,0:T(8,128)(2,1)S(1)} %fusion.1), channel_id=1, source_target_pairs={{0,4},{4,0},{8,12},{12,8},{16,20},{20,16},{24,28},{28,24},{1,5},{5... | collective-permute-start | bytes 3538952 | tf_op jit(solution)/shard_map/ppermute | solution.py:25
  283.2 2.3 collective-permute-start.37
  283.3 3.0 collective-permute-start.38
  289.0 35.0 %collective-permute-start.43 = (bf16[4,2,96,768]{3,2,1,0:T(8,128)(2,1)}, bf16[4,2,96,768]{3,2,1,0:T(8,128)(2,1)}, u32[]{:S(2)}, u32[]{:S(2)}) collective-permute-start(bf16[4,2,96,768]{3,2,1,0:T(8,128)(2,1)} %fusion), channel_id=1, source_target_pairs={{0,4},{4,0},{8,12},{12,8},{16,20},{20,16},{24,28},{28,24},{1,5},{5... | collective-permute-start | bytes 3538952 | tf_op jit(solution)/shard_map/ppermute | solution.py:25
  300.5 32.4 %all-to-all-start.4 = ((bf16[4,192,768]{2,1,0:T(8,128)(2,1)}), bf16[4,192,768]{2,1,0:T(8,128)(2,1)S(1)}, u32[]{:S(2)}, u32[]{:S(2)}) async-start(bf16[4,192,768]{2,1,0:T(8,128)(2,1)} %bitcast.40), calls=%async_computation.4 | async-start | bytes 2359296 | tf_op jit(solution)/shard_map/all_to_all | solution.py:496
  305.3 18.7 %collective-permute-start.40 = (bf16[4,2,96,768]{3,2,1,0:T(8,128)(2,1)}, bf16[4,2,96,768]{3,2,1,0:T(8,128)(2,1)}, u32[]{:S(2)}, u32[]{:S(2)}) collective-permute-start(bf16[4,2,96,768]{3,2,1,0:T(8,128)(2,1)} %get-tuple-element.234), channel_id=1, source_target_pairs={{0,1},{1,0},{2,3},{3,2},{4,5},{5,4},{6,7},{7,6},{8,9},{9,8},{10,11... | collective-permute-start | bytes 3538952 | tf_op jit(solution)/shard_map/ppermute | solution.py:25
  306.4 16.1 %collective-permute-start.39 = (bf16[384,768]{1,0:T(8,128)(2,1)}, bf16[384,768]{1,0:T(8,128)(2,1)}, u32[]{:S(2)}, u32[]{:S(2)}) collective-permute-start(bf16[384,768]{1,0:T(8,128)(2,1)} %pad_maximum_fusion.9), channel_id=1, source_target_pairs={{0,2},{1,3},{2,0},{3,1},{4,6},{5,7},{6,4},{7,5},{8,10},{9,11},{10,... | collective-permute-start | bytes 1769480 | tf_op jit(solution)/shard_map/ppermute | solution.py:25
  307.1 1.2 collective-permute-start.41
  308.3 15.7 %collective-permute-start.42 = (bf16[16,768]{1,0:T(8,128)(2,1)S(1)}, bf16[16,768]{1,0:T(8,128)(2,1)S(1)}, u32[]{:S(2)}, u32[]{:S(2)}) collective-permute-start(bf16[16,768]{1,0:T(8,128)(2,1)S(1)} %add_convert_fusion.5), channel_id=1, source_target_pairs={{0,4},{4,0},{8,12},{12,8},{16,20},{20,16},{24,28},{28,24},{1,5},{5... | collective-permute-start | bytes 73736 | tf_op jit(solution)/shard_map/ppermute | solution.py:25
  327.3 14.9 %collective-permute-start.49 = (bf16[384,768]{1,0:T(8,128)(2,1)}, bf16[384,768]{1,0:T(8,128)(2,1)}, u32[]{:S(2)}, u32[]{:S(2)}) collective-permute-start(bf16[384,768]{1,0:T(8,128)(2,1)} %pad_maximum_fusion.9), channel_id=1, source_target_pairs={{0,1},{1,0},{2,3},{3,2},{4,5},{5,4},{6,7},{7,6},{8,9},{9,8},{10,11... | collective-permute-start | bytes 1769480 | tf_op jit(solution)/shard_map/ppermute | solution.py:25
  327.3 14.9 %collective-permute-start.50 = (bf16[384,768]{1,0:T(8,128)(2,1)}, bf16[384,768]{1,0:T(8,128)(2,1)}, u32[]{:S(2)}, u32[]{:S(2)}) collective-permute-start(bf16[384,768]{1,0:T(8,128)(2,1)} %collective-permute-done.39), channel_id=1, source_target_pairs={{0,1},{1,0},{2,3},{3,2},{4,5},{5,4},{6,7},{7,6},{8,9},{9,8},{10,11... | collective-permute-start | bytes 1769480 | tf_op jit(solution)/shard_map/ppermute | solution.py:25
  333.0 33.6 %all-to-all-start.3 = ((bf16[4,208,768]{2,1,0:T(8,128)(2,1)}), bf16[4,208,768]{2,1,0:T(8,128)(2,1)S(1)}, u32[]{:S(2)}, u32[]{:S(2)}) async-start(bf16[4,208,768]{2,1,0:T(8,128)(2,1)} %pad_maximum_fusion.1), calls=%async_computation.3 | async-start | bytes 2555904 | tf_op jit(solution)/shard_map/all_to_all | solution.py:496
  336.5 13.2 %collective-permute-start.47 = (bf16[8,32,768]{2,1,0:T(8,128)(2,1)}, bf16[8,32,768]{2,1,0:T(8,128)(2,1)}, u32[]{:S(2)}, u32[]{:S(2)}) collective-permute-start(bf16[8,32,768]{2,1,0:T(8,128)(2,1)} %get-tuple-element.257.refs_4_), channel_id=1, source_target_pairs={{0,2},{1,3},{2,0},{3,1},{4,6},{5,7},{6,4},{7,5},{8,10},{9,11},{10,... | collective-permute-start | bytes 1179656 | tf_op jit(solution)/shard_map/ppermute | solution.py:25
  337.2 20.1 %collective-permute-start.48 = (bf16[8,32,768]{2,1,0:T(8,128)(2,1)S(1)}, bf16[8,32,768]{2,1,0:T(8,128)(2,1)}, u32[]{:S(2)}, u32[]{:S(2)}) collective-permute-start(bf16[8,32,768]{2,1,0:T(8,128)(2,1)S(1)} %copy-done.5), channel_id=1, source_target_pairs={{0,2},{1,3},{2,0},{3,1},{4,6},{5,7},{6,4},{7,5},{8,10},{9,11},{10,... | collective-permute-start | bytes 1179656 | tf_op jit(solution)/shard_map/ppermute | solution.py:25
  346.9 14.8 %collective-permute-start.46 = (bf16[192,768]{1,0:T(8,128)(2,1)}, bf16[192,768]{1,0:T(8,128)(2,1)}, u32[]{:S(2)}, u32[]{:S(2)}) collective-permute-start(bf16[192,768]{1,0:T(8,128)(2,1)} %reduce_sum.44), channel_id=1, source_target_pairs={{0,2},{1,3},{2,0},{3,1},{4,6},{5,7},{6,4},{7,5},{8,10},{9,11},{10,... | collective-permute-start | bytes 884744 | tf_op jit(solution)/shard_map/ppermute | solution.py:25
  366.9 4.0 %collective-permute-start.56 = (bf16[192,768]{1,0:T(8,128)(2,1)}, bf16[192,768]{1,0:T(8,128)(2,1)}, u32[]{:S(2)}, u32[]{:S(2)}) collective-permute-start(bf16[192,768]{1,0:T(8,128)(2,1)} %reduce_sum.44), channel_id=1, source_target_pairs={{0,1},{1,0},{2,3},{3,2},{4,5},{5,4},{6,7},{7,6},{8,9},{9,8},{10,11... | collective-permute-start | bytes 884744 | tf_op jit(solution)/shard_map/ppermute | solution.py:25
  367.0 3.9 %collective-permute-start.57 = (bf16[192,768]{1,0:T(8,128)(2,1)}, bf16[192,768]{1,0:T(8,128)(2,1)}, u32[]{:S(2)}, u32[]{:S(2)}) collective-permute-start(bf16[192,768]{1,0:T(8,128)(2,1)} %collective-permute-done.46), channel_id=1, source_target_pairs={{0,1},{1,0},{2,3},{3,2},{4,5},{5,4},{6,7},{7,6},{8,9},{9,8},{10,11... | collective-permute-start | bytes 884744 | tf_op jit(solution)/shard_map/ppermute | solution.py:25
  368.6 5.5 %collective-permute-start.52 = (bf16[2,8,32,768]{3,2,1,0:T(8,128)(2,1)S(1)}, bf16[2,8,32,768]{3,2,1,0:T(8,128)(2,1)S(1)}, u32[]{:S(2)}, u32[]{:S(2)}) collective-permute-start(bf16[2,8,32,768]{3,2,1,0:T(8,128)(2,1)S(1)} %pad_maximum_fusion.8), channel_id=1, source_target_pairs={{0,1},{1,0},{2,3},{3,2},{4,5},{5,4},{6,7},{7,6},{8,9},{9,8},{10,11... | collective-permute-start | bytes 2359304 | tf_op jit(solution)/shard_map/ppermute | solution.py:25
  369.8 4.2 %collective-permute-start.51 = (bf16[2,8,32,768]{3,2,1,0:T(8,128)(2,1)S(1)}, bf16[2,8,32,768]{3,2,1,0:T(8,128)(2,1)S(1)}, u32[]{:S(2)}, u32[]{:S(2)}) collective-permute-start(bf16[2,8,32,768]{3,2,1,0:T(8,128)(2,1)S(1)} %pad_maximum_fusion.7), channel_id=1, source_target_pairs={{0,1},{1,0},{2,3},{3,2},{4,5},{5,4},{6,7},{7,6},{8,9},{9,8},{10,11... | collective-permute-start | bytes 2359304 | tf_op jit(solution)/shard_map/ppermute | solution.py:25
  370.3 9.5 %collective-permute-start.53 = (bf16[208,768]{1,0:T(8,128)(2,1)S(1)}, bf16[208,768]{1,0:T(8,128)(2,1)S(1)}, u32[]{:S(2)}, u32[]{:S(2)}) collective-permute-start(bf16[208,768]{1,0:T(8,128)(2,1)S(1)} %reduce_sum.45), channel_id=1, source_target_pairs={{0,2},{1,3},{2,0},{3,1},{4,6},{5,7},{6,4},{7,5},{8,10},{9,11},{10,... | collective-permute-start | bytes 958472 | tf_op jit(solution)/shard_map/ppermute | solution.py:25
  379.8 2.0 collective-permute-start.54
  379.9 2.0 collective-permute-start.55
  (41 other events, 236.9 us)

commit v2 on v1

--- a/solution.py
+++ b/solution.py
@@ -830,23 +830,20 @@
         60_000_000,
     )
     in_scatter.came, _ = lax.optimization_barrier((in_scatter.came, gx1))
-    out_total = out_scatter.add_fast(*in_scatter.came)
-    out_scatter.send_slow()
+    dense_total = [one.add_fast(*in_scatter.came) for one in (out_scatter, in_scatter)]
+    dense_total = jnp.concatenate(dense_total, axis=1)
+    dense_came = over_slow(dense_total, slow, fast)
     mem_pieces = grad_memory[:1] + [swap(grad_memory[d], "mem", d) for d in range(1, mem)]
     grads = run(
         cross_grads,
-        [(SMEM, where), (VMEM, after(gx2, out_total, *in_scatter.came)), (VMEM, a2), (VMEM, o2), (VMEM, dq2)]
+        [(SMEM, where), (VMEM, after(gx2, dense_total)), (VMEM, a2), (VMEM, o2), (VMEM, dq2)]
         + [(pl.BlockSpec((examples, total, width), lambda j: (0, 0, j)), dkv), (ANY, all_memory)],
         grads_like,
         [square, scratch(width, examples * total), scratch(examples, total, width)],
         max(mem, blocks),
         (2,),
-        45_000_000,
-    )
-    out_final = out_scatter.add_slow()
-    in_scatter.add_fast(out_final)
-    in_scatter.send_slow()
-    cross_scatter = scatter(grads, out_final, *mem_pieces[1:3])
+    )
+    cross_scatter = scatter(grads, *mem_pieces[1:3])
     cross_sum = cross_scatter.add_cores()
     cross_scatter.send_fast()
     gx1 = after(gx1, *cross_sum)
@@ -858,15 +855,13 @@
         [flat((examples, length, width), BF), flat((16, width), BF)] + grads_like,
         [square, own_rows, square, scratch(rows, 3 * width), scratch(*wide)],
         1 + blocks,
-        moved=40_000_000,
     )
     self_scatter = scatter(grads, *mem_pieces[3:4], vectors=vecs_self)
     self_sum = self_scatter.add_cores()
     self_scatter.send_fast()
     cross_scatter.add_fast(*self_sum)
     cross_scatter.send_slow()
-    in_final = in_scatter.add_slow(*self_sum)
-    dense_sum = jnp.concatenate([out_final, in_final])
+    dense_sum = jnp.sum(after(dense_came, *self_sum).astype(F32), axis=0)
     dense_sum = Replicas(dense_sum, 2 * part, across)
     self_total = self_scatter.add_fast(*dense_sum.halves)
     self_scatter.send_slow()

time: 392 us -> 384 us (0.980); the launches traced: 384 us -> 381 us
  Pallas kernels: 105 us -> 117 us
  waiting for transfers between devices: 148 us -> 138 us
    all_to_all x4 -> x3, waiting for transfers between devices: 22.2 us -> 9.74 us  [over_slow(): lax.all_to_all(value, 'fsdp', 0, 0, axis_index_groups=groups, tiled=True)]
    pallas_call x10, Pallas kernels: 105 us -> 117 us  [run(): pl.pallas_call(body, grid=grid, in_specs=[spec for spec, _ in flat_in], o...]
    all_to_all x4 -> x3, starting transfers between devices: 20.3 us -> 17 us  [over_slow(): lax.all_to_all(value, 'fsdp', 0, 0, axis_index_groups=groups, tiled=True)]
  transfers between devices with their start and end apart: 63 -> 62, of which waited for: 25 -> 28; matrix products, arithmetic and copies ran while one was open for 11% -> 10% of each run, Pallas kernels for 27% -> 31%
where the time goes in v2:
time: 384 us; the launch traced here: 381 us
  waiting for transfers between devices  138 us (36%)
  Pallas kernels  117 us (30%)
  starting transfers between devices  76 us (20%)
  other arithmetic  33.9 us (9%)
  local copies, waits for them, and re-layouts  14.7 us (4%)
    ppermute x58, waiting for transfers between devices, swap(): return lax.ppermute(value, axis, [(i, i ^ distance) for i in range(size)])  128 us
    pallas_call x10, Pallas kernels, run(): pl.pallas_call(body, grid=grid, in_specs=[spec for spec, _ in flat_in], o...  117 us
    ppermute x58, starting transfers between devices, swap(): return lax.ppermute(value, axis, [(i, i ^ distance) for i in range(size)])  54.7 us
    all_to_all x3, starting transfers between devices, over_slow(): lax.all_to_all(value, 'fsdp', 0, 0, axis_index_groups=groups, tiled=True)  17 us
    all_to_all x3, waiting for transfers between devices, over_slow(): lax.all_to_all(value, 'fsdp', 0, 0, axis_index_groups=groups, tiled=True)  9.74 us
  transfers between devices with their start and end apart: 62, of which 28 were waited for; matrix products, arithmetic and copies ran while one was open for 10% of the time, Pallas kernels for 31%

profile of v2, /device:TPU:0, one launch (start us, length us, event | category | flops | bytes accessed | tf_op | source)
XLA Modules:
  0.0 380.9 jit_solution(10913014458467793461)
XLA Ops:
  0.8 4.4 %all-to-all-start = ((bf16[4,8,64,768]{3,2,1,0:T(8,128)(2,1)}), bf16[4,8,64,768]{3,2,1,0:T(8,128)(2,1)S(1)}, u32[]{:S(2)}, u32[]{:S(2)}) async-start(bf16[4,8,64,768]{3,2,1,0:T(8,128)(2,1)} %bitcast.76), calls=%async_computation | async-start | bytes 6291456 | tf_op jit(solution)/shard_map/all_to_all | solution.py:694
  6.4 2.6 collective-permute-start
  9.0 2.6 collective-permute-start.1
  11.6 12.0 %collective-permute-done = bf16[208,768]{1,0:T(8,128)(2,1)S(1)} collective-permute-done((bf16[208,768]{1,0:T(8,128)(2,1)S(1)}, bf16[208,768]{1,0:T(8,128)(2,1)S(1)}, u32[]{:S(2)}, u32[]{:S(2)}) %collective-permute-start) | collective-permute-done | bytes 319520 | tf_op jit(solution)/shard_map/ppermute | solution.py:25
  23.5 10.5 %collective-permute-done.1 = bf16[208,768]{1,0:T(8,128)(2,1)S(1)} collective-permute-done((bf16[208,768]{1,0:T(8,128)(2,1)S(1)}, bf16[208,768]{1,0:T(8,128)(2,1)S(1)}, u32[]{:S(2)}, u32[]{:S(2)}) %collective-permute-start.1) | collective-permute-done | bytes 319520 | tf_op jit(solution)/shard_map/ppermute | solution.py:25
  34.0 1.2 pad_maximum_fusion.1.refs_2_.refs_12_
  35.2 1.6 collective-permute-start.3
  37.1 6.7 %collective-permute-start.4 = (bf16[192,768]{1,0:T(8,128)(2,1)S(1)}, bf16[192,768]{1,0:T(8,128)(2,1)S(1)}, u32[]{:S(2)}, u32[]{:S(2)}) collective-permute-start(bf16[192,768]{1,0:T(8,128)(2,1)S(1)} %get-tuple-element.151), channel_id=1, source_target_pairs={{0,8},{4,12},{8,0},{12,4},{16,24},{20,28},{24,16},{28,20},{1,9},{5... | collective-permute-start | bytes 884744 | tf_op jit(solution)/shard_map/ppermute | solution.py:25
  44.9 1.4 collective-permute-start.6
  46.2 8.9 %collective-permute-done.4 = bf16[192,768]{1,0:T(8,128)(2,1)S(1)} collective-permute-done((bf16[192,768]{1,0:T(8,128)(2,1)S(1)}, bf16[192,768]{1,0:T(8,128)(2,1)S(1)}, u32[]{:S(2)}, u32[]{:S(2)}) %collective-permute-start.4) | collective-permute-done | bytes 294944 | tf_op jit(solution)/shard_map/ppermute | solution.py:25
  55.2 12.1 %collective-permute-done.5 = bf16[192,768]{1,0:T(8,128)(2,1)S(1)} collective-permute-done((bf16[192,768]{1,0:T(8,128)(2,1)S(1)}, bf16[192,768]{1,0:T(8,128)(2,1)S(1)}, u32[]{:S(2)}, u32[]{:S(2)}) %collective-permute-start.5) | collective-permute-done | bytes 294944 | tf_op jit(solution)/shard_map/ppermute | solution.py:25
  68.8 3.3 pad_maximum_fusion.3.refs_5_.refs_7_
  73.0 4.3 %collective-permute-start.10 = (bf16[192,768]{1,0:T(8,128)(2,1)S(1)}, bf16[192,768]{1,0:T(8,128)(2,1)}, u32[]{:S(2)}, u32[]{:S(2)}) collective-permute-start(bf16[192,768]{1,0:T(8,128)(2,1)S(1)} %get-tuple-element.160), channel_id=1, source_target_pairs={{0,8},{4,12},{8,0},{12,4},{16,24},{20,28},{24,16},{28,20},{1,9},{5... | collective-permute-start | bytes 884744 | tf_op jit(solution)/shard_map/ppermute | solution.py:25
  78.3 1.5 collective-permute-start.12
  80.3 7.7 %shard_map.373 = (f32[256,768]{1,0:T(8,128)}, bf16[256,768]{1,0:T(8,128)(2,1)}, bf16[256,2304]{1,0:T(8,128)(2,1)}, bf16[6,512,128]{2,1,0:T(8,128)(2,1)}, bf16[256,768]{1,0:T(8,128)(2,1)}, /*index=5*/f32[16,768]{1,0:T(8,128)}) custom-call(s32[4]{0:T(128)} %pad_add_fusion.1.refs_0_, bf16[32,32,768]{2,1,0:T(8,128)(2,1)} %refs_1_.5, ...), custom_call_target="tpu_custom_call" | custom-call | tf_op jit(solution)/shard_map/pallas_call | solution.py:475
  89.1 11.7 %collective-permute-done.11 = bf16[192,768]{1,0:T(8,128)(2,1)} collective-permute-done((bf16[192,768]{1,0:T(8,128)(2,1)S(1)}, bf16[192,768]{1,0:T(8,128)(2,1)}, u32[]{:S(2)}, u32[]{:S(2)}) %collective-permute-start.11) | collective-permute-done | bytes 294944 | tf_op jit(solution)/shard_map/ppermute | solution.py:25
  100.9 1.4 pad_maximum_fusion.4.refs_5_
  103.1 5.0 %collective-permute-start.16 = (bf16[192,768]{1,0:T(8,128)(2,1)S(1)}, bf16[192,768]{1,0:T(8,128)(2,1)S(1)}, u32[]{:S(2)}, u32[]{:S(2)}) collective-permute-start(bf16[192,768]{1,0:T(8,128)(2,1)S(1)} %slice_select_fusion), channel_id=1, source_target_pairs={{0,8},{4,12},{8,0},{12,4},{16,24},{20,28},{24,16},{28,20},{1,9},{5... | collective-permute-start | bytes 884744 | tf_op jit(solution)/shard_map/ppermute | solution.py:25
  109.2 1.4 collective-permute-start.18
  111.6 15.2 %shard_map.374 = (f32[256,768]{1,0:T(8,128)}, bf16[256,768]{1,0:T(8,128)(2,1)}, bf16[256,768]{1,0:T(8,128)(2,1)}, bf16[8,256,1536]{2,1,0:T(8,128)(2,1)}, bf16[8,...) custom-call(s32[4]{0:T(128)} %pad_add_fusion.1.refs_0_, s32[32]{0:T(128)} %refs_1_.4, ...), custom_call_target="tpu_custom_call" | custom-call | tf_op jit(solution)/shard_map/pallas_call | solution.py:475
  126.8 4.7 %collective-permute-done.17 = bf16[192,768]{1,0:T(8,128)(2,1)S(1)} collective-permute-done((bf16[192,768]{1,0:T(8,128)(2,1)S(1)}, bf16[192,768]{1,0:T(8,128)(2,1)S(1)}, u32[]{:S(2)}, u32[]{:S(2)}) %collective-permute-start.17) | collective-permute-done | bytes 294944 | tf_op jit(solution)/shard_map/ppermute | solution.py:25
  131.6 1.3 pad_maximum_fusion.5.refs_7_
  132.9 1.2 collective-permute-start.21
  139.9 13.7 %shard_map.375 = (bf16[256,768]{1,0:T(8,128)(2,1)}, bf16[256,3072]{1,0:T(8,128)(2,1)}, bf16[256,3072]{1,0:T(8,128)(2,1)}, bf16[4,2,96,768]{3,2,1,0:T(8,128)(2,1)...) custom-call(s32[4]{0:T(128)} %pad_add_fusion.1.refs_0_, ...), custom_call_target="tpu_custom_call" | custom-call | tf_op jit(solution)/shard_map/pallas_call | solution.py:475
  153.6 7.9 %collective-permute-done.21.refs_8_ = bf16[4,192,768]{2,1,0:T(8,128)(2,1)} collective-permute-done((bf16[4,192,768]{2,1,0:T(8,128)(2,1)}, bf16[4,192,768]{2,1,0:T(8,128)(2,1)}, u32[]{:S(2)}, u32[]{:S(2)}) %collective-permute-start.21) | collective-permute-done | bytes 1179680 | tf_op jit(solution)/shard_map/ppermute | solution.py:25
  164.6 1.5 fusion.3
  166.1 1.3 collective-permute-start.26
  168.9 11.7 %shard_map.376 = (bf16[8,32,768]{2,1,0:T(8,128)(2,1)}, bf16[256,3072]{1,0:T(8,128)(2,1)}, f32[1,768]{1,0:T(1,128)}, f32[1,3072]{1,0:T(1,128)}, bf16[4,2,96,768]{...) custom-call(s32[4]{0:T(128)} %pad_add_fusion.1.refs_0_, ...), custom_call_target="tpu_custom_call" | custom-call | tf_op jit(solution)/shard_map/pallas_call | solution.py:475
  180.6 19.1 %shard_map.377 = (f32[256,768]{1,0:T(8,128)}, f32[2,768]{1,0:T(2,128)}) custom-call(s32[4]{0:T(128)} %pad_add_fusion.1.refs_0_, f32[256,768]{1,0:T(8,128)} %get-tuple-element.177.refs_1_, f32[16,768]{1,0:T(8,128)} %get-tuple-element.150.refs_3_.refs_2_, bf16[256,3072]{1,0:T(8,128)(2,1)} %get-tuple-element.181.refs_3_, bf16[32,32,768]{2,1,0:T(8,128)(2,1)} %refs_4_.3, ...), custom_call_target="tpu_custom_call" | custom-call | tf_op jit(solution)/shard_map/pallas_call | solution.py:475
  200.3 1.5 collective-permute-done.27
  203.0 1.3 collective-permute-start.29
  204.8 17.8 %shard_map.378 = (f32[256,768]{1,0:T(8,128)}, f32[2,768]{1,0:T(2,128)}, bf16[8,256,1536]{2,1,0:T(8,128)(2,1)}, bf16[256,768]{1,0:T(8,128)(2,1)}, bf16[8,64,768]{...) custom-call(s32[4]{0:T(128)} %pad_add_fusion.1.refs_0_, ...), custom_call_target="tpu_custom_call" | custom-call | bytes 60000000 | tf_op jit(solution)/shard_map/pallas_call | solution.py:475
  222.6 8.5 %collective-permute-done.29 = bf16[4,2,96,768]{3,2,1,0:T(8,128)(2,1)S(1)} collective-permute-done((bf16[4,2,96,768]{3,2,1,0:T(8,128)(2,1)S(1)}, bf16[4,2,96,768]{3,2,1,0:T(8,128)(2,1)S(1)}, u32[]{:S(2)}, u32[]{:S(2)}) %collective-permute-start.29) | collective-permute-done | bytes 1179680 | tf_op jit(solution)/shard_map/ppermute | solution.py:25
  232.8 1.6 pad_maximum_fusion
  234.4 8.1 %all-to-all-start.1 = ((bf16[4,384,768]{2,1,0:T(8,128)(2,1)}), bf16[4,384,768]{2,1,0:T(8,128)(2,1)S(1)}, u32[]{:S(2)}, u32[]{:S(2)}) async-start(bf16[4,384,768]{2,1,0:T(8,128)(2,1)} %pad_maximum_fusion), calls=%async_computation.1 | async-start | bytes 4718592 | tf_op jit(solution)/shard_map/all_to_all | solution.py:496
  242.5 1.4 collective-permute-start.33
  243.9 13.2 %shard_map.379 = (bf16[4,2,96,768]{3,2,1,0:T(8,128)(2,1)}, bf16[1,4,2,96,768]{4,3,2,1,0:T(8,128)(2,1)}, bf16[4,2,96,768]{3,2,1,0:T(8,128)(2,1)}, bf16[2,2,96,768]{3,2,1,0:T(8,128)(2,1)}, bf16[2,2,96,768]{3,2,1,0:T(8,128)(2,1)}) custom-call(s32[4]{0:T(128)} %pad_add_fusion.1.refs_0_, f32[256,768]{1,0:T(8,128)} %get-tuple-element.203.refs_3_.refs_1_, ...), custom_call_target="tpu_custom_call" | custom-call | tf_op jit(solution)/shard_map/pallas_call | solution.py:475
  257.1 5.5 %collective-permute-done.33.refs_3_ = bf16[8,64,768]{2,1,0:T(8,128)(2,1)S(1)} collective-permute-done((bf16[8,64,768]{2,1,0:T(8,128)(2,1)}, bf16[8,64,768]{2,1,0:T(8,128)(2,1)S(1)}, u32[]{:S(2)}, u32[]{:S(2)}) %collective-permute-start.33) | collective-permute-done | bytes 786464 | tf_op jit(solution)/shard_map/ppermute | solution.py:25
  265.7 1.5 fusion.1
  267.3 1.3 collective-permute-start.45
  268.6 11.7 %shard_map.380 = (bf16[8,32,768]{2,1,0:T(8,128)(2,1)}, bf16[16,768]{1,0:T(8,128)(2,1)}, bf16[4,2,96,768]{3,2,1,0:T(8,128)(2,1)}, bf16[1,4,2,96,768]{4,3,2,1,0:T(...) custom-call(s32[4]{0:T(128)} %pad_add_fusion.1.refs_0_, ...), custom_call_target="tpu_custom_call" | custom-call | tf_op jit(solution)/shard_map/pallas_call | solution.py:475
  280.3 2.5 collective-permute-done.36.refs_4_
  283.3 1.7 collective-permute-done.37
  285.9 2.7 fusion
  288.6 1.2 collective-permute-start.43
  289.8 6.3 %collective-permute-done.45 = bf16[4,2,96,768]{3,2,1,0:T(8,128)(2,1)S(1)} collective-permute-done((bf16[4,2,96,768]{3,2,1,0:T(8,128)(2,1)S(1)}, bf16[4,2,96,768]{3,2,1,0:T(8,128)(2,1)S(1)}, u32[]{:S(2)}, u32[]{:S(2)}) %collective-permute-start.45) | collective-permute-done | bytes 1179680 | tf_op jit(solution)/shard_map/ppermute | solution.py:25
  296.1 1.5 add_convert_fusion
  297.6 5.3 %all-to-all-start.3 = ((bf16[4,192,768]{2,1,0:T(8,128)(2,1)}), bf16[4,192,768]{2,1,0:T(8,128)(2,1)S(1)}, u32[]{:S(2)}, u32[]{:S(2)}) async-start(bf16[4,192,768]{2,1,0:T(8,128)(2,1)} %bitcast.73), calls=%async_computation.3 | async-start | bytes 2359296 | tf_op jit(solution)/shard_map/all_to_all | solution.py:496
  303.0 1.3 reduce_sum.36
  304.3 1.4 collective-permute-start.39
  307.9 1.3 collective-permute-start.42
  309.2 12.0 %collective-permute-done.42 = bf16[16,768]{1,0:T(8,128)(2,1)S(1)} collective-permute-done((bf16[16,768]{1,0:T(8,128)(2,1)S(1)}, bf16[16,768]{1,0:T(8,128)(2,1)S(1)}, u32[]{:S(2)}, u32[]{:S(2)}) %collective-permute-start.42) | collective-permute-done | bytes 24608 | tf_op jit(solution)/shard_map/ppermute | solution.py:25
  321.2 2.4 add_convert_fusion.1
  325.4 4.7 %all-to-all-done.3 = bf16[4,192,768]{2,1,0:T(8,128)(2,1)S(1)} async-done(((bf16[4,192,768]{2,1,0:T(8,128)(2,1)}), bf16[4,192,768]{2,1,0:T(8,128)(2,1)S(1)}, u32[]{:S(2)}, u32[]{:S(2)}) %all-to-all-start.3) | async-done | bytes 1179680 | tf_op jit(solution)/shard_map/all_to_all | solution.py:496
  330.1 3.5 all-to-all-start.2
  333.7 1.5 collective-permute-start.47
  336.1 1.4 collective-permute-start.48
  337.5 3.5 shard_map.381
  341.1 1.8 fusion.5
  345.2 7.1 %collective-permute-done.46 = bf16[192,768]{1,0:T(8,128)(2,1)S(1)} collective-permute-done((bf16[192,768]{1,0:T(8,128)(2,1)S(1)}, bf16[192,768]{1,0:T(8,128)(2,1)S(1)}, u32[]{:S(2)}, u32[]{:S(2)}) %collective-permute-start.46) | collective-permute-done | bytes 294944 | tf_op jit(solution)/shard_map/ppermute | solution.py:25
  352.3 6.4 %collective-permute-done.48.refs_2_ = bf16[8,32,768]{2,1,0:T(8,128)(2,1)S(1)} collective-permute-done((bf16[8,32,768]{2,1,0:T(8,128)(2,1)}, bf16[8,32,768]{2,1,0:T(8,128)(2,1)S(1)}, u32[]{:S(2)}, u32[]{:S(2)}) %collective-permute-start.48) | collective-permute-done | bytes 393248 | tf_op jit(solution)/shard_map/ppermute | solution.py:25
  358.8 5.0 %all-to-all-done.2 = bf16[4,208,768]{2,1,0:T(8,128)(2,1)S(1)} async-done(((bf16[4,208,768]{2,1,0:T(8,128)(2,1)}), bf16[4,208,768]{2,1,0:T(8,128)(2,1)S(1)}, u32[]{:S(2)}, u32[]{:S(2)}) %all-to-all-start.2) | async-done | bytes 1277984 | tf_op jit(solution)/shard_map/all_to_all | solution.py:496
  367.3 1.4 collective-permute-start.53
  372.4 3.4 shard_map.382
  (220 shorter events, 48.8 us)
Async XLA Ops:
  0.8 67.9 %all-to-all-start = ((bf16[4,8,64,768]{3,2,1,0:T(8,128)(2,1)}), bf16[4,8,64,768]{3,2,1,0:T(8,128)(2,1)S(1)}, u32[]{:S(2)}, u32[]{:S(2)}) async-start(bf16[4,8,64,768]{3,2,1,0:T(8,128)(2,1)} %bitcast.76), calls=%async_computation | async-start | bytes 6291456 | tf_op jit(solution)/shard_map/all_to_all | solution.py:694
  6.4 17.2 %collective-permute-start = (bf16[208,768]{1,0:T(8,128)(2,1)S(1)}, bf16[208,768]{1,0:T(8,128)(2,1)S(1)}, u32[]{:S(2)}, u32[]{:S(2)}) collective-permute-start(bf16[208,768]{1,0:T(8,128)(2,1)S(1)} %pad_maximum_fusion.10), channel_id=1, source_target_pairs={{0,8},{4,12},{8,0},{12,4},{16,24},{20,28},{24,16},{28,20},{1,9},{5... | collective-permute-start | bytes 958472 | tf_op jit(solution)/shard_map/ppermute | solution.py:25
  9.0 25.0 %collective-permute-start.1 = (bf16[208,768]{1,0:T(8,128)(2,1)S(1)}, bf16[208,768]{1,0:T(8,128)(2,1)S(1)}, u32[]{:S(2)}, u32[]{:S(2)}) collective-permute-start(bf16[208,768]{1,0:T(8,128)(2,1)S(1)} %pad_maximum_fusion.10), channel_id=1, source_target_pairs={{0,16},{4,20},{8,24},{12,28},{16,0},{20,4},{24,8},{28,12},{1,17},{... | collective-permute-start | bytes 958472 | tf_op jit(solution)/shard_map/ppermute | solution.py:25
  11.6 22.4 %collective-permute-start.2 = (bf16[208,768]{1,0:T(8,128)(2,1)S(1)}, bf16[208,768]{1,0:T(8,128)(2,1)S(1)}, u32[]{:S(2)}, u32[]{:S(2)}) collective-permute-start(bf16[208,768]{1,0:T(8,128)(2,1)S(1)} %pad_maximum_fusion.10), channel_id=1, source_target_pairs={{0,24},{4,28},{8,16},{12,20},{16,8},{20,12},{24,0},{28,4},{1,25},{... | collective-permute-start | bytes 958472 | tf_op jit(solution)/shard_map/ppermute | solution.py:25
  35.2 33.4 %collective-permute-start.3 = (bf16[4,208,768]{2,1,0:T(8,128)(2,1)}, bf16[4,208,768]{2,1,0:T(8,128)(2,1)}, u32[]{:S(2)}, u32[]{:S(2)}) collective-permute-start(bf16[4,208,768]{2,1,0:T(8,128)(2,1)} %pad_maximum_fusion.1.refs_2_.refs_12_), channel_id=1, source_target_pairs={{0,4},{4,0},{8,12},{12,8},{16,20},{20,16},{24,28},{28,24},{1,5},{5... | collective-permute-start | bytes 3833864 | tf_op jit(solution)/shard_map/ppermute | solution.py:25
  37.1 30.2 %copy-start.12 = (bf16[192,768]{1,0:T(8,128)(2,1)}, bf16[192,768]{1,0:T(8,128)(2,1)S(1)}, u32[]{:S(2)}) copy-start(bf16[192,768]{1,0:T(8,128)(2,1)S(1)} %get-tuple-element.151) | copy-start | bytes 884740
  37.1 18.1 %collective-permute-start.4 = (bf16[192,768]{1,0:T(8,128)(2,1)S(1)}, bf16[192,768]{1,0:T(8,128)(2,1)S(1)}, u32[]{:S(2)}, u32[]{:S(2)}) collective-permute-start(bf16[192,768]{1,0:T(8,128)(2,1)S(1)} %get-tuple-element.151), channel_id=1, source_target_pairs={{0,8},{4,12},{8,0},{12,4},{16,24},{20,28},{24,16},{28,20},{1,9},{5... | collective-permute-start | bytes 884744 | tf_op jit(solution)/shard_map/ppermute | solution.py:25
  43.8 23.5 %collective-permute-start.5 = (bf16[192,768]{1,0:T(8,128)(2,1)S(1)}, bf16[192,768]{1,0:T(8,128)(2,1)S(1)}, u32[]{:S(2)}, u32[]{:S(2)}) collective-permute-start(bf16[192,768]{1,0:T(8,128)(2,1)S(1)} %get-tuple-element.151), channel_id=1, source_target_pairs={{0,16},{4,20},{8,24},{12,28},{16,0},{20,4},{24,8},{28,12},{1,17},{... | collective-permute-start | bytes 884744 | tf_op jit(solution)/shard_map/ppermute | solution.py:25
  44.9 22.4 %collective-permute-start.6 = (bf16[192,768]{1,0:T(8,128)(2,1)S(1)}, bf16[192,768]{1,0:T(8,128)(2,1)S(1)}, u32[]{:S(2)}, u32[]{:S(2)}) collective-permute-start(bf16[192,768]{1,0:T(8,128)(2,1)S(1)} %get-tuple-element.151), channel_id=1, source_target_pairs={{0,24},{4,28},{8,16},{12,20},{16,8},{20,12},{24,0},{28,4},{1,25},{... | collective-permute-start | bytes 884744 | tf_op jit(solution)/shard_map/ppermute | solution.py:25
  46.2 32.0 %collective-permute-start.7 = (bf16[4,208,768]{2,1,0:T(8,128)(2,1)}, bf16[4,208,768]{2,1,0:T(8,128)(2,1)}, u32[]{:S(2)}, u32[]{:S(2)}) collective-permute-start(bf16[4,208,768]{2,1,0:T(8,128)(2,1)} %pad_maximum_fusion.1.refs_2_.refs_12_), channel_id=1, source_target_pairs={{0,1},{1,0},{2,3},{3,2},{4,5},{5,4},{6,7},{7,6},{8,9},{9,8},{10,11... | collective-permute-start | bytes 3833864 | tf_op jit(solution)/shard_map/ppermute | solution.py:25
  68.7 11.1 %collective-permute-start.8 = (bf16[4,208,768]{2,1,0:T(8,128)(2,1)}, bf16[4,208,768]{2,1,0:T(8,128)(2,1)}, u32[]{:S(2)}, u32[]{:S(2)}) collective-permute-start(bf16[4,208,768]{2,1,0:T(8,128)(2,1)} %collective-permute-done.3.refs_3_.refs_13_), channel_id=1, source_target_pairs={{0,1},{1,0},{2,3},{3,2},{4,5},{5,4},{6,7},{7,6},{8,9},{9,8},{10,11... | collective-permute-start | bytes 3833864 | tf_op jit(solution)/shard_map/ppermute | solution.py:25
  72.1 28.8 %collective-permute-start.9 = (bf16[4,192,768]{2,1,0:T(8,128)(2,1)}, bf16[4,192,768]{2,1,0:T(8,128)(2,1)}, u32[]{:S(2)}, u32[]{:S(2)}) collective-permute-start(bf16[4,192,768]{2,1,0:T(8,128)(2,1)} %pad_maximum_fusion.3.refs_5_.refs_7_), channel_id=1, source_target_pairs={{0,4},{4,0},{8,12},{12,8},{16,20},{20,16},{24,28},{28,24},{1,5},{5... | collective-permute-start | bytes 3538952 | tf_op jit(solution)/shard_map/ppermute | solution.py:25
  73.0 16.1 %collective-permute-start.10 = (bf16[192,768]{1,0:T(8,128)(2,1)S(1)}, bf16[192,768]{1,0:T(8,128)(2,1)}, u32[]{:S(2)}, u32[]{:S(2)}) collective-permute-start(bf16[192,768]{1,0:T(8,128)(2,1)S(1)} %get-tuple-element.160), channel_id=1, source_target_pairs={{0,8},{4,12},{8,0},{12,4},{16,24},{20,28},{24,16},{28,20},{1,9},{5... | collective-permute-start | bytes 884744 | tf_op jit(solution)/shard_map/ppermute | solution.py:25
  77.3 23.6 %collective-permute-start.11 = (bf16[192,768]{1,0:T(8,128)(2,1)S(1)}, bf16[192,768]{1,0:T(8,128)(2,1)}, u32[]{:S(2)}, u32[]{:S(2)}) collective-permute-start(bf16[192,768]{1,0:T(8,128)(2,1)S(1)} %get-tuple-element.160), channel_id=1, source_target_pairs={{0,16},{4,20},{8,24},{12,28},{16,0},{20,4},{24,8},{28,12},{1,17},{... | collective-permute-start | bytes 884744 | tf_op jit(solution)/shard_map/ppermute | solution.py:25
  78.3 22.6 %collective-permute-start.12 = (bf16[192,768]{1,0:T(8,128)(2,1)S(1)}, bf16[192,768]{1,0:T(8,128)(2,1)}, u32[]{:S(2)}, u32[]{:S(2)}) collective-permute-start(bf16[192,768]{1,0:T(8,128)(2,1)S(1)} %get-tuple-element.160), channel_id=1, source_target_pairs={{0,24},{4,28},{8,16},{12,20},{16,8},{20,12},{24,0},{28,4},{1,25},{... | collective-permute-start | bytes 884744 | tf_op jit(solution)/shard_map/ppermute | solution.py:25
  79.8 29.5 %collective-permute-start.13 = (bf16[4,192,768]{2,1,0:T(8,128)(2,1)}, bf16[4,192,768]{2,1,0:T(8,128)(2,1)}, u32[]{:S(2)}, u32[]{:S(2)}) collective-permute-start(bf16[4,192,768]{2,1,0:T(8,128)(2,1)} %pad_maximum_fusion.3.refs_5_.refs_7_), channel_id=1, source_target_pairs={{0,1},{1,0},{2,3},{3,2},{4,5},{5,4},{6,7},{7,6},{8,9},{9,8},{10,11... | collective-permute-start | bytes 3538952 | tf_op jit(solution)/shard_map/ppermute | solution.py:25
  100.9 9.7 %collective-permute-start.14 = (bf16[4,192,768]{2,1,0:T(8,128)(2,1)}, bf16[4,192,768]{2,1,0:T(8,128)(2,1)S(1)}, u32[]{:S(2)}, u32[]{:S(2)}) collective-permute-start(bf16[4,192,768]{2,1,0:T(8,128)(2,1)} %collective-permute-done.9.refs_6_.refs_8_), channel_id=1, source_target_pairs={{0,1},{1,0},{2,3},{3,2},{4,5},{5,4},{6,7},{7,6},{8,9},{9,8},{10,11... | collective-permute-start | bytes 3538952 | tf_op jit(solution)/shard_map/ppermute | solution.py:25
  102.3 29.3 %collective-permute-start.15 = (bf16[4,192,768]{2,1,0:T(8,128)(2,1)S(1)}, bf16[4,192,768]{2,1,0:T(8,128)(2,1)S(1)}, u32[]{:S(2)}, u32[]{:S(2)}) collective-permute-start(bf16[4,192,768]{2,1,0:T(8,128)(2,1)S(1)} %pad_maximum_fusion.4.refs_5_), channel_id=1, source_target_pairs={{0,4},{4,0},{8,12},{12,8},{16,20},{20,16},{24,28},{28,24},{1,5},{5... | collective-permute-start | bytes 3538952 | tf_op jit(solution)/shard_map/ppermute | solution.py:25
  103.1 23.7 %collective-permute-start.16 = (bf16[192,768]{1,0:T(8,128)(2,1)S(1)}, bf16[192,768]{1,0:T(8,128)(2,1)S(1)}, u32[]{:S(2)}, u32[]{:S(2)}) collective-permute-start(bf16[192,768]{1,0:T(8,128)(2,1)S(1)} %slice_select_fusion), channel_id=1, source_target_pairs={{0,8},{4,12},{8,0},{12,4},{16,24},{20,28},{24,16},{28,20},{1,9},{5... | collective-permute-start | bytes 884744 | tf_op jit(solution)/shard_map/ppermute | solution.py:25
  108.1 23.4 %collective-permute-start.17 = (bf16[192,768]{1,0:T(8,128)(2,1)S(1)}, bf16[192,768]{1,0:T(8,128)(2,1)S(1)}, u32[]{:S(2)}, u32[]{:S(2)}) collective-permute-start(bf16[192,768]{1,0:T(8,128)(2,1)S(1)} %slice_select_fusion), channel_id=1, source_target_pairs={{0,16},{4,20},{8,24},{12,28},{16,0},{20,4},{24,8},{28,12},{1,17},{... | collective-permute-start | bytes 884744 | tf_op jit(solution)/shard_map/ppermute | solution.py:25
  109.2 22.3 %collective-permute-start.18 = (bf16[192,768]{1,0:T(8,128)(2,1)S(1)}, bf16[192,768]{1,0:T(8,128)(2,1)S(1)}, u32[]{:S(2)}, u32[]{:S(2)}) collective-permute-start(bf16[192,768]{1,0:T(8,128)(2,1)S(1)} %slice_select_fusion), channel_id=1, source_target_pairs={{0,24},{4,28},{8,16},{12,20},{16,8},{20,12},{24,0},{28,4},{1,25},{... | collective-permute-start | bytes 884744 | tf_op jit(solution)/shard_map/ppermute | solution.py:25
  110.6 28.2 %collective-permute-start.19 = (bf16[4,192,768]{2,1,0:T(8,128)(2,1)S(1)}, bf16[4,192,768]{2,1,0:T(8,128)(2,1)}, u32[]{:S(2)}, u32[]{:S(2)}) collective-permute-start(bf16[4,192,768]{2,1,0:T(8,128)(2,1)S(1)} %pad_maximum_fusion.4.refs_5_), channel_id=1, source_target_pairs={{0,1},{1,0},{2,3},{3,2},{4,5},{5,4},{6,7},{7,6},{8,9},{9,8},{10,11... | collective-permute-start | bytes 3538952 | tf_op jit(solution)/shard_map/ppermute | solution.py:25
  131.6 7.3 %collective-permute-start.20 = (bf16[4,192,768]{2,1,0:T(8,128)(2,1)S(1)}, bf16[4,192,768]{2,1,0:T(8,128)(2,1)S(1)}, u32[]{:S(2)}, u32[]{:S(2)}) collective-permute-start(bf16[4,192,768]{2,1,0:T(8,128)(2,1)S(1)} %collective-permute-done.15.refs_6_), channel_id=1, source_target_pairs={{0,1},{1,0},{2,3},{3,2},{4,5},{5,4},{6,7},{7,6},{8,9},{9,8},{10,11... | collective-permute-start | bytes 3538952 | tf_op jit(solution)/shard_map/ppermute | solution.py:25
  132.9 28.5 %collective-permute-start.21 = (bf16[4,192,768]{2,1,0:T(8,128)(2,1)}, bf16[4,192,768]{2,1,0:T(8,128)(2,1)}, u32[]{:S(2)}, u32[]{:S(2)}) collective-permute-start(bf16[4,192,768]{2,1,0:T(8,128)(2,1)} %pad_maximum_fusion.5.refs_7_), channel_id=1, source_target_pairs={{0,4},{4,0},{8,12},{12,8},{16,20},{20,16},{24,28},{28,24},{1,5},{5... | collective-permute-start | bytes 3538952 | tf_op jit(solution)/shard_map/ppermute | solution.py:25
  161.5 2.2 collective-permute-start.22
  161.5 3.1 collective-permute-start.23
  162.0 5.4 %collective-permute-start.24 = (bf16[4,192,768]{2,1,0:T(8,128)(2,1)}, bf16[4,192,768]{2,1,0:T(8,128)(2,1)S(1)}, u32[]{:S(2)}, u32[]{:S(2)}) collective-permute-start(bf16[4,192,768]{2,1,0:T(8,128)(2,1)} %pad_maximum_fusion.5.refs_7_), channel_id=1, source_target_pairs={{0,1},{1,0},{2,3},{3,2},{4,5},{5,4},{6,7},{7,6},{8,9},{9,8},{10,11... | collective-permute-start | bytes 3538952 | tf_op jit(solution)/shard_map/ppermute | solution.py:25
  162.0 5.9 %collective-permute-start.25 = (bf16[4,192,768]{2,1,0:T(8,128)(2,1)}, bf16[4,192,768]{2,1,0:T(8,128)(2,1)S(1)}, u32[]{:S(2)}, u32[]{:S(2)}) collective-permute-start(bf16[4,192,768]{2,1,0:T(8,128)(2,1)} %collective-permute-done.21.refs_8_), channel_id=1, source_target_pairs={{0,1},{1,0},{2,3},{3,2},{4,5},{5,4},{6,7},{7,6},{8,9},{9,8},{10,11... | collective-permute-start | bytes 3538952 | tf_op jit(solution)/shard_map/ppermute | solution.py:25
  166.1 34.2 %collective-permute-start.26 = (bf16[4,2,96,768]{3,2,1,0:T(8,128)(2,1)S(1)}, bf16[4,2,96,768]{3,2,1,0:T(8,128)(2,1)S(1)}, u32[]{:S(2)}, u32[]{:S(2)}) collective-permute-start(bf16[4,2,96,768]{3,2,1,0:T(8,128)(2,1)S(1)} %fusion.3), channel_id=1, source_target_pairs={{0,4},{4,0},{8,12},{12,8},{16,20},{20,16},{24,28},{28,24},{1,5},{5... | collective-permute-start | bytes 3538952 | tf_op jit(solution)/shard_map/ppermute | solution.py:25
  199.7 2.1 collective-permute-start.27
  200.0 2.7 collective-permute-start.28
  203.0 28.1 %collective-permute-start.29 = (bf16[4,2,96,768]{3,2,1,0:T(8,128)(2,1)S(1)}, bf16[4,2,96,768]{3,2,1,0:T(8,128)(2,1)S(1)}, u32[]{:S(2)}, u32[]{:S(2)}) collective-permute-start(bf16[4,2,96,768]{3,2,1,0:T(8,128)(2,1)S(1)} %fusion.2), channel_id=1, source_target_pairs={{0,4},{4,0},{8,12},{12,8},{16,20},{20,16},{24,28},{28,24},{1,5},{5... | collective-permute-start | bytes 3538952 | tf_op jit(solution)/shard_map/ppermute | solution.py:25
  204.3 26.8 %collective-permute-start.30 = (bf16[4,2,96,768]{3,2,1,0:T(8,128)(2,1)S(1)}, bf16[4,2,96,768]{3,2,1,0:T(8,128)(2,1)S(1)}, u32[]{:S(2)}, u32[]{:S(2)}) collective-permute-start(bf16[4,2,96,768]{3,2,1,0:T(8,128)(2,1)S(1)} %copy-done.41), channel_id=1, source_target_pairs={{0,1},{1,0},{2,3},{3,2},{4,5},{5,4},{6,7},{7,6},{8,9},{9,8},{10,11... | collective-permute-start | bytes 3538952 | tf_op jit(solution)/shard_map/ppermute | solution.py:25
  204.3 27.2 %collective-permute-start.31 = (bf16[4,2,96,768]{3,2,1,0:T(8,128)(2,1)}, bf16[4,2,96,768]{3,2,1,0:T(8,128)(2,1)S(1)}, u32[]{:S(2)}, u32[]{:S(2)}) collective-permute-start(bf16[4,2,96,768]{3,2,1,0:T(8,128)(2,1)} %get-tuple-element.202), channel_id=1, source_target_pairs={{0,1},{1,0},{2,3},{3,2},{4,5},{5,4},{6,7},{7,6},{8,9},{9,8},{10,11... | collective-permute-start | bytes 3538952 | tf_op jit(solution)/shard_map/ppermute | solution.py:25
  204.8 26.3 %copy-start.13 = (bf16[4,2,96,768]{3,2,1,0:T(8,128)(2,1)S(1)}, bf16[4,2,96,768]{3,2,1,0:T(8,128)(2,1)}, u32[]{:S(2)}) copy-start(bf16[4,2,96,768]{3,2,1,0:T(8,128)(2,1)} %get-tuple-element.196) | copy-start | bytes 3538948
  234.4 63.2 %all-to-all-start.1 = ((bf16[4,384,768]{2,1,0:T(8,128)(2,1)}), bf16[4,384,768]{2,1,0:T(8,128)(2,1)S(1)}, u32[]{:S(2)}, u32[]{:S(2)}) async-start(bf16[4,384,768]{2,1,0:T(8,128)(2,1)} %pad_maximum_fusion), calls=%async_computation.1 | async-start | bytes 4718592 | tf_op jit(solution)/shard_map/all_to_all | solution.py:496
  242.5 14.6 %collective-permute-start.32 = (bf16[8,64,768]{2,1,0:T(8,128)(2,1)}, bf16[8,64,768]{2,1,0:T(8,128)(2,1)S(1)}, u32[]{:S(2)}, u32[]{:S(2)}) collective-permute-start(bf16[8,64,768]{2,1,0:T(8,128)(2,1)} %get-tuple-element.210), channel_id=1, source_target_pairs={{0,1},{1,0},{2,3},{3,2},{4,5},{5,4},{6,7},{7,6},{8,9},{9,8},{10,11... | collective-permute-start | bytes 2359304 | tf_op jit(solution)/shard_map/ppermute | solution.py:25
  242.5 20.2 %collective-permute-start.33 = (bf16[8,64,768]{2,1,0:T(8,128)(2,1)}, bf16[8,64,768]{2,1,0:T(8,128)(2,1)S(1)}, u32[]{:S(2)}, u32[]{:S(2)}) collective-permute-start(bf16[8,64,768]{2,1,0:T(8,128)(2,1)} %get-tuple-element.211), channel_id=1, source_target_pairs={{0,2},{1,3},{2,0},{3,1},{4,6},{5,7},{6,4},{7,5},{8,10},{9,11},{10,... | collective-permute-start | bytes 2359304 | tf_op jit(solution)/shard_map/ppermute | solution.py:25
  262.6 2.2 collective-permute-start.34
  262.7 3.1 collective-permute-start.35
  263.2 19.7 %collective-permute-start.36 = (bf16[8,64,768]{2,1,0:T(8,128)(2,1)S(1)}, bf16[8,64,768]{2,1,0:T(8,128)(2,1)S(1)}, u32[]{:S(2)}, u32[]{:S(2)}) collective-permute-start(bf16[8,64,768]{2,1,0:T(8,128)(2,1)S(1)} %copy-done.42), channel_id=1, source_target_pairs={{0,3},{1,2},{2,1},{3,0},{4,7},{5,6},{6,5},{7,4},{8,11},{9,10},{10,... | collective-permute-start | bytes 2359304 | tf_op jit(solution)/shard_map/ppermute | solution.py:25
  264.2 25.6 %collective-permute-start.44 = (bf16[4,2,96,768]{3,2,1,0:T(8,128)(2,1)}, bf16[4,2,96,768]{3,2,1,0:T(8,128)(2,1)S(1)}, u32[]{:S(2)}, u32[]{:S(2)}) collective-permute-start(bf16[4,2,96,768]{3,2,1,0:T(8,128)(2,1)} %get-tuple-element.243), channel_id=1, source_target_pairs={{0,1},{1,0},{2,3},{3,2},{4,5},{5,4},{6,7},{7,6},{8,9},{9,8},{10,11... | collective-permute-start | bytes 3538952 | tf_op jit(solution)/shard_map/ppermute | solution.py:25
  267.3 28.9 %collective-permute-start.45 = (bf16[4,2,96,768]{3,2,1,0:T(8,128)(2,1)S(1)}, bf16[4,2,96,768]{3,2,1,0:T(8,128)(2,1)S(1)}, u32[]{:S(2)}, u32[]{:S(2)}) collective-permute-start(bf16[4,2,96,768]{3,2,1,0:T(8,128)(2,1)S(1)} %fusion.1), channel_id=1, source_target_pairs={{0,4},{4,0},{8,12},{12,8},{16,20},{20,16},{24,28},{28,24},{1,5},{5... | collective-permute-start | bytes 3538952 | tf_op jit(solution)/shard_map/ppermute | solution.py:25
  282.8 2.2 collective-permute-start.37
  283.1 2.8 collective-permute-start.38
  288.6 32.6 %collective-permute-start.43 = (bf16[4,2,96,768]{3,2,1,0:T(8,128)(2,1)}, bf16[4,2,96,768]{3,2,1,0:T(8,128)(2,1)}, u32[]{:S(2)}, u32[]{:S(2)}) collective-permute-start(bf16[4,2,96,768]{3,2,1,0:T(8,128)(2,1)} %fusion), channel_id=1, source_target_pairs={{0,4},{4,0},{8,12},{12,8},{16,20},{20,16},{24,28},{28,24},{1,5},{5... | collective-permute-start | bytes 3538952 | tf_op jit(solution)/shard_map/ppermute | solution.py:25
  297.6 32.5 %all-to-all-start.3 = ((bf16[4,192,768]{2,1,0:T(8,128)(2,1)}), bf16[4,192,768]{2,1,0:T(8,128)(2,1)S(1)}, u32[]{:S(2)}, u32[]{:S(2)}) async-start(bf16[4,192,768]{2,1,0:T(8,128)(2,1)} %bitcast.73), calls=%async_computation.3 | async-start | bytes 2359296 | tf_op jit(solution)/shard_map/all_to_all | solution.py:496
  302.9 18.3 %collective-permute-start.40 = (bf16[4,2,96,768]{3,2,1,0:T(8,128)(2,1)}, bf16[4,2,96,768]{3,2,1,0:T(8,128)(2,1)}, u32[]{:S(2)}, u32[]{:S(2)}) collective-permute-start(bf16[4,2,96,768]{3,2,1,0:T(8,128)(2,1)} %get-tuple-element.234), channel_id=1, source_target_pairs={{0,1},{1,0},{2,3},{3,2},{4,5},{5,4},{6,7},{7,6},{8,9},{9,8},{10,11... | collective-permute-start | bytes 3538952 | tf_op jit(solution)/shard_map/ppermute | solution.py:25
  304.3 16.9 %collective-permute-start.39 = (bf16[384,768]{1,0:T(8,128)(2,1)}, bf16[384,768]{1,0:T(8,128)(2,1)}, u32[]{:S(2)}, u32[]{:S(2)}) collective-permute-start(bf16[384,768]{1,0:T(8,128)(2,1)} %reduce_sum.36), channel_id=1, source_target_pairs={{0,2},{1,3},{2,0},{3,1},{4,6},{5,7},{6,4},{7,5},{8,10},{9,11},{10,... | collective-permute-start | bytes 1769480 | tf_op jit(solution)/shard_map/ppermute | solution.py:25
  305.7 1.4 collective-permute-start.41
  307.9 13.3 %collective-permute-start.42 = (bf16[16,768]{1,0:T(8,128)(2,1)S(1)}, bf16[16,768]{1,0:T(8,128)(2,1)S(1)}, u32[]{:S(2)}, u32[]{:S(2)}) collective-permute-start(bf16[16,768]{1,0:T(8,128)(2,1)S(1)} %add_convert_fusion.5), channel_id=1, source_target_pairs={{0,4},{4,0},{8,12},{12,8},{16,20},{20,16},{24,28},{28,24},{1,5},{5... | collective-permute-start | bytes 73736 | tf_op jit(solution)/shard_map/ppermute | solution.py:25
  324.9 16.2 %collective-permute-start.49 = (bf16[384,768]{1,0:T(8,128)(2,1)S(1)}, bf16[384,768]{1,0:T(8,128)(2,1)}, u32[]{:S(2)}, u32[]{:S(2)}) collective-permute-start(bf16[384,768]{1,0:T(8,128)(2,1)S(1)} %copy-done.5), channel_id=1, source_target_pairs={{0,1},{1,0},{2,3},{3,2},{4,5},{5,4},{6,7},{7,6},{8,9},{9,8},{10,11... | collective-permute-start | bytes 1769480 | tf_op jit(solution)/shard_map/ppermute | solution.py:25
  324.9 16.2 %collective-permute-start.50 = (bf16[384,768]{1,0:T(8,128)(2,1)}, bf16[384,768]{1,0:T(8,128)(2,1)}, u32[]{:S(2)}, u32[]{:S(2)}) collective-permute-start(bf16[384,768]{1,0:T(8,128)(2,1)} %collective-permute-done.39), channel_id=1, source_target_pairs={{0,1},{1,0},{2,3},{3,2},{4,5},{5,4},{6,7},{7,6},{8,9},{9,8},{10,11... | collective-permute-start | bytes 1769480 | tf_op jit(solution)/shard_map/ppermute | solution.py:25
  330.1 33.7 %all-to-all-start.2 = ((bf16[4,208,768]{2,1,0:T(8,128)(2,1)}), bf16[4,208,768]{2,1,0:T(8,128)(2,1)S(1)}, u32[]{:S(2)}, u32[]{:S(2)}) async-start(bf16[4,208,768]{2,1,0:T(8,128)(2,1)} %pad_maximum_fusion.2), calls=%async_computation.2 | async-start | bytes 2555904 | tf_op jit(solution)/shard_map/all_to_all | solution.py:496
  333.7 18.6 %collective-permute-start.47 = (bf16[8,32,768]{2,1,0:T(8,128)(2,1)}, bf16[8,32,768]{2,1,0:T(8,128)(2,1)}, u32[]{:S(2)}, u32[]{:S(2)}) collective-permute-start(bf16[8,32,768]{2,1,0:T(8,128)(2,1)} %get-tuple-element.257.refs_4_), channel_id=1, source_target_pairs={{0,2},{1,3},{2,0},{3,1},{4,6},{5,7},{6,4},{7,5},{8,10},{9,11},{10,... | collective-permute-start | bytes 1179656 | tf_op jit(solution)/shard_map/ppermute | solution.py:25
  335.4 16.9 %collective-permute-start.46 = (bf16[192,768]{1,0:T(8,128)(2,1)S(1)}, bf16[192,768]{1,0:T(8,128)(2,1)S(1)}, u32[]{:S(2)}, u32[]{:S(2)}) collective-permute-start(bf16[192,768]{1,0:T(8,128)(2,1)S(1)} %reduce_sum.37), channel_id=1, source_target_pairs={{0,2},{1,3},{2,0},{3,1},{4,6},{5,7},{6,4},{7,5},{8,10},{9,11},{10,... | collective-permute-start | bytes 884744 | tf_op jit(solution)/shard_map/ppermute | solution.py:25
  336.1 22.7 %collective-permute-start.48 = (bf16[8,32,768]{2,1,0:T(8,128)(2,1)}, bf16[8,32,768]{2,1,0:T(8,128)(2,1)S(1)}, u32[]{:S(2)}, u32[]{:S(2)}) collective-permute-start(bf16[8,32,768]{2,1,0:T(8,128)(2,1)} %get-tuple-element.255.refs_1_), channel_id=1, source_target_pairs={{0,2},{1,3},{2,0},{3,1},{4,6},{5,7},{6,4},{7,5},{8,10},{9,11},{10,... | collective-permute-start | bytes 1179656 | tf_op jit(solution)/shard_map/ppermute | solution.py:25
  364.1 4.6 %collective-permute-start.56 = (bf16[192,768]{1,0:T(8,128)(2,1)S(1)}, bf16[192,768]{1,0:T(8,128)(2,1)S(1)}, u32[]{:S(2)}, u32[]{:S(2)}) collective-permute-start(bf16[192,768]{1,0:T(8,128)(2,1)S(1)} %copy-done.11), channel_id=1, source_target_pairs={{0,1},{1,0},{2,3},{3,2},{4,5},{5,4},{6,7},{7,6},{8,9},{9,8},{10,11... | collective-permute-start | bytes 884744 | tf_op jit(solution)/shard_map/ppermute | solution.py:25
  364.2 4.5 %collective-permute-start.57 = (bf16[192,768]{1,0:T(8,128)(2,1)S(1)}, bf16[192,768]{1,0:T(8,128)(2,1)}, u32[]{:S(2)}, u32[]{:S(2)}) collective-permute-start(bf16[192,768]{1,0:T(8,128)(2,1)S(1)} %collective-permute-done.46), channel_id=1, source_target_pairs={{0,1},{1,0},{2,3},{3,2},{4,5},{5,4},{6,7},{7,6},{8,9},{9,8},{10,11... | collective-permute-start | bytes 884744 | tf_op jit(solution)/shard_map/ppermute | solution.py:25
  365.7 5.8 %collective-permute-start.52 = (bf16[2,8,32,768]{3,2,1,0:T(8,128)(2,1)S(1)}, bf16[2,8,32,768]{3,2,1,0:T(8,128)(2,1)}, u32[]{:S(2)}, u32[]{:S(2)}) collective-permute-start(bf16[2,8,32,768]{3,2,1,0:T(8,128)(2,1)S(1)} %pad_maximum_fusion.9), channel_id=1, source_target_pairs={{0,1},{1,0},{2,3},{3,2},{4,5},{5,4},{6,7},{7,6},{8,9},{9,8},{10,11... | collective-permute-start | bytes 2359304 | tf_op jit(solution)/shard_map/ppermute | solution.py:25
  366.8 4.7 %collective-permute-start.51 = (bf16[2,8,32,768]{3,2,1,0:T(8,128)(2,1)}, bf16[2,8,32,768]{3,2,1,0:T(8,128)(2,1)S(1)}, u32[]{:S(2)}, u32[]{:S(2)}) collective-permute-start(bf16[2,8,32,768]{3,2,1,0:T(8,128)(2,1)} %pad_maximum_fusion.8), channel_id=1, source_target_pairs={{0,1},{1,0},{2,3},{3,2},{4,5},{5,4},{6,7},{7,6},{8,9},{9,8},{10,11... | collective-permute-start | bytes 2359304 | tf_op jit(solution)/shard_map/ppermute | solution.py:25
  367.3 9.5 %collective-permute-start.53 = (bf16[208,768]{1,0:T(8,128)(2,1)S(1)}, bf16[208,768]{1,0:T(8,128)(2,1)S(1)}, u32[]{:S(2)}, u32[]{:S(2)}) collective-permute-start(bf16[208,768]{1,0:T(8,128)(2,1)S(1)} %reduce_sum.38), channel_id=1, source_target_pairs={{0,2},{1,3},{2,0},{3,1},{4,6},{5,7},{6,4},{7,5},{8,10},{9,11},{10,... | collective-permute-start | bytes 958472 | tf_op jit(solution)/shard_map/ppermute | solution.py:25
  376.8 2.0 collective-permute-start.54
  376.9 2.0 collective-permute-start.55
  (43 other events, 284.7 us)

commit v3 on v2

--- a/solution.py
+++ b/solution.py
@@ -82,17 +82,19 @@
     rows = whole.shape[2] if by_rows else whole.shape[1] // SHARDS[0]
     started = []
     for which, pieces in ((c, weights[0]), (1 - c, weights[1])):
-        fast = len(pieces)
-        for b, piece in enumerate(pieces):
-            for k in range(piece.shape[0]):
-                shard = (z ^ k) * fast + (y ^ b)
-                for i in range(2):
-                    source = piece.at[k, pl.ds(i * rows, rows)]
-                    if by_rows:
-                        target = whole.at[shard, 2 * which + i]
-                    else:
-                        target = whole.at[2 * which + i, rows_of(shard * rows, rows)]
-                    started.append(copies.start(source, target))
+        slow = 4 if SHARDS[0] % 4 == 0 else 1
+        fast = SHARDS[0] // slow
+        for b, k in [(b, k) for b in range(fast) for k in range(slow)]:
+            shard = (z ^ k) * fast + (y ^ b)
+            first = slow - pieces[b].shape[0]
+            piece = pieces[b].at[k - first] if k >= first else pieces[fast + b]
+            for i in range(2):
+                source = piece.at[pl.ds(i * rows, rows)]
+                if by_rows:
+                    target = whole.at[shard, 2 * which + i]
+                else:
+                    target = whole.at[2 * which + i, rows_of(shard * rows, rows)]
+                started.append(copies.start(source, target))
     return started
 
 
@@ -209,7 +211,7 @@
 
 
 def cross_forward(
-    where, counts, x1, vec, memory, weights, x2, a2, q2, kv, p2, o2, weight, sems
+    where, counts, x1, vec, memory, weights, x2, a2, q2, kv, p2, o2, turned, weight, sems
 ):
     rows, width = x1.shape
     per = kv.shape[0]
@@ -229,6 +231,7 @@
         tokens = memory[:, i].reshape(total, width)
         for j in range(2):
             kv[i, :, columns(j, width)] = dot(tokens, weight[1 + j]).astype(BF)
+        turned[:, columns(i, total)] = tokens.T
     mask = head_mask(length)
     position = lax.broadcasted_iota(jnp.int32, (1, total), 1)
     probs = {}
@@ -385,27 +388,19 @@
         vecs[1:2, :] = shift_grad
 
 
-def cross_grads(
-    where, gx2, a2, o2, dq2, dkv, all_memory, near, far, theirs, grad, turned, memory, sems
-):
-    rows, width = gx2.shape
-    mem, examples, slots, _ = all_memory.shape
+def cross_grads(where, gx2, a2, o2, dq2, dkv, turned, near, far, theirs, grad, memory, sems):
+    width = gx2.shape[1]
     half = pl.program_id(0)
-    tokens = mem * examples * slots
 
     @pl.when(half == 0)
     def _():
-        copies = Copies(sems)
-        loads = [
-            copies.start(all_memory.at[d], memory.at[:, d * slots : (d + 1) * slots, :])
-            for d in range(mem)
-        ]
+        load = Copies(sems).start(turned, memory)
         grad[0] = dot_tn(a2[...], dq2[...]).astype(BF)
         grad[3] = dot_tn(o2[...], gx2[...].astype(BF)).astype(BF)
-        wait_all(loads)
-        turned[...] = memory[...].reshape(tokens, width).T
-
-    grad[1 + half] = dot(turned[...], dkv[...].reshape(tokens, width)).astype(BF)
+        load.wait()
+
+    part = dkv[...].reshape(memory.shape[1], width)
+    grad[1 + half] = dot(memory[...], part).astype(BF)
 
     @pl.when(half == 1)
     def _():
@@ -499,20 +494,28 @@
 class Gather:
     def __init__(self, half, slow, fast):
         self.half, self.slow, self.fast = half, slow, fast
+        self.own, self.own_other = [], []
 
     def send_slow(self, *others):
         half = after(self.half, *others)
         self.came = [half] + [swap(half, "fsdp", k * self.fast) for k in range(1, self.slow)]
 
+    def send_own(self):
+        self.own = [self.half] + [swap(self.half, "fsdp", b) for b in range(1, self.fast)]
+
+    def send_own_cores(self, *others):
+        self.own_other = [swap(after(piece, *others), "mem", 1) for piece in self.own]
+
     def send_fast(self, *others):
-        self.near = jnp.stack([after(piece, *others) for piece in self.came])
+        came = [after(piece, *others) for piece in self.came[1 if self.own else 0 :]]
+        self.near = jnp.stack(came)
         self.near_other = swap(self.near, "mem", 1)
         self.far = [swap(self.near, "fsdp", b) for b in range(1, self.fast)]
 
     def whole(self):
         mine = [self.near] + self.far
         theirs = [self.near_other] + [swap(piece, "mem", 1) for piece in self.far]
-        return mine, theirs
+        return mine + self.own, theirs + self.own_other
 
     @staticmethod
     def refs(weights):
@@ -693,9 +696,10 @@
         blocks = value.reshape((mem, examples) + value.shape[1:])
         return lax.all_to_all(blocks, "mem", 0, 0, tiled=True)
 
-    all_memory = exchange(memory)
+    all_memory = exchange(after(memory, self_gather.half))
     self_gather.send_slow()
-    sent = self_gather.came
+    out_gather.send_own()
+    sent = [*self_gather.came, *out_gather.own[1:]]
     self_gather.send_fast(*sent)
     cross_gather.send_slow(*sent)
     sent = [*self_gather.far, *cross_gather.came, all_memory]
@@ -753,7 +757,10 @@
     cross_weights = Gather.refs(cross_gather.whole())
     in_gather.send_fast(*cross_gather.far)
     out_gather.send_slow(*cross_gather.far)
-    x2, a2, q2, kv, p2, o2 = run(
+    out_gather.send_own_cores(*cross_gather.far)
+    tokens = examples * total
+    turned_spec = pl.BlockSpec((width, per * total), lambda e: (0, e))
+    x2, a2, q2, kv, p2, o2, turned = run(
         cross_forward,
         [(SMEM, where), (SMEM, counts), (VMEM, x1), (VMEM, vec)]
         + [slots_of_example(all_memory), cross_weights],
@@ -764,6 +771,7 @@
             per_example(shape_of((examples, total, 2 * width), BF)),
             per_example(shape_of((examples, GROUPS, TOGETHER * length, total), BF)),
             flat(wide, BF),
+            (turned_spec, shape_of((width, tokens), BF)),
         ],
         [square],
         blocks,
@@ -776,9 +784,10 @@
     in_gather.far = [after(piece, x2, *out_gather.came) for piece in in_gather.far]
     in_weights = Gather.refs(in_gather.whole())
     out_gather.send_fast(*in_gather.far)
+    ready = after(x2, out_gather.near_other, *out_gather.own_other)
     a3, h, slope, *grads = run(
         dense_inner,
-        [(SMEM, where), (VMEM, x2), (VMEM, vec), (VMEM, bias_in), (ANY, cotangent), in_weights],
+        [(SMEM, where), (VMEM, ready), (VMEM, vec), (VMEM, bias_in), (ANY, cotangent), in_weights],
         [flat(wide, BF), flat((rows, inner), BF), flat((rows, inner), BF)] + grads_like,
         [square, scratch(fsdp, 4, part, width), own_rows],
         1 + blocks,
@@ -837,10 +846,10 @@
     grads = run(
         cross_grads,
         [(SMEM, where), (VMEM, after(gx2, dense_total)), (VMEM, a2), (VMEM, o2), (VMEM, dq2)]
-        + [(pl.BlockSpec((examples, total, width), lambda j: (0, 0, j)), dkv), (ANY, all_memory)],
+        + [(pl.BlockSpec((examples, total, width), lambda j: (0, 0, j)), dkv), (ANY, turned)],
         grads_like,
-        [square, scratch(width, examples * total), scratch(examples, total, width)],
-        max(mem, blocks),
+        [square, scratch(width, tokens)],
+        blocks,
         (2,),
     )
     cross_scatter = scatter(grads, *mem_pieces[1:3])
@@ -880,13 +889,12 @@
     (out_low, in_low, out_high, in_high), _ = dense_sum.combine(c)
     grad_in = jnp.concatenate([in_low[:part], in_low[part:], in_high[:part], in_high[part:]], axis=1)
     grad_out = jnp.concatenate([out_low, out_high])
-    done = [*cross_sum.halves, *suffix_rows, *y_rows, grad_in, grad_out, memory_grad]
+    y_all, suffix_all = jnp.stack(y_rows), jnp.stack(suffix_rows)
+    done = [*cross_sum.halves, y_all, suffix_all, grad_in, grad_out, memory_grad]
     self_final = Replicas(self_scatter.add_slow(*done), part, across)
     cross_sum.swap_cores(self_final.halves[0])
-    y_rows = [after(value, self_final.halves[0]) for value in y_rows]
-    y_far = swap(jnp.stack(y_rows), "mem", 1)
-    suffix_rows = [after(value, self_final.halves[0]) for value in suffix_rows]
-    suffix_far = swap(jnp.stack(suffix_rows), "mem", 1)
+    y_far = swap(after(y_all, self_final.halves[0]), "mem", 1)
+    suffix_far = swap(after(suffix_all, self_final.halves[0]), "mem", 1)
     blocks = [([(ANY, x) for x in y_rows], (ANY, y_far))]
     blocks += [([(ANY, x) for x in suffix_rows], (ANY, suffix_far))]
     ((block_output, suffix_grad),) = run(

time: 384 us -> 378 us (0.984)
  waiting for transfers between devices: 138 us -> 128 us
    ppermute x58 -> x61, waiting for transfers between devices: 128 us -> 113 us  [swap(): return lax.ppermute(value, axis, [(i, i ^ distance) for i in range(size)])]
    all_to_all x3, waiting for transfers between devices: 9.74 us -> 15 us  [over_slow(): lax.all_to_all(value, 'fsdp', 0, 0, axis_index_groups=groups, tiled=True)]
    ppermute x58 -> x61, starting transfers between devices: 54.7 us -> 54.5 us  [swap(): return lax.ppermute(value, axis, [(i, i ^ distance) for i in range(size)])]
  transfers between devices with their start and end apart: 62 -> 65, of which waited for: 28 -> 29; matrix products, arithmetic and copies ran while one was open for 10% -> 10% of each run, Pallas kernels for 31% -> 31%
where the time goes in v3:
time: 378 us; the launch traced here: 374 us
  waiting for transfers between devices  128 us (34%)
  Pallas kernels  117 us (31%)
  starting transfers between devices  75.6 us (20%)
  other arithmetic  37.3 us (10%)
  local copies, waits for them, and re-layouts  15.2 us (4%)
    pallas_call x10, Pallas kernels, run(): pl.pallas_call(body, grid=grid, in_specs=[spec for spec, _ in flat_in], o...  117 us
    ppermute x61, waiting for transfers between devices, swap(): return lax.ppermute(value, axis, [(i, i ^ distance) for i in range(size)])  113 us
    ppermute x61, starting transfers between devices, swap(): return lax.ppermute(value, axis, [(i, i ^ distance) for i in range(size)])  54.5 us
    all_to_all x3, starting transfers between devices, over_slow(): lax.all_to_all(value, 'fsdp', 0, 0, axis_index_groups=groups, tiled=True)  16.9 us
    all_to_all x3, waiting for transfers between devices, over_slow(): lax.all_to_all(value, 'fsdp', 0, 0, axis_index_groups=groups, tiled=True)  15 us
  transfers between devices with their start and end apart: 65, of which 29 were waited for; matrix products, arithmetic and copies ran while one was open for 10% of the time, Pallas kernels for 31%

profile of v3, /device:TPU:0, one launch (start us, length us, event | category | flops | bytes accessed | tf_op | source)
XLA Modules:
  0.0 374.4 jit_solution(5928348238142226878)
XLA Ops:
  1.6 1.2 maximum_select_fusion
  3.6 4.2 %all-to-all-start = ((bf16[4,8,64,768]{3,2,1,0:T(8,128)(2,1)}), bf16[4,8,64,768]{3,2,1,0:T(8,128)(2,1)S(1)}, u32[]{:S(2)}, u32[]{:S(2)}) async-start(bf16[4,8,64,768]{3,2,1,0:T(8,128)(2,1)} %bitcast.75), calls=%async_computation | async-start | bytes 6291456 | tf_op jit(solution)/shard_map/all_to_all | solution.py:697
  7.8 2.6 collective-permute-start
  10.4 2.6 collective-permute-start.1
  13.0 1.8 slice_select_fusion.refs_9_
  14.8 1.7 collective-permute-start.3
  16.5 7.3 %collective-permute-done.3.refs_10_ = bf16[192,768]{1,0:T(8,128)(2,1)S(1)} collective-permute-done((bf16[192,768]{1,0:T(8,128)(2,1)}, bf16[192,768]{1,0:T(8,128)(2,1)S(1)}, u32[]{:S(2)}, u32[]{:S(2)}) %collective-permute-start.3) | collective-permute-done | bytes 294944 | tf_op jit(solution)/shard_map/ppermute | solution.py:25
  24.9 10.5 %collective-permute-done.1 = bf16[208,768]{1,0:T(8,128)(2,1)S(1)} collective-permute-done((bf16[208,768]{1,0:T(8,128)(2,1)S(1)}, bf16[208,768]{1,0:T(8,128)(2,1)S(1)}, u32[]{:S(2)}, u32[]{:S(2)}) %collective-permute-start.1) | collective-permute-done | bytes 319520 | tf_op jit(solution)/shard_map/ppermute | solution.py:25
  35.4 1.3 pad_maximum_fusion.1.refs_2_.refs_12_
  36.7 1.6 collective-permute-start.4
  38.5 6.7 %collective-permute-start.5 = (bf16[192,768]{1,0:T(8,128)(2,1)S(1)}, bf16[192,768]{1,0:T(8,128)(2,1)S(1)}, u32[]{:S(2)}, u32[]{:S(2)}) collective-permute-start(bf16[192,768]{1,0:T(8,128)(2,1)S(1)} %get-tuple-element.153), channel_id=1, source_target_pairs={{0,8},{4,12},{8,0},{12,4},{16,24},{20,28},{24,16},{28,20},{1,9},{5... | collective-permute-start | bytes 884744 | tf_op jit(solution)/shard_map/ppermute | solution.py:25
  46.3 1.4 collective-permute-start.7
  47.7 8.9 %collective-permute-done.5 = bf16[192,768]{1,0:T(8,128)(2,1)S(1)} collective-permute-done((bf16[192,768]{1,0:T(8,128)(2,1)S(1)}, bf16[192,768]{1,0:T(8,128)(2,1)S(1)}, u32[]{:S(2)}, u32[]{:S(2)}) %collective-permute-start.5) | collective-permute-done | bytes 294944 | tf_op jit(solution)/shard_map/ppermute | solution.py:25
  56.6 12.1 %collective-permute-done.6 = bf16[192,768]{1,0:T(8,128)(2,1)S(1)} collective-permute-done((bf16[192,768]{1,0:T(8,128)(2,1)S(1)}, bf16[192,768]{1,0:T(8,128)(2,1)S(1)}, u32[]{:S(2)}, u32[]{:S(2)}) %collective-permute-start.6) | collective-permute-done | bytes 294944 | tf_op jit(solution)/shard_map/ppermute | solution.py:25
  70.2 3.3 pad_maximum_fusion.3.refs_5_.refs_7_
  74.5 4.2 %collective-permute-start.11 = (bf16[192,768]{1,0:T(8,128)(2,1)S(1)}, bf16[192,768]{1,0:T(8,128)(2,1)}, u32[]{:S(2)}, u32[]{:S(2)}) collective-permute-start(bf16[192,768]{1,0:T(8,128)(2,1)S(1)} %get-tuple-element.161), channel_id=1, source_target_pairs={{0,8},{4,12},{8,0},{12,4},{16,24},{20,28},{24,16},{28,20},{1,9},{5... | collective-permute-start | bytes 884744 | tf_op jit(solution)/shard_map/ppermute | solution.py:25
  79.7 1.5 collective-permute-start.13
  81.8 7.6 %shard_map.373 = (f32[256,768]{1,0:T(8,128)}, bf16[256,768]{1,0:T(8,128)(2,1)}, bf16[256,2304]{1,0:T(8,128)(2,1)}, bf16[6,512,128]{2,1,0:T(8,128)(2,1)}, bf16[256,768]{1,0:T(8,128)(2,1)}, /*index=5*/f32[16,768]{1,0:T(8,128)}) custom-call(s32[4]{0:T(128)} %pad_add_fusion.1.refs_0_, bf16[32,32,768]{2,1,0:T(8,128)(2,1)} %refs_1_.5, ...), custom_call_target="tpu_custom_call" | custom-call | tf_op jit(solution)/shard_map/pallas_call | solution.py:470
  90.6 11.7 %collective-permute-done.12 = bf16[192,768]{1,0:T(8,128)(2,1)} collective-permute-done((bf16[192,768]{1,0:T(8,128)(2,1)S(1)}, bf16[192,768]{1,0:T(8,128)(2,1)}, u32[]{:S(2)}, u32[]{:S(2)}) %collective-permute-start.12) | collective-permute-done | bytes 294944 | tf_op jit(solution)/shard_map/ppermute | solution.py:25
  102.3 1.3 pad_maximum_fusion.4.refs_5_
  104.5 4.9 %collective-permute-start.16 = (bf16[192,768]{1,0:T(8,128)(2,1)}, bf16[192,768]{1,0:T(8,128)(2,1)S(1)}, u32[]{:S(2)}, u32[]{:S(2)}) collective-permute-start(bf16[192,768]{1,0:T(8,128)(2,1)} %slice_select_fusion.refs_9_), channel_id=1, source_target_pairs={{0,8},{4,12},{8,0},{12,4},{16,24},{20,28},{24,16},{28,20},{1,9},{5... | collective-permute-start | bytes 884744 | tf_op jit(solution)/shard_map/ppermute | solution.py:25
  110.4 1.5 collective-permute-start.19
  113.0 15.5 %shard_map.374 = (f32[256,768]{1,0:T(8,128)}, bf16[256,768]{1,0:T(8,128)(2,1)}, bf16[256,768]{1,0:T(8,128)(2,1)}, bf16[8,256,1536]{2,1,0:T(8,128)(2,1)}, bf16[8,...) custom-call(s32[4]{0:T(128)} %pad_add_fusion.1.refs_0_, s32[32]{0:T(128)} %refs_1_.4, ...), custom_call_target="tpu_custom_call" | custom-call | tf_op jit(solution)/shard_map/pallas_call | solution.py:470
  128.5 4.5 %collective-permute-done.18 = bf16[192,768]{1,0:T(8,128)(2,1)S(1)} collective-permute-done((bf16[192,768]{1,0:T(8,128)(2,1)}, bf16[192,768]{1,0:T(8,128)(2,1)S(1)}, u32[]{:S(2)}, u32[]{:S(2)}) %collective-permute-start.18) | collective-permute-done | bytes 294944 | tf_op jit(solution)/shard_map/ppermute | solution.py:25
  133.1 1.2 pad_maximum_fusion.7.refs_7_
  134.6 1.2 collective-permute-start.25
  142.8 13.6 %shard_map.375 = (bf16[256,768]{1,0:T(8,128)(2,1)}, bf16[256,3072]{1,0:T(8,128)(2,1)}, bf16[256,3072]{1,0:T(8,128)(2,1)}, bf16[4,2,96,768]{3,2,1,0:T(8,128)(2,1)...) custom-call(s32[4]{0:T(128)} %pad_add_fusion.1.refs_0_, ...), custom_call_target="tpu_custom_call" | custom-call | tf_op jit(solution)/shard_map/pallas_call | solution.py:470
  157.2 1.7 collective-permute-done.26
  159.8 1.6 fusion.3
  161.4 1.3 collective-permute-start.29
  163.6 11.8 %shard_map.376 = (bf16[8,32,768]{2,1,0:T(8,128)(2,1)}, bf16[256,3072]{1,0:T(8,128)(2,1)}, f32[1,768]{1,0:T(1,128)}, f32[1,3072]{1,0:T(1,128)}, bf16[4,2,96,768]{...) custom-call(s32[4]{0:T(128)} %pad_add_fusion.1.refs_0_, ...), custom_call_target="tpu_custom_call" | custom-call | tf_op jit(solution)/shard_map/pallas_call | solution.py:470
  175.5 19.9 %shard_map.377 = (f32[256,768]{1,0:T(8,128)}, f32[2,768]{1,0:T(2,128)}) custom-call(s32[4]{0:T(128)} %pad_add_fusion.1.refs_0_, f32[256,768]{1,0:T(8,128)} %get-tuple-element.180.refs_1_, f32[16,768]{1,0:T(8,128)} %get-tuple-element.152.refs_3_.refs_2_, bf16[256,3072]{1,0:T(8,128)(2,1)} %get-tuple-element.184.refs_3_, bf16[32,32,768]{2,1,0:T(8,128)(2,1)} %refs_4_.3, ...), custom_call_target="tpu_custom_call" | custom-call | tf_op jit(solution)/shard_map/pallas_call | solution.py:470
  195.9 1.5 collective-permute-done.30
  200.0 17.8 %shard_map.378 = (f32[256,768]{1,0:T(8,128)}, f32[2,768]{1,0:T(2,128)}, bf16[8,256,1536]{2,1,0:T(8,128)(2,1)}, bf16[256,768]{1,0:T(8,128)(2,1)}, bf16[8,64,768]{...) custom-call(s32[4]{0:T(128)} %pad_add_fusion.1.refs_0_, ...), custom_call_target="tpu_custom_call" | custom-call | bytes 60000000 | tf_op jit(solution)/shard_map/pallas_call | solution.py:470
  217.7 8.9 %collective-permute-done.32 = bf16[4,2,96,768]{3,2,1,0:T(8,128)(2,1)S(1)} collective-permute-done((bf16[4,2,96,768]{3,2,1,0:T(8,128)(2,1)S(1)}, bf16[4,2,96,768]{3,2,1,0:T(8,128)(2,1)S(1)}, u32[]{:S(2)}, u32[]{:S(2)}) %collective-permute-start.32) | collective-permute-done | bytes 1179680 | tf_op jit(solution)/shard_map/ppermute | solution.py:25
  228.4 1.6 pad_maximum_fusion
  230.0 8.0 %all-to-all-start.1 = ((bf16[4,384,768]{2,1,0:T(8,128)(2,1)}), bf16[4,384,768]{2,1,0:T(8,128)(2,1)S(1)}, u32[]{:S(2)}, u32[]{:S(2)}) async-start(bf16[4,384,768]{2,1,0:T(8,128)(2,1)} %pad_maximum_fusion), calls=%async_computation.1 | async-start | bytes 4718592 | tf_op jit(solution)/shard_map/all_to_all | solution.py:491
  238.0 1.4 collective-permute-start.36
  239.4 12.3 %shard_map.379 = (bf16[4,2,96,768]{3,2,1,0:T(8,128)(2,1)}, bf16[1,4,2,96,768]{4,3,2,1,0:T(8,128)(2,1)}, bf16[4,2,96,768]{3,2,1,0:T(8,128)(2,1)}, bf16[2,2,96,768]{3,2,1,0:T(8,128)(2,1)}, bf16[2,2,96,768]{3,2,1,0:T(8,128)(2,1)}) custom-call(s32[4]{0:T(128)} %pad_add_fusion.1.refs_0_, f32[256,768]{1,0:T(8,128)} %get-tuple-element.206.refs_3_.refs_1_, ...), custom_call_target="tpu_custom_call" | custom-call | tf_op jit(solution)/shard_map/pallas_call | solution.py:470
  251.7 6.4 %collective-permute-done.36.refs_3_ = bf16[8,64,768]{2,1,0:T(8,128)(2,1)S(1)} collective-permute-done((bf16[8,64,768]{2,1,0:T(8,128)(2,1)}, bf16[8,64,768]{2,1,0:T(8,128)(2,1)S(1)}, u32[]{:S(2)}, u32[]{:S(2)}) %collective-permute-start.36) | collective-permute-done | bytes 786464 | tf_op jit(solution)/shard_map/ppermute | solution.py:25
  261.3 1.5 fusion.1
  263.7 11.7 %shard_map.380 = (bf16[8,32,768]{2,1,0:T(8,128)(2,1)}, bf16[16,768]{1,0:T(8,128)(2,1)}, bf16[4,2,96,768]{3,2,1,0:T(8,128)(2,1)}, bf16[1,4,2,96,768]{4,3,2,1,0:T(...) custom-call(s32[4]{0:T(128)} %pad_add_fusion.1.refs_0_, ...), custom_call_target="tpu_custom_call" | custom-call | tf_op jit(solution)/shard_map/pallas_call | solution.py:470
  275.4 3.0 collective-permute-done.39.refs_4_
  278.9 1.7 collective-permute-done.40
  281.4 2.7 fusion
  284.9 6.8 %collective-permute-done.49 = bf16[4,2,96,768]{3,2,1,0:T(8,128)(2,1)S(1)} collective-permute-done((bf16[4,2,96,768]{3,2,1,0:T(8,128)(2,1)S(1)}, bf16[4,2,96,768]{3,2,1,0:T(8,128)(2,1)S(1)}, u32[]{:S(2)}, u32[]{:S(2)}) %collective-permute-start.49) | collective-permute-done | bytes 1179680 | tf_op jit(solution)/shard_map/ppermute | solution.py:25
  291.7 1.5 add_convert_fusion
  293.2 5.1 %all-to-all-start.3 = ((bf16[4,192,768]{2,1,0:T(8,128)(2,1)}), bf16[4,192,768]{2,1,0:T(8,128)(2,1)S(1)}, u32[]{:S(2)}, u32[]{:S(2)}) async-start(bf16[4,192,768]{2,1,0:T(8,128)(2,1)} %bitcast.72), calls=%async_computation.3 | async-start | bytes 2359296 | tf_op jit(solution)/shard_map/all_to_all | solution.py:491
  298.2 1.3 reduce_sum.36
  299.6 1.4 collective-permute-start.42
  303.9 12.8 %collective-permute-done.45 = bf16[16,768]{1,0:T(8,128)(2,1)S(1)} collective-permute-done((bf16[16,768]{1,0:T(8,128)(2,1)S(1)}, bf16[16,768]{1,0:T(8,128)(2,1)S(1)}, u32[]{:S(2)}, u32[]{:S(2)}) %collective-permute-start.45) | collective-permute-done | bytes 24608 | tf_op jit(solution)/shard_map/ppermute | solution.py:25
  316.7 2.4 add_convert_fusion.1
  320.3 1.4 collective-permute-start.51
  322.2 3.2 all-to-all-done.3
  325.5 3.8 %all-to-all-start.2 = ((bf16[4,208,768]{2,1,0:T(8,128)(2,1)}), bf16[4,208,768]{2,1,0:T(8,128)(2,1)S(1)}, u32[]{:S(2)}, u32[]{:S(2)}) async-start(bf16[4,208,768]{2,1,0:T(8,128)(2,1)} %pad_maximum_fusion.2), calls=%async_computation.2 | async-start | bytes 2555904 | tf_op jit(solution)/shard_map/all_to_all | solution.py:491
  329.2 1.5 collective-permute-start.47
  332.3 3.5 shard_map.381
  337.0 4.5 %collective-permute-done.47.refs_2_ = bf16[8,32,768]{2,1,0:T(8,128)(2,1)} collective-permute-done((bf16[8,32,768]{2,1,0:T(8,128)(2,1)S(1)}, bf16[8,32,768]{2,1,0:T(8,128)(2,1)}, u32[]{:S(2)}, u32[]{:S(2)}) %collective-permute-start.47) | collective-permute-done | bytes 393248 | tf_op jit(solution)/shard_map/ppermute | solution.py:25
  341.4 1.9 pad_maximum_fusion.8
  343.4 1.7 fusion.5
  347.5 11.8 %all-to-all-done.2 = bf16[4,208,768]{2,1,0:T(8,128)(2,1)S(1)} async-done(((bf16[4,208,768]{2,1,0:T(8,128)(2,1)}), bf16[4,208,768]{2,1,0:T(8,128)(2,1)S(1)}, u32[]{:S(2)}, u32[]{:S(2)}) %all-to-all-start.2) | async-done | bytes 1277984 | tf_op jit(solution)/shard_map/all_to_all | solution.py:491
  360.7 1.4 collective-permute-start.56
  364.3 3.4 shard_map.382
  367.8 2.5 collective-permute-done.56
  (200 shorter events, 50.5 us)
Async XLA Ops:
  3.6 66.5 %all-to-all-start = ((bf16[4,8,64,768]{3,2,1,0:T(8,128)(2,1)}), bf16[4,8,64,768]{3,2,1,0:T(8,128)(2,1)S(1)}, u32[]{:S(2)}, u32[]{:S(2)}) async-start(bf16[4,8,64,768]{3,2,1,0:T(8,128)(2,1)} %bitcast.75), calls=%async_computation | async-start | bytes 6291456 | tf_op jit(solution)/shard_map/all_to_all | solution.py:697
  7.8 17.1 %collective-permute-start = (bf16[208,768]{1,0:T(8,128)(2,1)S(1)}, bf16[208,768]{1,0:T(8,128)(2,1)S(1)}, u32[]{:S(2)}, u32[]{:S(2)}) collective-permute-start(bf16[208,768]{1,0:T(8,128)(2,1)S(1)} %pad_maximum_fusion.10), channel_id=1, source_target_pairs={{0,8},{4,12},{8,0},{12,4},{16,24},{20,28},{24,16},{28,20},{1,9},{5... | collective-permute-start | bytes 958472 | tf_op jit(solution)/shard_map/ppermute | solution.py:25
  10.4 25.0 %collective-permute-start.1 = (bf16[208,768]{1,0:T(8,128)(2,1)S(1)}, bf16[208,768]{1,0:T(8,128)(2,1)S(1)}, u32[]{:S(2)}, u32[]{:S(2)}) collective-permute-start(bf16[208,768]{1,0:T(8,128)(2,1)S(1)} %pad_maximum_fusion.10), channel_id=1, source_target_pairs={{0,16},{4,20},{8,24},{12,28},{16,0},{20,4},{24,8},{28,12},{1,17},{... | collective-permute-start | bytes 958472 | tf_op jit(solution)/shard_map/ppermute | solution.py:25
  13.0 22.4 %collective-permute-start.2 = (bf16[208,768]{1,0:T(8,128)(2,1)S(1)}, bf16[208,768]{1,0:T(8,128)(2,1)S(1)}, u32[]{:S(2)}, u32[]{:S(2)}) collective-permute-start(bf16[208,768]{1,0:T(8,128)(2,1)S(1)} %pad_maximum_fusion.10), channel_id=1, source_target_pairs={{0,24},{4,28},{8,16},{12,20},{16,8},{20,12},{24,0},{28,4},{1,25},{... | collective-permute-start | bytes 958472 | tf_op jit(solution)/shard_map/ppermute | solution.py:25
  14.8 9.0 %collective-permute-start.3 = (bf16[192,768]{1,0:T(8,128)(2,1)}, bf16[192,768]{1,0:T(8,128)(2,1)S(1)}, u32[]{:S(2)}, u32[]{:S(2)}) collective-permute-start(bf16[192,768]{1,0:T(8,128)(2,1)} %slice_select_fusion.refs_9_), channel_id=1, source_target_pairs={{0,4},{4,0},{8,12},{12,8},{16,20},{20,16},{24,28},{28,24},{1,5},{5... | collective-permute-start | bytes 884744 | tf_op jit(solution)/shard_map/ppermute | solution.py:25
  36.7 33.4 %collective-permute-start.4 = (bf16[4,208,768]{2,1,0:T(8,128)(2,1)}, bf16[4,208,768]{2,1,0:T(8,128)(2,1)}, u32[]{:S(2)}, u32[]{:S(2)}) collective-permute-start(bf16[4,208,768]{2,1,0:T(8,128)(2,1)} %pad_maximum_fusion.1.refs_2_.refs_12_), channel_id=1, source_target_pairs={{0,4},{4,0},{8,12},{12,8},{16,20},{20,16},{24,28},{28,24},{1,5},{5... | collective-permute-start | bytes 3833864 | tf_op jit(solution)/shard_map/ppermute | solution.py:25
  38.5 18.0 %collective-permute-start.5 = (bf16[192,768]{1,0:T(8,128)(2,1)S(1)}, bf16[192,768]{1,0:T(8,128)(2,1)S(1)}, u32[]{:S(2)}, u32[]{:S(2)}) collective-permute-start(bf16[192,768]{1,0:T(8,128)(2,1)S(1)} %get-tuple-element.153), channel_id=1, source_target_pairs={{0,8},{4,12},{8,0},{12,4},{16,24},{20,28},{24,16},{28,20},{1,9},{5... | collective-permute-start | bytes 884744 | tf_op jit(solution)/shard_map/ppermute | solution.py:25
  45.2 23.5 %collective-permute-start.6 = (bf16[192,768]{1,0:T(8,128)(2,1)S(1)}, bf16[192,768]{1,0:T(8,128)(2,1)S(1)}, u32[]{:S(2)}, u32[]{:S(2)}) collective-permute-start(bf16[192,768]{1,0:T(8,128)(2,1)S(1)} %get-tuple-element.153), channel_id=1, source_target_pairs={{0,16},{4,20},{8,24},{12,28},{16,0},{20,4},{24,8},{28,12},{1,17},{... | collective-permute-start | bytes 884744 | tf_op jit(solution)/shard_map/ppermute | solution.py:25
  46.3 22.4 %collective-permute-start.7 = (bf16[192,768]{1,0:T(8,128)(2,1)S(1)}, bf16[192,768]{1,0:T(8,128)(2,1)S(1)}, u32[]{:S(2)}, u32[]{:S(2)}) collective-permute-start(bf16[192,768]{1,0:T(8,128)(2,1)S(1)} %get-tuple-element.153), channel_id=1, source_target_pairs={{0,24},{4,28},{8,16},{12,20},{16,8},{20,12},{24,0},{28,4},{1,25},{... | collective-permute-start | bytes 884744 | tf_op jit(solution)/shard_map/ppermute | solution.py:25
  47.7 32.0 %collective-permute-start.8 = (bf16[4,208,768]{2,1,0:T(8,128)(2,1)}, bf16[4,208,768]{2,1,0:T(8,128)(2,1)}, u32[]{:S(2)}, u32[]{:S(2)}) collective-permute-start(bf16[4,208,768]{2,1,0:T(8,128)(2,1)} %pad_maximum_fusion.1.refs_2_.refs_12_), channel_id=1, source_target_pairs={{0,1},{1,0},{2,3},{3,2},{4,5},{5,4},{6,7},{7,6},{8,9},{9,8},{10,11... | collective-permute-start | bytes 3833864 | tf_op jit(solution)/shard_map/ppermute | solution.py:25
  70.1 11.0 %collective-permute-start.9 = (bf16[4,208,768]{2,1,0:T(8,128)(2,1)}, bf16[4,208,768]{2,1,0:T(8,128)(2,1)}, u32[]{:S(2)}, u32[]{:S(2)}) collective-permute-start(bf16[4,208,768]{2,1,0:T(8,128)(2,1)} %collective-permute-done.4.refs_3_.refs_13_), channel_id=1, source_target_pairs={{0,1},{1,0},{2,3},{3,2},{4,5},{5,4},{6,7},{7,6},{8,9},{9,8},{10,11... | collective-permute-start | bytes 3833864 | tf_op jit(solution)/shard_map/ppermute | solution.py:25
  73.5 28.8 %collective-permute-start.10 = (bf16[4,192,768]{2,1,0:T(8,128)(2,1)}, bf16[4,192,768]{2,1,0:T(8,128)(2,1)}, u32[]{:S(2)}, u32[]{:S(2)}) collective-permute-start(bf16[4,192,768]{2,1,0:T(8,128)(2,1)} %pad_maximum_fusion.3.refs_5_.refs_7_), channel_id=1, source_target_pairs={{0,4},{4,0},{8,12},{12,8},{16,20},{20,16},{24,28},{28,24},{1,5},{5... | collective-permute-start | bytes 3538952 | tf_op jit(solution)/shard_map/ppermute | solution.py:25
  74.5 16.1 %collective-permute-start.11 = (bf16[192,768]{1,0:T(8,128)(2,1)S(1)}, bf16[192,768]{1,0:T(8,128)(2,1)}, u32[]{:S(2)}, u32[]{:S(2)}) collective-permute-start(bf16[192,768]{1,0:T(8,128)(2,1)S(1)} %get-tuple-element.161), channel_id=1, source_target_pairs={{0,8},{4,12},{8,0},{12,4},{16,24},{20,28},{24,16},{28,20},{1,9},{5... | collective-permute-start | bytes 884744 | tf_op jit(solution)/shard_map/ppermute | solution.py:25
  78.7 23.6 %collective-permute-start.12 = (bf16[192,768]{1,0:T(8,128)(2,1)S(1)}, bf16[192,768]{1,0:T(8,128)(2,1)}, u32[]{:S(2)}, u32[]{:S(2)}) collective-permute-start(bf16[192,768]{1,0:T(8,128)(2,1)S(1)} %get-tuple-element.161), channel_id=1, source_target_pairs={{0,16},{4,20},{8,24},{12,28},{16,0},{20,4},{24,8},{28,12},{1,17},{... | collective-permute-start | bytes 884744 | tf_op jit(solution)/shard_map/ppermute | solution.py:25
  79.7 22.6 %collective-permute-start.13 = (bf16[192,768]{1,0:T(8,128)(2,1)S(1)}, bf16[192,768]{1,0:T(8,128)(2,1)}, u32[]{:S(2)}, u32[]{:S(2)}) collective-permute-start(bf16[192,768]{1,0:T(8,128)(2,1)S(1)} %get-tuple-element.161), channel_id=1, source_target_pairs={{0,24},{4,28},{8,16},{12,20},{16,8},{20,12},{24,0},{28,4},{1,25},{... | collective-permute-start | bytes 884744 | tf_op jit(solution)/shard_map/ppermute | solution.py:25
  81.2 29.2 %collective-permute-start.14 = (bf16[4,192,768]{2,1,0:T(8,128)(2,1)}, bf16[4,192,768]{2,1,0:T(8,128)(2,1)}, u32[]{:S(2)}, u32[]{:S(2)}) collective-permute-start(bf16[4,192,768]{2,1,0:T(8,128)(2,1)} %pad_maximum_fusion.3.refs_5_.refs_7_), channel_id=1, source_target_pairs={{0,1},{1,0},{2,3},{3,2},{4,5},{5,4},{6,7},{7,6},{8,9},{9,8},{10,11... | collective-permute-start | bytes 3538952 | tf_op jit(solution)/shard_map/ppermute | solution.py:25
  102.3 9.6 %collective-permute-start.15 = (bf16[4,192,768]{2,1,0:T(8,128)(2,1)}, bf16[4,192,768]{2,1,0:T(8,128)(2,1)S(1)}, u32[]{:S(2)}, u32[]{:S(2)}) collective-permute-start(bf16[4,192,768]{2,1,0:T(8,128)(2,1)} %collective-permute-done.10.refs_6_.refs_8_), channel_id=1, source_target_pairs={{0,1},{1,0},{2,3},{3,2},{4,5},{5,4},{6,7},{7,6},{8,9},{9,8},{10,11... | collective-permute-start | bytes 3538952 | tf_op jit(solution)/shard_map/ppermute | solution.py:25
  103.6 29.4 %collective-permute-start.17 = (bf16[4,192,768]{2,1,0:T(8,128)(2,1)S(1)}, bf16[4,192,768]{2,1,0:T(8,128)(2,1)S(1)}, u32[]{:S(2)}, u32[]{:S(2)}) collective-permute-start(bf16[4,192,768]{2,1,0:T(8,128)(2,1)S(1)} %pad_maximum_fusion.4.refs_5_), channel_id=1, source_target_pairs={{0,4},{4,0},{8,12},{12,8},{16,20},{20,16},{24,28},{28,24},{1,5},{5... | collective-permute-start | bytes 3538952 | tf_op jit(solution)/shard_map/ppermute | solution.py:25
  104.5 24.0 %collective-permute-start.16 = (bf16[192,768]{1,0:T(8,128)(2,1)}, bf16[192,768]{1,0:T(8,128)(2,1)S(1)}, u32[]{:S(2)}, u32[]{:S(2)}) collective-permute-start(bf16[192,768]{1,0:T(8,128)(2,1)} %slice_select_fusion.refs_9_), channel_id=1, source_target_pairs={{0,8},{4,12},{8,0},{12,4},{16,24},{20,28},{24,16},{28,20},{1,9},{5... | collective-permute-start | bytes 884744 | tf_op jit(solution)/shard_map/ppermute | solution.py:25
  109.4 23.6 %collective-permute-start.18 = (bf16[192,768]{1,0:T(8,128)(2,1)}, bf16[192,768]{1,0:T(8,128)(2,1)S(1)}, u32[]{:S(2)}, u32[]{:S(2)}) collective-permute-start(bf16[192,768]{1,0:T(8,128)(2,1)} %slice_select_fusion.refs_9_), channel_id=1, source_target_pairs={{0,16},{4,20},{8,24},{12,28},{16,0},{20,4},{24,8},{28,12},{1,17},{... | collective-permute-start | bytes 884744 | tf_op jit(solution)/shard_map/ppermute | solution.py:25
  110.4 22.6 %collective-permute-start.19 = (bf16[192,768]{1,0:T(8,128)(2,1)}, bf16[192,768]{1,0:T(8,128)(2,1)S(1)}, u32[]{:S(2)}, u32[]{:S(2)}) collective-permute-start(bf16[192,768]{1,0:T(8,128)(2,1)} %slice_select_fusion.refs_9_), channel_id=1, source_target_pairs={{0,24},{4,28},{8,16},{12,20},{16,8},{20,12},{24,0},{28,4},{1,25},{... | collective-permute-start | bytes 884744 | tf_op jit(solution)/shard_map/ppermute | solution.py:25
  111.9 29.9 %collective-permute-start.23 = (bf16[4,192,768]{2,1,0:T(8,128)(2,1)S(1)}, bf16[4,192,768]{2,1,0:T(8,128)(2,1)}, u32[]{:S(2)}, u32[]{:S(2)}) collective-permute-start(bf16[4,192,768]{2,1,0:T(8,128)(2,1)S(1)} %pad_maximum_fusion.4.refs_5_), channel_id=1, source_target_pairs={{0,1},{1,0},{2,3},{3,2},{4,5},{5,4},{6,7},{7,6},{8,9},{9,8},{10,11... | collective-permute-start | bytes 3538952 | tf_op jit(solution)/shard_map/ppermute | solution.py:25
  133.0 8.7 %collective-permute-start.24 = (bf16[4,192,768]{2,1,0:T(8,128)(2,1)S(1)}, bf16[4,192,768]{2,1,0:T(8,128)(2,1)S(1)}, u32[]{:S(2)}, u32[]{:S(2)}) collective-permute-start(bf16[4,192,768]{2,1,0:T(8,128)(2,1)S(1)} %collective-permute-done.17.refs_6_), channel_id=1, source_target_pairs={{0,1},{1,0},{2,3},{3,2},{4,5},{5,4},{6,7},{7,6},{8,9},{9,8},{10,11... | collective-permute-start | bytes 3538952 | tf_op jit(solution)/shard_map/ppermute | solution.py:25
  134.3 7.4 %collective-permute-start.20 = (bf16[3,192,768]{2,1,0:T(8,128)(2,1)}, bf16[3,192,768]{2,1,0:T(8,128)(2,1)}, u32[]{:S(2)}, u32[]{:S(2)}) collective-permute-start(bf16[3,192,768]{2,1,0:T(8,128)(2,1)} %pad_maximum_fusion.7.refs_7_), channel_id=1, source_target_pairs={{0,1},{1,0},{2,3},{3,2},{4,5},{5,4},{6,7},{7,6},{8,9},{9,8},{10,11... | collective-permute-start | bytes 2654216 | tf_op jit(solution)/shard_map/ppermute | solution.py:25
  134.6 22.1 %collective-permute-start.25 = (bf16[3,192,768]{2,1,0:T(8,128)(2,1)}, bf16[3,192,768]{2,1,0:T(8,128)(2,1)}, u32[]{:S(2)}, u32[]{:S(2)}) collective-permute-start(bf16[3,192,768]{2,1,0:T(8,128)(2,1)} %pad_maximum_fusion.7.refs_7_), channel_id=1, source_target_pairs={{0,4},{4,0},{8,12},{12,8},{16,20},{20,16},{24,28},{28,24},{1,5},{5... | collective-permute-start | bytes 2654216 | tf_op jit(solution)/shard_map/ppermute | solution.py:25
  135.9 2.0 collective-permute-start.22
  138.6 3.2 collective-permute-start.21
  156.7 2.2 collective-permute-start.26
  156.7 3.1 collective-permute-start.27
  157.2 5.4 %collective-permute-start.28 = (bf16[3,192,768]{2,1,0:T(8,128)(2,1)}, bf16[3,192,768]{2,1,0:T(8,128)(2,1)S(1)}, u32[]{:S(2)}, u32[]{:S(2)}) collective-permute-start(bf16[3,192,768]{2,1,0:T(8,128)(2,1)} %collective-permute-done.25.refs_8_), channel_id=1, source_target_pairs={{0,1},{1,0},{2,3},{3,2},{4,5},{5,4},{6,7},{7,6},{8,9},{9,8},{10,11... | collective-permute-start | bytes 2654216 | tf_op jit(solution)/shard_map/ppermute | solution.py:25
  161.4 34.6 %collective-permute-start.29 = (bf16[4,2,96,768]{3,2,1,0:T(8,128)(2,1)S(1)}, bf16[4,2,96,768]{3,2,1,0:T(8,128)(2,1)S(1)}, u32[]{:S(2)}, u32[]{:S(2)}) collective-permute-start(bf16[4,2,96,768]{3,2,1,0:T(8,128)(2,1)S(1)} %fusion.3), channel_id=1, source_target_pairs={{0,4},{4,0},{8,12},{12,8},{16,20},{20,16},{24,28},{28,24},{1,5},{5... | collective-permute-start | bytes 3538952 | tf_op jit(solution)/shard_map/ppermute | solution.py:25
  195.4 2.1 collective-permute-start.30
  195.4 2.8 collective-permute-start.31
  198.6 28.1 %collective-permute-start.32 = (bf16[4,2,96,768]{3,2,1,0:T(8,128)(2,1)S(1)}, bf16[4,2,96,768]{3,2,1,0:T(8,128)(2,1)S(1)}, u32[]{:S(2)}, u32[]{:S(2)}) collective-permute-start(bf16[4,2,96,768]{3,2,1,0:T(8,128)(2,1)S(1)} %fusion.2), channel_id=1, source_target_pairs={{0,4},{4,0},{8,12},{12,8},{16,20},{20,16},{24,28},{28,24},{1,5},{5... | collective-permute-start | bytes 3538952 | tf_op jit(solution)/shard_map/ppermute | solution.py:25
  199.5 27.2 %collective-permute-start.33 = (bf16[4,2,96,768]{3,2,1,0:T(8,128)(2,1)S(1)}, bf16[4,2,96,768]{3,2,1,0:T(8,128)(2,1)S(1)}, u32[]{:S(2)}, u32[]{:S(2)}) collective-permute-start(bf16[4,2,96,768]{3,2,1,0:T(8,128)(2,1)S(1)} %copy-done.28), channel_id=1, source_target_pairs={{0,1},{1,0},{2,3},{3,2},{4,5},{5,4},{6,7},{7,6},{8,9},{9,8},{10,11... | collective-permute-start | bytes 3538952 | tf_op jit(solution)/shard_map/ppermute | solution.py:25
  199.5 27.7 %collective-permute-start.34 = (bf16[4,2,96,768]{3,2,1,0:T(8,128)(2,1)}, bf16[4,2,96,768]{3,2,1,0:T(8,128)(2,1)S(1)}, u32[]{:S(2)}, u32[]{:S(2)}) collective-permute-start(bf16[4,2,96,768]{3,2,1,0:T(8,128)(2,1)} %get-tuple-element.205), channel_id=1, source_target_pairs={{0,1},{1,0},{2,3},{3,2},{4,5},{5,4},{6,7},{7,6},{8,9},{9,8},{10,11... | collective-permute-start | bytes 3538952 | tf_op jit(solution)/shard_map/ppermute | solution.py:25
  230.0 63.2 %all-to-all-start.1 = ((bf16[4,384,768]{2,1,0:T(8,128)(2,1)}), bf16[4,384,768]{2,1,0:T(8,128)(2,1)S(1)}, u32[]{:S(2)}, u32[]{:S(2)}) async-start(bf16[4,384,768]{2,1,0:T(8,128)(2,1)} %pad_maximum_fusion), calls=%async_computation.1 | async-start | bytes 4718592 | tf_op jit(solution)/shard_map/all_to_all | solution.py:491
  238.0 13.7 %collective-permute-start.35 = (bf16[8,64,768]{2,1,0:T(8,128)(2,1)}, bf16[8,64,768]{2,1,0:T(8,128)(2,1)S(1)}, u32[]{:S(2)}, u32[]{:S(2)}) collective-permute-start(bf16[8,64,768]{2,1,0:T(8,128)(2,1)} %get-tuple-element.214), channel_id=1, source_target_pairs={{0,1},{1,0},{2,3},{3,2},{4,5},{5,4},{6,7},{7,6},{8,9},{9,8},{10,11... | collective-permute-start | bytes 2359304 | tf_op jit(solution)/shard_map/ppermute | solution.py:25
  238.0 20.2 %collective-permute-start.36 = (bf16[8,64,768]{2,1,0:T(8,128)(2,1)}, bf16[8,64,768]{2,1,0:T(8,128)(2,1)S(1)}, u32[]{:S(2)}, u32[]{:S(2)}) collective-permute-start(bf16[8,64,768]{2,1,0:T(8,128)(2,1)} %get-tuple-element.215), channel_id=1, source_target_pairs={{0,2},{1,3},{2,0},{3,1},{4,6},{5,7},{6,4},{7,5},{8,10},{9,11},{10,... | collective-permute-start | bytes 2359304 | tf_op jit(solution)/shard_map/ppermute | solution.py:25
  258.2 2.2 collective-permute-start.37
  258.2 3.1 collective-permute-start.38
  258.7 19.7 %collective-permute-start.39 = (bf16[8,64,768]{2,1,0:T(8,128)(2,1)S(1)}, bf16[8,64,768]{2,1,0:T(8,128)(2,1)S(1)}, u32[]{:S(2)}, u32[]{:S(2)}) collective-permute-start(bf16[8,64,768]{2,1,0:T(8,128)(2,1)S(1)} %copy-done.29), channel_id=1, source_target_pairs={{0,3},{1,2},{2,1},{3,0},{4,7},{5,6},{6,5},{7,4},{8,11},{9,10},{10,... | collective-permute-start | bytes 2359304 | tf_op jit(solution)/shard_map/ppermute | solution.py:25
  259.7 25.2 %collective-permute-start.48 = (bf16[4,2,96,768]{3,2,1,0:T(8,128)(2,1)}, bf16[4,2,96,768]{3,2,1,0:T(8,128)(2,1)S(1)}, u32[]{:S(2)}, u32[]{:S(2)}) collective-permute-start(bf16[4,2,96,768]{3,2,1,0:T(8,128)(2,1)} %get-tuple-element.247), channel_id=1, source_target_pairs={{0,1},{1,0},{2,3},{3,2},{4,5},{5,4},{6,7},{7,6},{8,9},{9,8},{10,11... | collective-permute-start | bytes 3538952 | tf_op jit(solution)/shard_map/ppermute | solution.py:25
  262.8 28.9 %collective-permute-start.49 = (bf16[4,2,96,768]{3,2,1,0:T(8,128)(2,1)S(1)}, bf16[4,2,96,768]{3,2,1,0:T(8,128)(2,1)S(1)}, u32[]{:S(2)}, u32[]{:S(2)}) collective-permute-start(bf16[4,2,96,768]{3,2,1,0:T(8,128)(2,1)S(1)} %fusion.1), channel_id=1, source_target_pairs={{0,4},{4,0},{8,12},{12,8},{16,20},{20,16},{24,28},{28,24},{1,5},{5... | collective-permute-start | bytes 3538952 | tf_op jit(solution)/shard_map/ppermute | solution.py:25
  278.4 2.2 collective-permute-start.40
  278.7 2.8 collective-permute-start.41
  284.1 32.6 %collective-permute-start.46 = (bf16[4,2,96,768]{3,2,1,0:T(8,128)(2,1)}, bf16[4,2,96,768]{3,2,1,0:T(8,128)(2,1)}, u32[]{:S(2)}, u32[]{:S(2)}) collective-permute-start(bf16[4,2,96,768]{3,2,1,0:T(8,128)(2,1)} %fusion), channel_id=1, source_target_pairs={{0,4},{4,0},{8,12},{12,8},{16,20},{20,16},{24,28},{28,24},{1,5},{5... | collective-permute-start | bytes 3538952 | tf_op jit(solution)/shard_map/ppermute | solution.py:25
  293.2 32.3 %all-to-all-start.3 = ((bf16[4,192,768]{2,1,0:T(8,128)(2,1)}), bf16[4,192,768]{2,1,0:T(8,128)(2,1)S(1)}, u32[]{:S(2)}, u32[]{:S(2)}) async-start(bf16[4,192,768]{2,1,0:T(8,128)(2,1)} %bitcast.72), calls=%async_computation.3 | async-start | bytes 2359296 | tf_op jit(solution)/shard_map/all_to_all | solution.py:491
  298.2 18.5 %collective-permute-start.43 = (bf16[4,2,96,768]{3,2,1,0:T(8,128)(2,1)}, bf16[4,2,96,768]{3,2,1,0:T(8,128)(2,1)}, u32[]{:S(2)}, u32[]{:S(2)}) collective-permute-start(bf16[4,2,96,768]{3,2,1,0:T(8,128)(2,1)} %get-tuple-element.238), channel_id=1, source_target_pairs={{0,1},{1,0},{2,3},{3,2},{4,5},{5,4},{6,7},{7,6},{8,9},{9,8},{10,11... | collective-permute-start | bytes 3538952 | tf_op jit(solution)/shard_map/ppermute | solution.py:25
  299.6 17.2 %collective-permute-start.42 = (bf16[384,768]{1,0:T(8,128)(2,1)}, bf16[384,768]{1,0:T(8,128)(2,1)}, u32[]{:S(2)}, u32[]{:S(2)}) collective-permute-start(bf16[384,768]{1,0:T(8,128)(2,1)} %reduce_sum.36), channel_id=1, source_target_pairs={{0,2},{1,3},{2,0},{3,1},{4,6},{5,7},{6,4},{7,5},{8,10},{9,11},{10,... | collective-permute-start | bytes 1769480 | tf_op jit(solution)/shard_map/ppermute | solution.py:25
  303.1 13.6 %collective-permute-start.45 = (bf16[16,768]{1,0:T(8,128)(2,1)S(1)}, bf16[16,768]{1,0:T(8,128)(2,1)S(1)}, u32[]{:S(2)}, u32[]{:S(2)}) collective-permute-start(bf16[16,768]{1,0:T(8,128)(2,1)S(1)} %add_convert_fusion.5), channel_id=1, source_target_pairs={{0,4},{4,0},{8,12},{12,8},{16,20},{20,16},{24,28},{28,24},{1,5},{5... | collective-permute-start | bytes 73736 | tf_op jit(solution)/shard_map/ppermute | solution.py:25
  320.3 15.5 %collective-permute-start.51 = (bf16[8,32,768]{2,1,0:T(8,128)(2,1)}, bf16[8,32,768]{2,1,0:T(8,128)(2,1)}, u32[]{:S(2)}, u32[]{:S(2)}) collective-permute-start(bf16[8,32,768]{2,1,0:T(8,128)(2,1)} %get-tuple-element.250.refs_4_), channel_id=1, source_target_pairs={{0,2},{1,3},{2,0},{3,1},{4,6},{5,7},{6,4},{7,5},{8,10},{9,11},{10,... | collective-permute-start | bytes 1179656 | tf_op jit(solution)/shard_map/ppermute | solution.py:25
  321.7 21.7 %collective-permute-start.52 = (bf16[384,768]{1,0:T(8,128)(2,1)S(1)}, bf16[384,768]{1,0:T(8,128)(2,1)}, u32[]{:S(2)}, u32[]{:S(2)}) collective-permute-start(bf16[384,768]{1,0:T(8,128)(2,1)S(1)} %copy-done.5), channel_id=1, source_target_pairs={{0,1},{1,0},{2,3},{3,2},{4,5},{5,4},{6,7},{7,6},{8,9},{9,8},{10,11... | collective-permute-start | bytes 1769480 | tf_op jit(solution)/shard_map/ppermute | solution.py:25
  321.7 21.7 %collective-permute-start.53 = (bf16[384,768]{1,0:T(8,128)(2,1)}, bf16[384,768]{1,0:T(8,128)(2,1)}, u32[]{:S(2)}, u32[]{:S(2)}) collective-permute-start(bf16[384,768]{1,0:T(8,128)(2,1)} %collective-permute-done.42), channel_id=1, source_target_pairs={{0,1},{1,0},{2,3},{3,2},{4,5},{5,4},{6,7},{7,6},{8,9},{9,8},{10,11... | collective-permute-start | bytes 1769480 | tf_op jit(solution)/shard_map/ppermute | solution.py:25
  325.5 33.9 %all-to-all-start.2 = ((bf16[4,208,768]{2,1,0:T(8,128)(2,1)}), bf16[4,208,768]{2,1,0:T(8,128)(2,1)S(1)}, u32[]{:S(2)}, u32[]{:S(2)}) async-start(bf16[4,208,768]{2,1,0:T(8,128)(2,1)} %pad_maximum_fusion.2), calls=%async_computation.2 | async-start | bytes 2555904 | tf_op jit(solution)/shard_map/all_to_all | solution.py:491
  329.2 12.2 %collective-permute-start.47 = (bf16[8,32,768]{2,1,0:T(8,128)(2,1)S(1)}, bf16[8,32,768]{2,1,0:T(8,128)(2,1)}, u32[]{:S(2)}, u32[]{:S(2)}) collective-permute-start(bf16[8,32,768]{2,1,0:T(8,128)(2,1)S(1)} %copy-done.6), channel_id=1, source_target_pairs={{0,2},{1,3},{2,0},{3,1},{4,6},{5,7},{6,4},{7,5},{8,10},{9,11},{10,... | collective-permute-start | bytes 1179656 | tf_op jit(solution)/shard_map/ppermute | solution.py:25
  331.6 15.9 %collective-permute-start.50 = (bf16[192,768]{1,0:T(8,128)(2,1)}, bf16[192,768]{1,0:T(8,128)(2,1)S(1)}, u32[]{:S(2)}, u32[]{:S(2)}) collective-permute-start(bf16[192,768]{1,0:T(8,128)(2,1)} %reduce_sum.37), channel_id=1, source_target_pairs={{0,2},{1,3},{2,0},{3,1},{4,6},{5,7},{6,4},{7,5},{8,10},{9,11},{10,... | collective-permute-start | bytes 884744 | tf_op jit(solution)/shard_map/ppermute | solution.py:25
  359.6 2.5 collective-permute-start.59
  359.7 2.4 collective-permute-start.60
  360.2 3.9 %collective-permute-start.55 = (bf16[2,8,32,768]{3,2,1,0:T(8,128)(2,1)S(1)}, bf16[2,8,32,768]{3,2,1,0:T(8,128)(2,1)}, u32[]{:S(2)}, u32[]{:S(2)}) collective-permute-start(bf16[2,8,32,768]{3,2,1,0:T(8,128)(2,1)S(1)} %pad_maximum_fusion.9), channel_id=1, source_target_pairs={{0,1},{1,0},{2,3},{3,2},{4,5},{5,4},{6,7},{7,6},{8,9},{9,8},{10,11... | collective-permute-start | bytes 2359304 | tf_op jit(solution)/shard_map/ppermute | solution.py:25
  360.3 4.0 %collective-permute-start.54 = (bf16[2,8,32,768]{3,2,1,0:T(8,128)(2,1)}, bf16[2,8,32,768]{3,2,1,0:T(8,128)(2,1)}, u32[]{:S(2)}, u32[]{:S(2)}) collective-permute-start(bf16[2,8,32,768]{3,2,1,0:T(8,128)(2,1)} %pad_maximum_fusion.8), channel_id=1, source_target_pairs={{0,1},{1,0},{2,3},{3,2},{4,5},{5,4},{6,7},{7,6},{8,9},{9,8},{10,11... | collective-permute-start | bytes 2359304 | tf_op jit(solution)/shard_map/ppermute | solution.py:25
  360.7 9.5 %collective-permute-start.56 = (bf16[208,768]{1,0:T(8,128)(2,1)S(1)}, bf16[208,768]{1,0:T(8,128)(2,1)S(1)}, u32[]{:S(2)}, u32[]{:S(2)}) collective-permute-start(bf16[208,768]{1,0:T(8,128)(2,1)S(1)} %reduce_sum.38), channel_id=1, source_target_pairs={{0,2},{1,3},{2,0},{3,1},{4,6},{5,7},{6,4},{7,5},{8,10},{9,11},{10,... | collective-permute-start | bytes 958472 | tf_op jit(solution)/shard_map/ppermute | solution.py:25
  370.3 2.0 collective-permute-start.57
  370.4 2.0 collective-permute-start.58
  (33 other events, 293.3 us)

commit v4 on v3

--- a/solution.py
+++ b/solution.py
@@ -610,14 +610,19 @@
 
 
 def place_memory(where, pieces, out, scratch, sems):
-    examples = pieces[0].shape[0]
+    examples = scratch.shape[1]
     copies = Copies(sems)
-    loads = [copies.start(piece, scratch.at[d]) for d, piece in enumerate(pieces)]
+    loads = []
+    for d, parts in enumerate(pieces):
+        start = 0
+        for part in parts:
+            held = scratch.at[d, pl.ds(start, part.shape[0])]
+            loads.append((copies.start(part, held), held, (where[3] ^ d) * examples + start))
+            start += part.shape[0]
     stores = []
-    for d, load in enumerate(loads):
+    for load, held, place in loads:
         load.wait()
-        target = out.at[pl.ds((where[3] ^ d) * examples, examples)]
-        stores.append(copies.start(scratch.at[d], target))
+        stores.append(copies.start(held, out.at[pl.ds(place, held.shape[0])]))
     wait_all(stores)
 
 
@@ -753,6 +758,10 @@
         [square, own_rows, scratch(fsdp, 16, 128)],
         1 + fsdp + blocks,
     )
+    small = [after(piece, x1)[:, 2 * part + 7 : 2 * part + 11, :part] for piece in self_weights[0]]
+    order = jnp.arange(fsdp) ^ f
+    bias_in = jnp.take(jnp.concatenate(small), order % fast * slow + order // fast, axis=0)
+    bias_in = bias_in.astype(F32).reshape(1, inner)
     cross_gather.far = [after(piece, x1, *in_gather.came) for piece in cross_gather.far]
     cross_weights = Gather.refs(cross_gather.whole())
     in_gather.send_fast(*cross_gather.far)
@@ -762,7 +771,7 @@
     turned_spec = pl.BlockSpec((width, per * total), lambda e: (0, e))
     x2, a2, q2, kv, p2, o2, turned = run(
         cross_forward,
-        [(SMEM, where), (SMEM, counts), (VMEM, x1), (VMEM, vec)]
+        [(SMEM, where), (SMEM, counts), (VMEM, after(x1, bias_in)), (VMEM, vec)]
         + [slots_of_example(all_memory), cross_weights],
         [
             flat(wide, F32),
@@ -777,10 +786,6 @@
         blocks,
         (examples // per,),
     )
-    small = [after(piece, x1)[:, 2 * part + 7 : 2 * part + 11, :part] for piece in self_weights[0]]
-    order = jnp.arange(fsdp) ^ f
-    bias_in = jnp.take(jnp.concatenate(small), order % fast * slow + order // fast, axis=0)
-    bias_in = bias_in.astype(F32).reshape(1, inner)
     in_gather.far = [after(piece, x2, *out_gather.came) for piece in in_gather.far]
     in_weights = Gather.refs(in_gather.whole())
     out_gather.send_fast(*in_gather.far)
@@ -842,7 +847,11 @@
     dense_total = [one.add_fast(*in_scatter.came) for one in (out_scatter, in_scatter)]
     dense_total = jnp.concatenate(dense_total, axis=1)
     dense_came = over_slow(dense_total, slow, fast)
-    mem_pieces = grad_memory[:1] + [swap(grad_memory[d], "mem", d) for d in range(1, mem)]
+    cut = examples // 2
+    mem_pieces = [grad_memory[:1]]
+    for d in range(1, mem):
+        parts = [grad_memory[d][:cut], grad_memory[d][cut:]] if d == 2 else [grad_memory[d]]
+        mem_pieces.append([swap(part, "mem", d) for part in parts])
     grads = run(
         cross_grads,
         [(SMEM, where), (VMEM, after(gx2, dense_total)), (VMEM, a2), (VMEM, o2), (VMEM, dq2)]
@@ -852,7 +861,7 @@
         blocks,
         (2,),
     )
-    cross_scatter = scatter(grads, *mem_pieces[1:3])
+    cross_scatter = scatter(grads, *mem_pieces[1], *mem_pieces[2][:1])
     cross_sum = cross_scatter.add_cores()
     cross_scatter.send_fast()
     gx1 = after(gx1, *cross_sum)
@@ -865,7 +874,7 @@
         [square, own_rows, square, scratch(rows, 3 * width), scratch(*wide)],
         1 + blocks,
     )
-    self_scatter = scatter(grads, *mem_pieces[3:4], vectors=vecs_self)
+    self_scatter = scatter(grads, *mem_pieces[3], vectors=vecs_self)
     self_sum = self_scatter.add_cores()
     self_scatter.send_fast()
     cross_scatter.add_fast(*self_sum)
@@ -878,13 +887,13 @@
     suffix_rows = spread_across(after(suffix_part, self_total), mem)
     y_rows = spread_across(after(y, self_total), mem)
     dense_sum.swap_cores(self_total)
-    mem_pieces = [after(value, self_total) for value in mem_pieces]
+    mem_pieces = [[after(part, self_total) for part in parts] for parts in mem_pieces]
     (memory_grad,) = run(
         place_memory,
-        [(SMEM, where), [(ANY, value) for value in mem_pieces]],
+        [(SMEM, where), [[(ANY, part) for part in parts] for parts in mem_pieces]],
         [(ANY, shape_of(memory.shape, BF))],
         [scratch(mem, examples, slots, width)],
-        2 * mem,
+        2 * mem + 2,
     )
     (out_low, in_low, out_high, in_high), _ = dense_sum.combine(c)
     grad_in = jnp.concatenate([in_low[:part], in_low[part:], in_high[:part], in_high[part:]], axis=1)

time: 378 us -> 376 us (level)
    ppermute x61 -> x62, waiting for transfers between devices: 113 us -> 106 us  [swap(): return lax.ppermute(value, axis, [(i, i ^ distance) for i in range(size)])]
    all_to_all x3, waiting for transfers between devices: 15 us -> 20.2 us  [over_slow(): lax.all_to_all(value, 'fsdp', 0, 0, axis_index_groups=groups, tiled=True)]
    ppermute x61 -> x62, starting transfers between devices: 54.5 us -> 54.4 us  [swap(): return lax.ppermute(value, axis, [(i, i ^ distance) for i in range(size)])]
  transfers between devices with their start and end apart: 65 -> 66, of which waited for: 29 -> 32; matrix products, arithmetic and copies ran while one was open for 10% -> 11% of each run, Pallas kernels for 31% -> 31%
where the time goes in v4:
time: 376 us; the launch traced here: 372 us
  waiting for transfers between devices  126 us (34%)
  Pallas kernels  116 us (31%)
  starting transfers between devices  74.2 us (20%)
  other arithmetic  37.6 us (10%)
  local copies, waits for them, and re-layouts  16.4 us (4%)
    pallas_call x10, Pallas kernels, run(): pl.pallas_call(body, grid=grid, in_specs=[spec for spec, _ in flat_in], o...  116 us
    ppermute x62, waiting for transfers between devices, swap(): return lax.ppermute(value, axis, [(i, i ^ distance) for i in range(size)])  106 us
    ppermute x62, starting transfers between devices, swap(): return lax.ppermute(value, axis, [(i, i ^ distance) for i in range(size)])  54.4 us
    all_to_all x3, waiting for transfers between devices, over_slow(): lax.all_to_all(value, 'fsdp', 0, 0, axis_index_groups=groups, tiled=True)  20.2 us
    all_to_all x3, starting transfers between devices, over_slow(): lax.all_to_all(value, 'fsdp', 0, 0, axis_index_groups=groups, tiled=True)  15.6 us
  transfers between devices with their start and end apart: 66, of which 32 were waited for; matrix products, arithmetic and copies ran while one was open for 11% of the time, Pallas kernels for 31%

profile of v4, /device:TPU:0, one launch (start us, length us, event | category | flops | bytes accessed | tf_op | source)
XLA Modules:
  0.0 372.5 jit_solution(7898198588405891887)
XLA Ops:
  3.6 4.2 %all-to-all-start = ((bf16[4,8,64,768]{3,2,1,0:T(8,128)(2,1)}), bf16[4,8,64,768]{3,2,1,0:T(8,128)(2,1)S(1)}, u32[]{:S(2)}, u32[]{:S(2)}) async-start(bf16[4,8,64,768]{3,2,1,0:T(8,128)(2,1)} %bitcast.75), calls=%async_computation | async-start | bytes 6291456 | tf_op jit(solution)/shard_map/all_to_all | solution.py:702
  7.8 2.6 collective-permute-start
  10.4 2.6 collective-permute-start.1
  13.0 1.8 slice_select_fusion.refs_9_
  14.8 1.7 collective-permute-start.3
  16.5 7.3 %collective-permute-done.3.refs_10_ = bf16[192,768]{1,0:T(8,128)(2,1)S(1)} collective-permute-done((bf16[192,768]{1,0:T(8,128)(2,1)}, bf16[192,768]{1,0:T(8,128)(2,1)S(1)}, u32[]{:S(2)}, u32[]{:S(2)}) %collective-permute-start.3) | collective-permute-done | bytes 294944 | tf_op jit(solution)/shard_map/ppermute | solution.py:25
  24.9 10.5 %collective-permute-done.1 = bf16[208,768]{1,0:T(8,128)(2,1)S(1)} collective-permute-done((bf16[208,768]{1,0:T(8,128)(2,1)S(1)}, bf16[208,768]{1,0:T(8,128)(2,1)S(1)}, u32[]{:S(2)}, u32[]{:S(2)}) %collective-permute-start.1) | collective-permute-done | bytes 319520 | tf_op jit(solution)/shard_map/ppermute | solution.py:25
  36.7 1.6 collective-permute-start.4
  38.5 6.7 %collective-permute-start.5 = (bf16[192,768]{1,0:T(8,128)(2,1)S(1)}, bf16[192,768]{1,0:T(8,128)(2,1)S(1)}, u32[]{:S(2)}, u32[]{:S(2)}) collective-permute-start(bf16[192,768]{1,0:T(8,128)(2,1)S(1)} %get-tuple-element.158), channel_id=1, source_target_pairs={{0,8},{4,12},{8,0},{12,4},{16,24},{20,28},{24,16},{28,20},{1,9},{5... | collective-permute-start | bytes 884744 | tf_op jit(solution)/shard_map/ppermute | solution.py:25
  46.3 1.4 collective-permute-start.7
  47.7 8.9 %collective-permute-done.5 = bf16[192,768]{1,0:T(8,128)(2,1)S(1)} collective-permute-done((bf16[192,768]{1,0:T(8,128)(2,1)S(1)}, bf16[192,768]{1,0:T(8,128)(2,1)S(1)}, u32[]{:S(2)}, u32[]{:S(2)}) %collective-permute-start.5) | collective-permute-done | bytes 294944 | tf_op jit(solution)/shard_map/ppermute | solution.py:25
  56.6 12.1 %collective-permute-done.6 = bf16[192,768]{1,0:T(8,128)(2,1)S(1)} collective-permute-done((bf16[192,768]{1,0:T(8,128)(2,1)S(1)}, bf16[192,768]{1,0:T(8,128)(2,1)S(1)}, u32[]{:S(2)}, u32[]{:S(2)}) %collective-permute-start.6) | collective-permute-done | bytes 294944 | tf_op jit(solution)/shard_map/ppermute | solution.py:25
  70.2 3.3 pad_maximum_fusion.3.refs_5_.refs_7_
  74.5 4.2 %collective-permute-start.11 = (bf16[192,768]{1,0:T(8,128)(2,1)S(1)}, bf16[192,768]{1,0:T(8,128)(2,1)}, u32[]{:S(2)}, u32[]{:S(2)}) collective-permute-start(bf16[192,768]{1,0:T(8,128)(2,1)S(1)} %get-tuple-element.166), channel_id=1, source_target_pairs={{0,8},{4,12},{8,0},{12,4},{16,24},{20,28},{24,16},{28,20},{1,9},{5... | collective-permute-start | bytes 884744 | tf_op jit(solution)/shard_map/ppermute | solution.py:25
  79.7 1.5 collective-permute-start.13
  81.8 7.8 %shard_map.373 = (f32[256,768]{1,0:T(8,128)}, bf16[256,768]{1,0:T(8,128)(2,1)}, bf16[256,2304]{1,0:T(8,128)(2,1)}, bf16[6,512,128]{2,1,0:T(8,128)(2,1)}, bf16[256,768]{1,0:T(8,128)(2,1)}, /*index=5*/f32[16,768]{1,0:T(8,128)}) custom-call(s32[4]{0:T(128)} %pad_add_fusion.1.refs_0_, bf16[32,32,768]{2,1,0:T(8,128)(2,1)} %refs_1_.5, ...), custom_call_target="tpu_custom_call" | custom-call | tf_op jit(solution)/shard_map/pallas_call | solution.py:470
  90.6 11.7 %collective-permute-done.12 = bf16[192,768]{1,0:T(8,128)(2,1)} collective-permute-done((bf16[192,768]{1,0:T(8,128)(2,1)S(1)}, bf16[192,768]{1,0:T(8,128)(2,1)}, u32[]{:S(2)}, u32[]{:S(2)}) %collective-permute-start.12) | collective-permute-done | bytes 294944 | tf_op jit(solution)/shard_map/ppermute | solution.py:25
  105.0 4.9 %collective-permute-start.16 = (bf16[192,768]{1,0:T(8,128)(2,1)}, bf16[192,768]{1,0:T(8,128)(2,1)}, u32[]{:S(2)}, u32[]{:S(2)}) collective-permute-start(bf16[192,768]{1,0:T(8,128)(2,1)} %slice_select_fusion.refs_9_), channel_id=1, source_target_pairs={{0,8},{4,12},{8,0},{12,4},{16,24},{20,28},{24,16},{28,20},{1,9},{5... | collective-permute-start | bytes 884744 | tf_op jit(solution)/shard_map/ppermute | solution.py:25
  112.5 1.5 collective-permute-start.19
  117.7 15.5 %shard_map.374 = (f32[256,768]{1,0:T(8,128)}, bf16[256,768]{1,0:T(8,128)(2,1)}, bf16[256,768]{1,0:T(8,128)(2,1)}, bf16[8,256,1536]{2,1,0:T(8,128)(2,1)}, bf16[8,...) custom-call(s32[4]{0:T(128)} %pad_add_fusion.1.refs_0_, s32[32]{0:T(128)} %refs_1_.4, ...), custom_call_target="tpu_custom_call" | custom-call | tf_op jit(solution)/shard_map/pallas_call | solution.py:470
  133.8 1.6 pad_maximum_fusion.7.refs_7_
  136.9 1.5 collective-permute-done.22.refs_14_
  138.5 1.7 collective-permute-done.21.refs_13_
  142.3 13.6 %shard_map.375 = (bf16[256,768]{1,0:T(8,128)(2,1)}, bf16[256,3072]{1,0:T(8,128)(2,1)}, bf16[256,3072]{1,0:T(8,128)(2,1)}, bf16[4,2,96,768]{3,2,1,0:T(8,128)(2,1)...) custom-call(s32[4]{0:T(128)} %pad_add_fusion.1.refs_0_, ...), custom_call_target="tpu_custom_call" | custom-call | tf_op jit(solution)/shard_map/pallas_call | solution.py:470
  156.0 1.5 collective-permute-done.25.refs_8_
  158.0 1.7 collective-permute-done.26
  159.7 1.7 collective-permute-done.27
  161.4 1.5 fusion.3
  163.0 1.3 collective-permute-start.29
  165.2 11.8 %shard_map.376 = (bf16[8,32,768]{2,1,0:T(8,128)(2,1)}, bf16[256,3072]{1,0:T(8,128)(2,1)}, f32[1,768]{1,0:T(1,128)}, f32[1,3072]{1,0:T(1,128)}, bf16[4,2,96,768]{...) custom-call(s32[4]{0:T(128)} %pad_add_fusion.1.refs_0_, ...), custom_call_target="tpu_custom_call" | custom-call | tf_op jit(solution)/shard_map/pallas_call | solution.py:470
  177.1 18.7 %shard_map.377 = (f32[256,768]{1,0:T(8,128)}, f32[2,768]{1,0:T(2,128)}) custom-call(s32[4]{0:T(128)} %pad_add_fusion.1.refs_0_, f32[256,768]{1,0:T(8,128)} %get-tuple-element.183.refs_1_, f32[16,768]{1,0:T(8,128)} %get-tuple-element.157.refs_3_.refs_2_, bf16[256,3072]{1,0:T(8,128)(2,1)} %get-tuple-element.187.refs_3_, bf16[32,32,768]{2,1,0:T(8,128)(2,1)} %refs_4_.3, ...), custom_call_target="tpu_custom_call" | custom-call | tf_op jit(solution)/shard_map/pallas_call | solution.py:470
  196.4 1.5 collective-permute-done.30
  200.4 17.7 %shard_map.378 = (f32[256,768]{1,0:T(8,128)}, f32[2,768]{1,0:T(2,128)}, bf16[8,256,1536]{2,1,0:T(8,128)(2,1)}, bf16[256,768]{1,0:T(8,128)(2,1)}, bf16[8,64,768]{...) custom-call(s32[4]{0:T(128)} %pad_add_fusion.1.refs_0_, ...), custom_call_target="tpu_custom_call" | custom-call | bytes 60000000 | tf_op jit(solution)/shard_map/pallas_call | solution.py:470
  218.2 8.9 %collective-permute-done.32 = bf16[4,2,96,768]{3,2,1,0:T(8,128)(2,1)S(1)} collective-permute-done((bf16[4,2,96,768]{3,2,1,0:T(8,128)(2,1)S(1)}, bf16[4,2,96,768]{3,2,1,0:T(8,128)(2,1)S(1)}, u32[]{:S(2)}, u32[]{:S(2)}) %collective-permute-start.32) | collective-permute-done | bytes 1179680 | tf_op jit(solution)/shard_map/ppermute | solution.py:25
  228.9 1.6 pad_maximum_fusion
  230.4 8.3 %all-to-all-start.1 = ((bf16[4,384,768]{2,1,0:T(8,128)(2,1)}), bf16[4,384,768]{2,1,0:T(8,128)(2,1)S(1)}, u32[]{:S(2)}, u32[]{:S(2)}) async-start(bf16[4,384,768]{2,1,0:T(8,128)(2,1)} %pad_maximum_fusion), calls=%async_computation.1 | async-start | bytes 4718592 | tf_op jit(solution)/shard_map/all_to_all | solution.py:491
  239.6 1.4 collective-permute-start.36
  240.9 12.3 %shard_map.379 = (bf16[4,2,96,768]{3,2,1,0:T(8,128)(2,1)}, bf16[1,4,2,96,768]{4,3,2,1,0:T(8,128)(2,1)}, bf16[4,2,96,768]{3,2,1,0:T(8,128)(2,1)}, bf16[2,2,96,768]{3,2,1,0:T(8,128)(2,1)}, bf16[2,2,96,768]{3,2,1,0:T(8,128)(2,1)}) custom-call(s32[4]{0:T(128)} %pad_add_fusion.1.refs_0_, f32[256,768]{1,0:T(8,128)} %get-tuple-element.209.refs_3_.refs_1_, ...), custom_call_target="tpu_custom_call" | custom-call | tf_op jit(solution)/shard_map/pallas_call | solution.py:470
  256.4 1.5 fusion.1
  258.8 11.7 %shard_map.380 = (bf16[8,32,768]{2,1,0:T(8,128)(2,1)}, bf16[16,768]{1,0:T(8,128)(2,1)}, bf16[4,2,96,768]{3,2,1,0:T(8,128)(2,1)}, bf16[1,4,2,96,768]{4,3,2,1,0:T(...) custom-call(s32[4]{0:T(128)} %pad_add_fusion.1.refs_0_, ...), custom_call_target="tpu_custom_call" | custom-call | tf_op jit(solution)/shard_map/pallas_call | solution.py:470
  270.5 2.9 collective-permute-done.39.refs_5_
  273.9 1.8 collective-permute-done.40
  276.5 2.7 fusion
  280.0 6.8 %collective-permute-done.49 = bf16[4,2,96,768]{3,2,1,0:T(8,128)(2,1)S(1)} collective-permute-done((bf16[4,2,96,768]{3,2,1,0:T(8,128)(2,1)S(1)}, bf16[4,2,96,768]{3,2,1,0:T(8,128)(2,1)S(1)}, u32[]{:S(2)}, u32[]{:S(2)}) %collective-permute-start.49) | collective-permute-done | bytes 1179680 | tf_op jit(solution)/shard_map/ppermute | solution.py:25
  286.9 1.5 add_convert_fusion
  288.3 3.7 all-to-all-done.1
  292.0 3.7 %all-to-all-start.3 = ((bf16[4,192,768]{2,1,0:T(8,128)(2,1)}), bf16[4,192,768]{2,1,0:T(8,128)(2,1)S(1)}, u32[]{:S(2)}, u32[]{:S(2)}) async-start(bf16[4,192,768]{2,1,0:T(8,128)(2,1)} %bitcast.72), calls=%async_computation.3 | async-start | bytes 2359296 | tf_op jit(solution)/shard_map/all_to_all | solution.py:491
  295.9 1.3 reduce_sum.36
  297.2 1.4 collective-permute-start.42
  302.2 9.8 %collective-permute-done.45 = bf16[16,768]{1,0:T(8,128)(2,1)S(1)} collective-permute-done((bf16[16,768]{1,0:T(8,128)(2,1)S(1)}, bf16[16,768]{1,0:T(8,128)(2,1)S(1)}, u32[]{:S(2)}, u32[]{:S(2)}) %collective-permute-start.45) | collective-permute-done | bytes 24608 | tf_op jit(solution)/shard_map/ppermute | solution.py:25
  312.0 1.6 collective-permute-done.42
  313.6 2.4 add_convert_fusion.1
  317.2 1.4 collective-permute-start.51
  319.1 4.7 %all-to-all-done.3 = bf16[4,192,768]{2,1,0:T(8,128)(2,1)S(1)} async-done(((bf16[4,192,768]{2,1,0:T(8,128)(2,1)}), bf16[4,192,768]{2,1,0:T(8,128)(2,1)S(1)}, u32[]{:S(2)}, u32[]{:S(2)}) %all-to-all-start.3) | async-done | bytes 1179680 | tf_op jit(solution)/shard_map/all_to_all | solution.py:491
  323.8 3.5 all-to-all-start.2
  327.3 1.5 collective-permute-start.47
  330.4 3.5 shard_map.381
  335.1 4.4 %collective-permute-done.47.refs_2_ = bf16[8,32,768]{2,1,0:T(8,128)(2,1)} collective-permute-done((bf16[8,32,768]{2,1,0:T(8,128)(2,1)S(1)}, bf16[8,32,768]{2,1,0:T(8,128)(2,1)}, u32[]{:S(2)}, u32[]{:S(2)}) %collective-permute-start.47) | collective-permute-done | bytes 393248 | tf_op jit(solution)/shard_map/ppermute | solution.py:25
  339.5 1.9 pad_maximum_fusion.8
  341.5 1.7 fusion.5
  345.6 11.8 %all-to-all-done.2 = bf16[4,208,768]{2,1,0:T(8,128)(2,1)S(1)} async-done(((bf16[4,208,768]{2,1,0:T(8,128)(2,1)}), bf16[4,208,768]{2,1,0:T(8,128)(2,1)S(1)}, u32[]{:S(2)}, u32[]{:S(2)}) %all-to-all-start.2) | async-done | bytes 1277984 | tf_op jit(solution)/shard_map/all_to_all | solution.py:491
  358.8 1.4 collective-permute-start.57
  362.4 3.4 shard_map.382
  365.9 2.5 collective-permute-done.57
  (219 shorter events, 56.2 us)
Async XLA Ops:
  3.6 66.5 %all-to-all-start = ((bf16[4,8,64,768]{3,2,1,0:T(8,128)(2,1)}), bf16[4,8,64,768]{3,2,1,0:T(8,128)(2,1)S(1)}, u32[]{:S(2)}, u32[]{:S(2)}) async-start(bf16[4,8,64,768]{3,2,1,0:T(8,128)(2,1)} %bitcast.75), calls=%async_computation | async-start | bytes 6291456 | tf_op jit(solution)/shard_map/all_to_all | solution.py:702
  7.8 17.1 %collective-permute-start = (bf16[208,768]{1,0:T(8,128)(2,1)S(1)}, bf16[208,768]{1,0:T(8,128)(2,1)S(1)}, u32[]{:S(2)}, u32[]{:S(2)}) collective-permute-start(bf16[208,768]{1,0:T(8,128)(2,1)S(1)} %pad_maximum_fusion.10), channel_id=1, source_target_pairs={{0,8},{4,12},{8,0},{12,4},{16,24},{20,28},{24,16},{28,20},{1,9},{5... | collective-permute-start | bytes 958472 | tf_op jit(solution)/shard_map/ppermute | solution.py:25
  10.4 25.0 %collective-permute-start.1 = (bf16[208,768]{1,0:T(8,128)(2,1)S(1)}, bf16[208,768]{1,0:T(8,128)(2,1)S(1)}, u32[]{:S(2)}, u32[]{:S(2)}) collective-permute-start(bf16[208,768]{1,0:T(8,128)(2,1)S(1)} %pad_maximum_fusion.10), channel_id=1, source_target_pairs={{0,16},{4,20},{8,24},{12,28},{16,0},{20,4},{24,8},{28,12},{1,17},{... | collective-permute-start | bytes 958472 | tf_op jit(solution)/shard_map/ppermute | solution.py:25
  13.0 22.4 %collective-permute-start.2 = (bf16[208,768]{1,0:T(8,128)(2,1)S(1)}, bf16[208,768]{1,0:T(8,128)(2,1)S(1)}, u32[]{:S(2)}, u32[]{:S(2)}) collective-permute-start(bf16[208,768]{1,0:T(8,128)(2,1)S(1)} %pad_maximum_fusion.10), channel_id=1, source_target_pairs={{0,24},{4,28},{8,16},{12,20},{16,8},{20,12},{24,0},{28,4},{1,25},{... | collective-permute-start | bytes 958472 | tf_op jit(solution)/shard_map/ppermute | solution.py:25
  14.8 9.0 %collective-permute-start.3 = (bf16[192,768]{1,0:T(8,128)(2,1)}, bf16[192,768]{1,0:T(8,128)(2,1)S(1)}, u32[]{:S(2)}, u32[]{:S(2)}) collective-permute-start(bf16[192,768]{1,0:T(8,128)(2,1)} %slice_select_fusion.refs_9_), channel_id=1, source_target_pairs={{0,4},{4,0},{8,12},{12,8},{16,20},{20,16},{24,28},{28,24},{1,5},{5... | collective-permute-start | bytes 884744 | tf_op jit(solution)/shard_map/ppermute | solution.py:25
  36.7 33.4 %collective-permute-start.4 = (bf16[4,208,768]{2,1,0:T(8,128)(2,1)}, bf16[4,208,768]{2,1,0:T(8,128)(2,1)}, u32[]{:S(2)}, u32[]{:S(2)}) collective-permute-start(bf16[4,208,768]{2,1,0:T(8,128)(2,1)} %pad_maximum_fusion.1.refs_2_.refs_12_), channel_id=1, source_target_pairs={{0,4},{4,0},{8,12},{12,8},{16,20},{20,16},{24,28},{28,24},{1,5},{5... | collective-permute-start | bytes 3833864 | tf_op jit(solution)/shard_map/ppermute | solution.py:25
  38.5 18.0 %collective-permute-start.5 = (bf16[192,768]{1,0:T(8,128)(2,1)S(1)}, bf16[192,768]{1,0:T(8,128)(2,1)S(1)}, u32[]{:S(2)}, u32[]{:S(2)}) collective-permute-start(bf16[192,768]{1,0:T(8,128)(2,1)S(1)} %get-tuple-element.158), channel_id=1, source_target_pairs={{0,8},{4,12},{8,0},{12,4},{16,24},{20,28},{24,16},{28,20},{1,9},{5... | collective-permute-start | bytes 884744 | tf_op jit(solution)/shard_map/ppermute | solution.py:25
  45.2 23.5 %collective-permute-start.6 = (bf16[192,768]{1,0:T(8,128)(2,1)S(1)}, bf16[192,768]{1,0:T(8,128)(2,1)S(1)}, u32[]{:S(2)}, u32[]{:S(2)}) collective-permute-start(bf16[192,768]{1,0:T(8,128)(2,1)S(1)} %get-tuple-element.158), channel_id=1, source_target_pairs={{0,16},{4,20},{8,24},{12,28},{16,0},{20,4},{24,8},{28,12},{1,17},{... | collective-permute-start | bytes 884744 | tf_op jit(solution)/shard_map/ppermute | solution.py:25
  46.3 22.4 %collective-permute-start.7 = (bf16[192,768]{1,0:T(8,128)(2,1)S(1)}, bf16[192,768]{1,0:T(8,128)(2,1)S(1)}, u32[]{:S(2)}, u32[]{:S(2)}) collective-permute-start(bf16[192,768]{1,0:T(8,128)(2,1)S(1)} %get-tuple-element.158), channel_id=1, source_target_pairs={{0,24},{4,28},{8,16},{12,20},{16,8},{20,12},{24,0},{28,4},{1,25},{... | collective-permute-start | bytes 884744 | tf_op jit(solution)/shard_map/ppermute | solution.py:25
  47.7 32.0 %collective-permute-start.8 = (bf16[4,208,768]{2,1,0:T(8,128)(2,1)}, bf16[4,208,768]{2,1,0:T(8,128)(2,1)}, u32[]{:S(2)}, u32[]{:S(2)}) collective-permute-start(bf16[4,208,768]{2,1,0:T(8,128)(2,1)} %pad_maximum_fusion.1.refs_2_.refs_12_), channel_id=1, source_target_pairs={{0,1},{1,0},{2,3},{3,2},{4,5},{5,4},{6,7},{7,6},{8,9},{9,8},{10,11... | collective-permute-start | bytes 3833864 | tf_op jit(solution)/shard_map/ppermute | solution.py:25
  70.1 11.1 %collective-permute-start.9 = (bf16[4,208,768]{2,1,0:T(8,128)(2,1)}, bf16[4,208,768]{2,1,0:T(8,128)(2,1)}, u32[]{:S(2)}, u32[]{:S(2)}) collective-permute-start(bf16[4,208,768]{2,1,0:T(8,128)(2,1)} %collective-permute-done.4.refs_3_.refs_13_), channel_id=1, source_target_pairs={{0,1},{1,0},{2,3},{3,2},{4,5},{5,4},{6,7},{7,6},{8,9},{9,8},{10,11... | collective-permute-start | bytes 3833864 | tf_op jit(solution)/shard_map/ppermute | solution.py:25
  73.5 28.8 %collective-permute-start.10 = (bf16[4,192,768]{2,1,0:T(8,128)(2,1)}, bf16[4,192,768]{2,1,0:T(8,128)(2,1)}, u32[]{:S(2)}, u32[]{:S(2)}) collective-permute-start(bf16[4,192,768]{2,1,0:T(8,128)(2,1)} %pad_maximum_fusion.3.refs_5_.refs_7_), channel_id=1, source_target_pairs={{0,4},{4,0},{8,12},{12,8},{16,20},{20,16},{24,28},{28,24},{1,5},{5... | collective-permute-start | bytes 3538952 | tf_op jit(solution)/shard_map/ppermute | solution.py:25
  74.5 16.1 %collective-permute-start.11 = (bf16[192,768]{1,0:T(8,128)(2,1)S(1)}, bf16[192,768]{1,0:T(8,128)(2,1)}, u32[]{:S(2)}, u32[]{:S(2)}) collective-permute-start(bf16[192,768]{1,0:T(8,128)(2,1)S(1)} %get-tuple-element.166), channel_id=1, source_target_pairs={{0,8},{4,12},{8,0},{12,4},{16,24},{20,28},{24,16},{28,20},{1,9},{5... | collective-permute-start | bytes 884744 | tf_op jit(solution)/shard_map/ppermute | solution.py:25
  78.7 23.6 %collective-permute-start.12 = (bf16[192,768]{1,0:T(8,128)(2,1)S(1)}, bf16[192,768]{1,0:T(8,128)(2,1)}, u32[]{:S(2)}, u32[]{:S(2)}) collective-permute-start(bf16[192,768]{1,0:T(8,128)(2,1)S(1)} %get-tuple-element.166), channel_id=1, source_target_pairs={{0,16},{4,20},{8,24},{12,28},{16,0},{20,4},{24,8},{28,12},{1,17},{... | collective-permute-start | bytes 884744 | tf_op jit(solution)/shard_map/ppermute | solution.py:25
  79.7 22.6 %collective-permute-start.13 = (bf16[192,768]{1,0:T(8,128)(2,1)S(1)}, bf16[192,768]{1,0:T(8,128)(2,1)}, u32[]{:S(2)}, u32[]{:S(2)}) collective-permute-start(bf16[192,768]{1,0:T(8,128)(2,1)S(1)} %get-tuple-element.166), channel_id=1, source_target_pairs={{0,24},{4,28},{8,16},{12,20},{16,8},{20,12},{24,0},{28,4},{1,25},{... | collective-permute-start | bytes 884744 | tf_op jit(solution)/shard_map/ppermute | solution.py:25
  81.2 31.2 %collective-permute-start.14 = (bf16[4,192,768]{2,1,0:T(8,128)(2,1)}, bf16[4,192,768]{2,1,0:T(8,128)(2,1)}, u32[]{:S(2)}, u32[]{:S(2)}) collective-permute-start(bf16[4,192,768]{2,1,0:T(8,128)(2,1)} %pad_maximum_fusion.3.refs_5_.refs_7_), channel_id=1, source_target_pairs={{0,1},{1,0},{2,3},{3,2},{4,5},{5,4},{6,7},{7,6},{8,9},{9,8},{10,11... | collective-permute-start | bytes 3538952 | tf_op jit(solution)/shard_map/ppermute | solution.py:25
  102.3 14.3 %collective-permute-start.15 = (bf16[4,192,768]{2,1,0:T(8,128)(2,1)}, bf16[4,192,768]{2,1,0:T(8,128)(2,1)S(1)}, u32[]{:S(2)}, u32[]{:S(2)}) collective-permute-start(bf16[4,192,768]{2,1,0:T(8,128)(2,1)} %collective-permute-done.10.refs_6_.refs_8_), channel_id=1, source_target_pairs={{0,1},{1,0},{2,3},{3,2},{4,5},{5,4},{6,7},{7,6},{8,9},{9,8},{10,11... | collective-permute-start | bytes 3538952 | tf_op jit(solution)/shard_map/ppermute | solution.py:25
  103.6 30.1 %collective-permute-start.17 = (bf16[4,192,768]{2,1,0:T(8,128)(2,1)S(1)}, bf16[4,192,768]{2,1,0:T(8,128)(2,1)S(1)}, u32[]{:S(2)}, u32[]{:S(2)}) collective-permute-start(bf16[4,192,768]{2,1,0:T(8,128)(2,1)S(1)} %pad_maximum_fusion.4.refs_5_), channel_id=1, source_target_pairs={{0,4},{4,0},{8,12},{12,8},{16,20},{20,16},{24,28},{28,24},{1,5},{5... | collective-permute-start | bytes 3538952 | tf_op jit(solution)/shard_map/ppermute | solution.py:25
  105.0 28.2 %collective-permute-start.16 = (bf16[192,768]{1,0:T(8,128)(2,1)}, bf16[192,768]{1,0:T(8,128)(2,1)}, u32[]{:S(2)}, u32[]{:S(2)}) collective-permute-start(bf16[192,768]{1,0:T(8,128)(2,1)} %slice_select_fusion.refs_9_), channel_id=1, source_target_pairs={{0,8},{4,12},{8,0},{12,4},{16,24},{20,28},{24,16},{28,20},{1,9},{5... | collective-permute-start | bytes 884744 | tf_op jit(solution)/shard_map/ppermute | solution.py:25
  109.9 23.7 %collective-permute-start.18 = (bf16[192,768]{1,0:T(8,128)(2,1)}, bf16[192,768]{1,0:T(8,128)(2,1)}, u32[]{:S(2)}, u32[]{:S(2)}) collective-permute-start(bf16[192,768]{1,0:T(8,128)(2,1)} %slice_select_fusion.refs_9_), channel_id=1, source_target_pairs={{0,16},{4,20},{8,24},{12,28},{16,0},{20,4},{24,8},{28,12},{1,17},{... | collective-permute-start | bytes 884744 | tf_op jit(solution)/shard_map/ppermute | solution.py:25
  112.5 21.2 %collective-permute-start.19 = (bf16[192,768]{1,0:T(8,128)(2,1)}, bf16[192,768]{1,0:T(8,128)(2,1)}, u32[]{:S(2)}, u32[]{:S(2)}) collective-permute-start(bf16[192,768]{1,0:T(8,128)(2,1)} %slice_select_fusion.refs_9_), channel_id=1, source_target_pairs={{0,24},{4,28},{8,16},{12,20},{16,8},{20,12},{24,0},{28,4},{1,25},{... | collective-permute-start | bytes 884744 | tf_op jit(solution)/shard_map/ppermute | solution.py:25
  116.6 23.6 %collective-permute-start.23 = (bf16[4,192,768]{2,1,0:T(8,128)(2,1)S(1)}, bf16[4,192,768]{2,1,0:T(8,128)(2,1)S(1)}, u32[]{:S(2)}, u32[]{:S(2)}) collective-permute-start(bf16[4,192,768]{2,1,0:T(8,128)(2,1)S(1)} %pad_maximum_fusion.4.refs_5_), channel_id=1, source_target_pairs={{0,1},{1,0},{2,3},{3,2},{4,5},{5,4},{6,7},{7,6},{8,9},{9,8},{10,11... | collective-permute-start | bytes 3538952 | tf_op jit(solution)/shard_map/ppermute | solution.py:25
  133.7 6.5 %collective-permute-start.24 = (bf16[4,192,768]{2,1,0:T(8,128)(2,1)S(1)}, bf16[4,192,768]{2,1,0:T(8,128)(2,1)S(1)}, u32[]{:S(2)}, u32[]{:S(2)}) collective-permute-start(bf16[4,192,768]{2,1,0:T(8,128)(2,1)S(1)} %collective-permute-done.17.refs_6_), channel_id=1, source_target_pairs={{0,1},{1,0},{2,3},{3,2},{4,5},{5,4},{6,7},{7,6},{8,9},{9,8},{10,11... | collective-permute-start | bytes 3538952 | tf_op jit(solution)/shard_map/ppermute | solution.py:25
  135.4 4.8 %collective-permute-start.20 = (bf16[3,192,768]{2,1,0:T(8,128)(2,1)S(1)}, bf16[3,192,768]{2,1,0:T(8,128)(2,1)S(1)}, u32[]{:S(2)}, u32[]{:S(2)}) collective-permute-start(bf16[3,192,768]{2,1,0:T(8,128)(2,1)S(1)} %pad_maximum_fusion.7.refs_7_), channel_id=1, source_target_pairs={{0,1},{1,0},{2,3},{3,2},{4,5},{5,4},{6,7},{7,6},{8,9},{9,8},{10,11... | collective-permute-start | bytes 2654216 | tf_op jit(solution)/shard_map/ppermute | solution.py:25
  135.6 21.9 %collective-permute-start.25 = (bf16[3,192,768]{2,1,0:T(8,128)(2,1)S(1)}, bf16[3,192,768]{2,1,0:T(8,128)(2,1)S(1)}, u32[]{:S(2)}, u32[]{:S(2)}) collective-permute-start(bf16[3,192,768]{2,1,0:T(8,128)(2,1)S(1)} %pad_maximum_fusion.7.refs_7_), channel_id=1, source_target_pairs={{0,4},{4,0},{8,12},{12,8},{16,20},{20,16},{24,28},{28,24},{1,5},{5... | collective-permute-start | bytes 2654216 | tf_op jit(solution)/shard_map/ppermute | solution.py:25
  138.4 1.8 collective-permute-start.21
  157.5 2.2 collective-permute-start.26
  157.5 3.9 %collective-permute-start.27 = (bf16[2,2,96,768]{3,2,1,0:T(8,128)(2,1)}, bf16[2,2,96,768]{3,2,1,0:T(8,128)(2,1)S(1)}, u32[]{:S(2)}, u32[]{:S(2)}) collective-permute-start(bf16[2,2,96,768]{3,2,1,0:T(8,128)(2,1)} %get-tuple-element.182), channel_id=1, source_target_pairs={{0,1},{1,0},{2,3},{3,2},{4,5},{5,4},{6,7},{7,6},{8,9},{9,8},{10,11... | collective-permute-start | bytes 1769480 | tf_op jit(solution)/shard_map/ppermute | solution.py:25
  158.0 6.3 %collective-permute-start.28 = (bf16[3,192,768]{2,1,0:T(8,128)(2,1)S(1)}, bf16[3,192,768]{2,1,0:T(8,128)(2,1)S(1)}, u32[]{:S(2)}, u32[]{:S(2)}) collective-permute-start(bf16[3,192,768]{2,1,0:T(8,128)(2,1)S(1)} %collective-permute-done.25.refs_8_), channel_id=1, source_target_pairs={{0,1},{1,0},{2,3},{3,2},{4,5},{5,4},{6,7},{7,6},{8,9},{9,8},{10,11... | collective-permute-start | bytes 2654216 | tf_op jit(solution)/shard_map/ppermute | solution.py:25
  163.0 33.4 %collective-permute-start.29 = (bf16[4,2,96,768]{3,2,1,0:T(8,128)(2,1)S(1)}, bf16[4,2,96,768]{3,2,1,0:T(8,128)(2,1)S(1)}, u32[]{:S(2)}, u32[]{:S(2)}) collective-permute-start(bf16[4,2,96,768]{3,2,1,0:T(8,128)(2,1)S(1)} %fusion.3), channel_id=1, source_target_pairs={{0,4},{4,0},{8,12},{12,8},{16,20},{20,16},{24,28},{28,24},{1,5},{5... | collective-permute-start | bytes 3538952 | tf_op jit(solution)/shard_map/ppermute | solution.py:25
  195.8 2.1 collective-permute-start.30
  195.9 2.8 collective-permute-start.31
  199.0 28.1 %collective-permute-start.32 = (bf16[4,2,96,768]{3,2,1,0:T(8,128)(2,1)S(1)}, bf16[4,2,96,768]{3,2,1,0:T(8,128)(2,1)S(1)}, u32[]{:S(2)}, u32[]{:S(2)}) collective-permute-start(bf16[4,2,96,768]{3,2,1,0:T(8,128)(2,1)S(1)} %fusion.2), channel_id=1, source_target_pairs={{0,4},{4,0},{8,12},{12,8},{16,20},{20,16},{24,28},{28,24},{1,5},{5... | collective-permute-start | bytes 3538952 | tf_op jit(solution)/shard_map/ppermute | solution.py:25
  199.9 27.2 %collective-permute-start.33 = (bf16[4,2,96,768]{3,2,1,0:T(8,128)(2,1)S(1)}, bf16[4,2,96,768]{3,2,1,0:T(8,128)(2,1)S(1)}, u32[]{:S(2)}, u32[]{:S(2)}) collective-permute-start(bf16[4,2,96,768]{3,2,1,0:T(8,128)(2,1)S(1)} %copy-done.36), channel_id=1, source_target_pairs={{0,1},{1,0},{2,3},{3,2},{4,5},{5,4},{6,7},{7,6},{8,9},{9,8},{10,11... | collective-permute-start | bytes 3538952 | tf_op jit(solution)/shard_map/ppermute | solution.py:25
  199.9 27.7 %collective-permute-start.34 = (bf16[4,2,96,768]{3,2,1,0:T(8,128)(2,1)}, bf16[4,2,96,768]{3,2,1,0:T(8,128)(2,1)S(1)}, u32[]{:S(2)}, u32[]{:S(2)}) collective-permute-start(bf16[4,2,96,768]{3,2,1,0:T(8,128)(2,1)} %get-tuple-element.208), channel_id=1, source_target_pairs={{0,1},{1,0},{2,3},{3,2},{4,5},{5,4},{6,7},{7,6},{8,9},{9,8},{10,11... | collective-permute-start | bytes 3538952 | tf_op jit(solution)/shard_map/ppermute | solution.py:25
  230.4 61.6 %all-to-all-start.1 = ((bf16[4,384,768]{2,1,0:T(8,128)(2,1)}), bf16[4,384,768]{2,1,0:T(8,128)(2,1)S(1)}, u32[]{:S(2)}, u32[]{:S(2)}) async-start(bf16[4,384,768]{2,1,0:T(8,128)(2,1)} %pad_maximum_fusion), calls=%async_computation.1 | async-start | bytes 4718592 | tf_op jit(solution)/shard_map/all_to_all | solution.py:491
  238.7 14.6 %collective-permute-start.35 = (bf16[8,64,768]{2,1,0:T(8,128)(2,1)}, bf16[8,64,768]{2,1,0:T(8,128)(2,1)S(1)}, u32[]{:S(2)}, u32[]{:S(2)}) collective-permute-start(bf16[8,64,768]{2,1,0:T(8,128)(2,1)} %get-tuple-element.217), channel_id=1, source_target_pairs={{0,1},{1,0},{2,3},{3,2},{4,5},{5,4},{6,7},{7,6},{8,9},{9,8},{10,11... | collective-permute-start | bytes 2359304 | tf_op jit(solution)/shard_map/ppermute | solution.py:25
  239.6 13.7 %collective-permute-start.36 = (bf16[4,64,768]{2,1,0:T(8,128)(2,1)S(1)}, bf16[4,64,768]{2,1,0:T(8,128)(2,1)S(1)}, u32[]{:S(2)}, u32[]{:S(2)}) collective-permute-start(bf16[4,64,768]{2,1,0:T(8,128)(2,1)S(1)} %get-tuple-element.282), channel_id=1, source_target_pairs={{0,2},{1,3},{2,0},{3,1},{4,6},{5,7},{6,4},{7,5},{8,10},{9,11},{10,... | collective-permute-start | bytes 1179656 | tf_op jit(solution)/shard_map/ppermute | solution.py:25
  253.3 2.3 collective-permute-start.37
  253.6 2.8 collective-permute-start.38
  253.9 19.5 %collective-permute-start.39 = (bf16[8,64,768]{2,1,0:T(8,128)(2,1)S(1)}, bf16[8,64,768]{2,1,0:T(8,128)(2,1)S(1)}, u32[]{:S(2)}, u32[]{:S(2)}) collective-permute-start(bf16[8,64,768]{2,1,0:T(8,128)(2,1)S(1)} %copy-done.37), channel_id=1, source_target_pairs={{0,3},{1,2},{2,1},{3,0},{4,7},{5,6},{6,5},{7,4},{8,11},{9,10},{10,... | collective-permute-start | bytes 2359304 | tf_op jit(solution)/shard_map/ppermute | solution.py:25
  254.4 25.7 %collective-permute-start.48 = (bf16[4,2,96,768]{3,2,1,0:T(8,128)(2,1)}, bf16[4,2,96,768]{3,2,1,0:T(8,128)(2,1)S(1)}, u32[]{:S(2)}, u32[]{:S(2)}) collective-permute-start(bf16[4,2,96,768]{3,2,1,0:T(8,128)(2,1)} %get-tuple-element.250), channel_id=1, source_target_pairs={{0,1},{1,0},{2,3},{3,2},{4,5},{5,4},{6,7},{7,6},{8,9},{9,8},{10,11... | collective-permute-start | bytes 3538952 | tf_op jit(solution)/shard_map/ppermute | solution.py:25
  258.0 28.9 %collective-permute-start.49 = (bf16[4,2,96,768]{3,2,1,0:T(8,128)(2,1)S(1)}, bf16[4,2,96,768]{3,2,1,0:T(8,128)(2,1)S(1)}, u32[]{:S(2)}, u32[]{:S(2)}) collective-permute-start(bf16[4,2,96,768]{3,2,1,0:T(8,128)(2,1)S(1)} %fusion.1), channel_id=1, source_target_pairs={{0,4},{4,0},{8,12},{12,8},{16,20},{20,16},{24,28},{28,24},{1,5},{5... | collective-permute-start | bytes 3538952 | tf_op jit(solution)/shard_map/ppermute | solution.py:25
  273.4 2.3 collective-permute-start.40
  273.8 2.7 collective-permute-start.41
  279.2 32.7 %collective-permute-start.46 = (bf16[4,2,96,768]{3,2,1,0:T(8,128)(2,1)}, bf16[4,2,96,768]{3,2,1,0:T(8,128)(2,1)}, u32[]{:S(2)}, u32[]{:S(2)}) collective-permute-start(bf16[4,2,96,768]{3,2,1,0:T(8,128)(2,1)} %fusion), channel_id=1, source_target_pairs={{0,4},{4,0},{8,12},{12,8},{16,20},{20,16},{24,28},{28,24},{1,5},{5... | collective-permute-start | bytes 3538952 | tf_op jit(solution)/shard_map/ppermute | solution.py:25
  292.0 31.7 %all-to-all-start.3 = ((bf16[4,192,768]{2,1,0:T(8,128)(2,1)}), bf16[4,192,768]{2,1,0:T(8,128)(2,1)S(1)}, u32[]{:S(2)}, u32[]{:S(2)}) async-start(bf16[4,192,768]{2,1,0:T(8,128)(2,1)} %bitcast.72), calls=%async_computation.3 | async-start | bytes 2359296 | tf_op jit(solution)/shard_map/all_to_all | solution.py:491
  295.8 17.8 %collective-permute-start.43 = (bf16[4,2,96,768]{3,2,1,0:T(8,128)(2,1)}, bf16[4,2,96,768]{3,2,1,0:T(8,128)(2,1)}, u32[]{:S(2)}, u32[]{:S(2)}) collective-permute-start(bf16[4,2,96,768]{3,2,1,0:T(8,128)(2,1)} %get-tuple-element.241), channel_id=1, source_target_pairs={{0,1},{1,0},{2,3},{3,2},{4,5},{5,4},{6,7},{7,6},{8,9},{9,8},{10,11... | collective-permute-start | bytes 3538952 | tf_op jit(solution)/shard_map/ppermute | solution.py:25
  297.2 16.4 %collective-permute-start.42 = (bf16[384,768]{1,0:T(8,128)(2,1)}, bf16[384,768]{1,0:T(8,128)(2,1)}, u32[]{:S(2)}, u32[]{:S(2)}) collective-permute-start(bf16[384,768]{1,0:T(8,128)(2,1)} %reduce_sum.36), channel_id=1, source_target_pairs={{0,2},{1,3},{2,0},{3,1},{4,6},{5,7},{6,4},{7,5},{8,10},{9,11},{10,... | collective-permute-start | bytes 1769480 | tf_op jit(solution)/shard_map/ppermute | solution.py:25
  300.7 11.3 %collective-permute-start.45 = (bf16[16,768]{1,0:T(8,128)(2,1)S(1)}, bf16[16,768]{1,0:T(8,128)(2,1)S(1)}, u32[]{:S(2)}, u32[]{:S(2)}) collective-permute-start(bf16[16,768]{1,0:T(8,128)(2,1)S(1)} %add_convert_fusion.5), channel_id=1, source_target_pairs={{0,4},{4,0},{8,12},{12,8},{16,20},{20,16},{24,28},{28,24},{1,5},{5... | collective-permute-start | bytes 73736 | tf_op jit(solution)/shard_map/ppermute | solution.py:25
  301.5 27.2 %collective-permute-start.54 = (bf16[4,64,768]{2,1,0:T(8,128)(2,1)}, bf16[4,64,768]{2,1,0:T(8,128)(2,1)}, u32[]{:S(2)}, u32[]{:S(2)}) collective-permute-start(bf16[4,64,768]{2,1,0:T(8,128)(2,1)} %get-tuple-element.281), channel_id=1, source_target_pairs={{0,2},{1,3},{2,0},{3,1},{4,6},{5,7},{6,4},{7,5},{8,10},{9,11},{10,... | collective-permute-start | bytes 1179656 | tf_op jit(solution)/shard_map/ppermute | solution.py:25
  317.2 16.7 %collective-permute-start.51 = (bf16[8,32,768]{2,1,0:T(8,128)(2,1)}, bf16[8,32,768]{2,1,0:T(8,128)(2,1)}, u32[]{:S(2)}, u32[]{:S(2)}) collective-permute-start(bf16[8,32,768]{2,1,0:T(8,128)(2,1)} %get-tuple-element.253.refs_4_), channel_id=1, source_target_pairs={{0,2},{1,3},{2,0},{3,1},{4,6},{5,7},{6,4},{7,5},{8,10},{9,11},{10,... | collective-permute-start | bytes 1179656 | tf_op jit(solution)/shard_map/ppermute | solution.py:25
  318.6 22.9 %collective-permute-start.52 = (bf16[384,768]{1,0:T(8,128)(2,1)S(1)}, bf16[384,768]{1,0:T(8,128)(2,1)}, u32[]{:S(2)}, u32[]{:S(2)}) collective-permute-start(bf16[384,768]{1,0:T(8,128)(2,1)S(1)} %copy-done.7), channel_id=1, source_target_pairs={{0,1},{1,0},{2,3},{3,2},{4,5},{5,4},{6,7},{7,6},{8,9},{9,8},{10,11... | collective-permute-start | bytes 1769480 | tf_op jit(solution)/shard_map/ppermute | solution.py:25
  318.6 22.9 %collective-permute-start.53 = (bf16[384,768]{1,0:T(8,128)(2,1)}, bf16[384,768]{1,0:T(8,128)(2,1)}, u32[]{:S(2)}, u32[]{:S(2)}) collective-permute-start(bf16[384,768]{1,0:T(8,128)(2,1)} %collective-permute-done.42), channel_id=1, source_target_pairs={{0,1},{1,0},{2,3},{3,2},{4,5},{5,4},{6,7},{7,6},{8,9},{9,8},{10,11... | collective-permute-start | bytes 1769480 | tf_op jit(solution)/shard_map/ppermute | solution.py:25
  323.8 33.7 %all-to-all-start.2 = ((bf16[4,208,768]{2,1,0:T(8,128)(2,1)}), bf16[4,208,768]{2,1,0:T(8,128)(2,1)S(1)}, u32[]{:S(2)}, u32[]{:S(2)}) async-start(bf16[4,208,768]{2,1,0:T(8,128)(2,1)} %pad_maximum_fusion.2), calls=%async_computation.2 | async-start | bytes 2555904 | tf_op jit(solution)/shard_map/all_to_all | solution.py:491
  327.3 12.2 %collective-permute-start.47 = (bf16[8,32,768]{2,1,0:T(8,128)(2,1)S(1)}, bf16[8,32,768]{2,1,0:T(8,128)(2,1)}, u32[]{:S(2)}, u32[]{:S(2)}) collective-permute-start(bf16[8,32,768]{2,1,0:T(8,128)(2,1)S(1)} %copy-done.8), channel_id=1, source_target_pairs={{0,2},{1,3},{2,0},{3,1},{4,6},{5,7},{6,4},{7,5},{8,10},{9,11},{10,... | collective-permute-start | bytes 1179656 | tf_op jit(solution)/shard_map/ppermute | solution.py:25
  329.7 15.9 %collective-permute-start.50 = (bf16[192,768]{1,0:T(8,128)(2,1)}, bf16[192,768]{1,0:T(8,128)(2,1)S(1)}, u32[]{:S(2)}, u32[]{:S(2)}) collective-permute-start(bf16[192,768]{1,0:T(8,128)(2,1)} %reduce_sum.37), channel_id=1, source_target_pairs={{0,2},{1,3},{2,0},{3,1},{4,6},{5,7},{6,4},{7,5},{8,10},{9,11},{10,... | collective-permute-start | bytes 884744 | tf_op jit(solution)/shard_map/ppermute | solution.py:25
  357.7 2.5 collective-permute-start.60
  357.8 2.4 collective-permute-start.61
  358.3 3.9 %collective-permute-start.56 = (bf16[2,8,32,768]{3,2,1,0:T(8,128)(2,1)S(1)}, bf16[2,8,32,768]{3,2,1,0:T(8,128)(2,1)}, u32[]{:S(2)}, u32[]{:S(2)}) collective-permute-start(bf16[2,8,32,768]{3,2,1,0:T(8,128)(2,1)S(1)} %pad_maximum_fusion.9), channel_id=1, source_target_pairs={{0,1},{1,0},{2,3},{3,2},{4,5},{5,4},{6,7},{7,6},{8,9},{9,8},{10,11... | collective-permute-start | bytes 2359304 | tf_op jit(solution)/shard_map/ppermute | solution.py:25
  358.4 4.0 %collective-permute-start.55 = (bf16[2,8,32,768]{3,2,1,0:T(8,128)(2,1)}, bf16[2,8,32,768]{3,2,1,0:T(8,128)(2,1)}, u32[]{:S(2)}, u32[]{:S(2)}) collective-permute-start(bf16[2,8,32,768]{3,2,1,0:T(8,128)(2,1)} %pad_maximum_fusion.8), channel_id=1, source_target_pairs={{0,1},{1,0},{2,3},{3,2},{4,5},{5,4},{6,7},{7,6},{8,9},{9,8},{10,11... | collective-permute-start | bytes 2359304 | tf_op jit(solution)/shard_map/ppermute | solution.py:25
  358.8 9.5 %collective-permute-start.57 = (bf16[208,768]{1,0:T(8,128)(2,1)S(1)}, bf16[208,768]{1,0:T(8,128)(2,1)S(1)}, u32[]{:S(2)}, u32[]{:S(2)}) collective-permute-start(bf16[208,768]{1,0:T(8,128)(2,1)S(1)} %reduce_sum.38), channel_id=1, source_target_pairs={{0,2},{1,3},{2,0},{3,1},{4,6},{5,7},{6,4},{7,5},{8,10},{9,11},{10,... | collective-permute-start | bytes 958472 | tf_op jit(solution)/shard_map/ppermute | solution.py:25
  368.4 2.0 collective-permute-start.58
  368.5 2.0 collective-permute-start.59
  (42 other events, 424.7 us)

commit v5 on v4

--- a/solution.py
+++ b/solution.py
@@ -827,9 +827,11 @@
     in_scatter = scatter(in_grads, gx2)
     in_sum = in_scatter.add_cores(*out_scatter.came)
     in_scatter.send_fast()
+    out_total = out_scatter.add_fast(*in_sum)
+    out_scatter.send_slow()
     gx1, vecs_cross, dkv, dq2, grad_memory = run(
         cross_backward,
-        [(SMEM, where), (VMEM, x1), (VMEM, vec), (VMEM, after(gx2, *in_sum)), (VMEM, q2)]
+        [(SMEM, where), (VMEM, x1), (VMEM, vec), (VMEM, after(gx2, out_total, *in_sum)), (VMEM, q2)]
         + [per_example(kv), per_example(p2), cross_weights],
         [
             flat(wide, F32),
@@ -844,9 +846,9 @@
         60_000_000,
     )
     in_scatter.came, _ = lax.optimization_barrier((in_scatter.came, gx1))
-    dense_total = [one.add_fast(*in_scatter.came) for one in (out_scatter, in_scatter)]
-    dense_total = jnp.concatenate(dense_total, axis=1)
-    dense_came = over_slow(dense_total, slow, fast)
+    out_final = out_scatter.add_slow(*in_scatter.came)
+    in_total = in_scatter.add_fast(out_final)
+    in_scatter.send_slow()
     cut = examples // 2
     mem_pieces = [grad_memory[:1]]
     for d in range(1, mem):
@@ -854,7 +856,7 @@
         mem_pieces.append([swap(part, "mem", d) for part in parts])
     grads = run(
         cross_grads,
-        [(SMEM, where), (VMEM, after(gx2, dense_total)), (VMEM, a2), (VMEM, o2), (VMEM, dq2)]
+        [(SMEM, where), (VMEM, after(gx2, in_total)), (VMEM, a2), (VMEM, o2), (VMEM, dq2)]
         + [(pl.BlockSpec((examples, total, width), lambda j: (0, 0, j)), dkv), (ANY, turned)],
         grads_like,
         [square, scratch(width, tokens)],
@@ -874,12 +876,13 @@
         [square, own_rows, square, scratch(rows, 3 * width), scratch(*wide)],
         1 + blocks,
     )
-    self_scatter = scatter(grads, *mem_pieces[3], vectors=vecs_self)
+    in_final = in_scatter.add_slow(suffix_part)
+    self_scatter = scatter(grads, in_final, *mem_pieces[3], vectors=vecs_self)
     self_sum = self_scatter.add_cores()
     self_scatter.send_fast()
     cross_scatter.add_fast(*self_sum)
     cross_scatter.send_slow()
-    dense_sum = jnp.sum(after(dense_came, *self_sum).astype(F32), axis=0)
+    dense_sum = jnp.concatenate([out_final, after(in_final, *self_sum)])
     dense_sum = Replicas(dense_sum, 2 * part, across)
     self_total = self_scatter.add_fast(*dense_sum.halves)
     self_scatter.send_slow()

time: 376 us -> 383 us (1.019)
  starting transfers between devices: 74.2 us -> 80.1 us
  waiting for transfers between devices: 126 us -> 122 us
    all_to_all x3 -> x4, waiting for transfers between devices: 20.2 us -> 11.6 us  [over_slow(): lax.all_to_all(value, 'fsdp', 0, 0, axis_index_groups=groups, tiled=True)]
    all_to_all x3 -> x4, starting transfers between devices: 15.6 us -> 22 us  [over_slow(): lax.all_to_all(value, 'fsdp', 0, 0, axis_index_groups=groups, tiled=True)]
    convert_element_type x4, other arithmetic: 4.81 us -> 9.4 us  [add_fast(): self.total = total.astype(BF).reshape(self.slow, -1, total.shape[-1])]
    ppermute x62, waiting for transfers between devices: 106 us -> 110 us  [swap(): return lax.ppermute(value, axis, [(i, i ^ distance) for i in range(size)])]
  transfers between devices with their start and end apart: 66 -> 67, of which waited for: 32 -> 31; matrix products, arithmetic and copies ran while one was open for 11% -> 12% of each run, Pallas kernels for 31% -> 31%
where the time goes in v5:
time: 383 us; the launch traced here: 379 us
  waiting for transfers between devices  122 us (32%)
  Pallas kernels  117 us (31%)
  starting transfers between devices  80.1 us (21%)
  other arithmetic  39.9 us (10%)
  local copies, waits for them, and re-layouts  18.3 us (5%)
    pallas_call x10, Pallas kernels, run(): pl.pallas_call(body, grid=grid, in_specs=[spec for spec, _ in flat_in], o...  117 us
    ppermute x62, waiting for transfers between devices, swap(): return lax.ppermute(value, axis, [(i, i ^ distance) for i in range(size)])  110 us
    ppermute x62, starting transfers between devices, swap(): return lax.ppermute(value, axis, [(i, i ^ distance) for i in range(size)])  53.9 us
    all_to_all x4, starting transfers between devices, over_slow(): lax.all_to_all(value, 'fsdp', 0, 0, axis_index_groups=groups, tiled=True)  22 us
    all_to_all x4, waiting for transfers between devices, over_slow(): lax.all_to_all(value, 'fsdp', 0, 0, axis_index_groups=groups, tiled=True)  11.6 us
    convert_element_type x4, other arithmetic, add_fast(): self.total = total.astype(BF).reshape(self.slow, -1, total.shape[-1])  9.4 us
  transfers between devices with their start and end apart: 67, of which 31 were waited for; matrix products, arithmetic and copies ran while one was open for 12% of the time, Pallas kernels for 31%

profile of v5, /device:TPU:0, one launch (start us, length us, event | category | flops | bytes accessed | tf_op | source)
XLA Modules:
  0.0 379.0 jit_solution(17435093063898765502)
XLA Ops:
  3.6 4.2 %all-to-all-start = ((bf16[4,8,64,768]{3,2,1,0:T(8,128)(2,1)}), bf16[4,8,64,768]{3,2,1,0:T(8,128)(2,1)S(1)}, u32[]{:S(2)}, u32[]{:S(2)}) async-start(bf16[4,8,64,768]{3,2,1,0:T(8,128)(2,1)} %bitcast.72), calls=%async_computation | async-start | bytes 6291456 | tf_op jit(solution)/shard_map/all_to_all | solution.py:702
  7.8 2.6 collective-permute-start
  10.4 2.6 collective-permute-start.1
  13.0 1.8 slice_select_fusion.refs_9_
  14.8 1.7 collective-permute-start.3
  16.5 7.3 %collective-permute-done.3.refs_10_ = bf16[192,768]{1,0:T(8,128)(2,1)S(1)} collective-permute-done((bf16[192,768]{1,0:T(8,128)(2,1)}, bf16[192,768]{1,0:T(8,128)(2,1)S(1)}, u32[]{:S(2)}, u32[]{:S(2)}) %collective-permute-start.3) | collective-permute-done | bytes 294944 | tf_op jit(solution)/shard_map/ppermute | solution.py:25
  24.9 10.5 %collective-permute-done.1 = bf16[208,768]{1,0:T(8,128)(2,1)S(1)} collective-permute-done((bf16[208,768]{1,0:T(8,128)(2,1)S(1)}, bf16[208,768]{1,0:T(8,128)(2,1)S(1)}, u32[]{:S(2)}, u32[]{:S(2)}) %collective-permute-start.1) | collective-permute-done | bytes 319520 | tf_op jit(solution)/shard_map/ppermute | solution.py:25
  35.4 1.2 pad_maximum_fusion.refs_2_.refs_12_
  36.7 1.6 collective-permute-start.4
  38.5 6.7 %collective-permute-start.5 = (bf16[192,768]{1,0:T(8,128)(2,1)S(1)}, bf16[192,768]{1,0:T(8,128)(2,1)S(1)}, u32[]{:S(2)}, u32[]{:S(2)}) collective-permute-start(bf16[192,768]{1,0:T(8,128)(2,1)S(1)} %get-tuple-element.160), channel_id=1, source_target_pairs={{0,8},{4,12},{8,0},{12,4},{16,24},{20,28},{24,16},{28,20},{1,9},{5... | collective-permute-start | bytes 884744 | tf_op jit(solution)/shard_map/ppermute | solution.py:25
  46.3 1.4 collective-permute-start.7
  47.7 8.9 %collective-permute-done.5 = bf16[192,768]{1,0:T(8,128)(2,1)S(1)} collective-permute-done((bf16[192,768]{1,0:T(8,128)(2,1)S(1)}, bf16[192,768]{1,0:T(8,128)(2,1)S(1)}, u32[]{:S(2)}, u32[]{:S(2)}) %collective-permute-start.5) | collective-permute-done | bytes 294944 | tf_op jit(solution)/shard_map/ppermute | solution.py:25
  56.6 12.1 %collective-permute-done.6 = bf16[192,768]{1,0:T(8,128)(2,1)S(1)} collective-permute-done((bf16[192,768]{1,0:T(8,128)(2,1)S(1)}, bf16[192,768]{1,0:T(8,128)(2,1)S(1)}, u32[]{:S(2)}, u32[]{:S(2)}) %collective-permute-start.6) | collective-permute-done | bytes 294944 | tf_op jit(solution)/shard_map/ppermute | solution.py:25
  70.2 3.3 pad_maximum_fusion.2.refs_5_.refs_7_
  74.5 4.2 %collective-permute-start.11 = (bf16[192,768]{1,0:T(8,128)(2,1)S(1)}, bf16[192,768]{1,0:T(8,128)(2,1)}, u32[]{:S(2)}, u32[]{:S(2)}) collective-permute-start(bf16[192,768]{1,0:T(8,128)(2,1)S(1)} %get-tuple-element.168), channel_id=1, source_target_pairs={{0,8},{4,12},{8,0},{12,4},{16,24},{20,28},{24,16},{28,20},{1,9},{5... | collective-permute-start | bytes 884744 | tf_op jit(solution)/shard_map/ppermute | solution.py:25
  79.7 1.5 collective-permute-start.13
  81.8 7.8 %shard_map.373 = (f32[256,768]{1,0:T(8,128)}, bf16[256,768]{1,0:T(8,128)(2,1)}, bf16[256,2304]{1,0:T(8,128)(2,1)}, bf16[6,512,128]{2,1,0:T(8,128)(2,1)}, bf16[256,768]{1,0:T(8,128)(2,1)}, /*index=5*/f32[16,768]{1,0:T(8,128)}) custom-call(s32[4]{0:T(128)} %pad_add_fusion.1.refs_0_, bf16[32,32,768]{2,1,0:T(8,128)(2,1)} %refs_1_.5, ...), custom_call_target="tpu_custom_call" | custom-call | tf_op jit(solution)/shard_map/pallas_call | solution.py:470
  90.6 11.7 %collective-permute-done.12 = bf16[192,768]{1,0:T(8,128)(2,1)} collective-permute-done((bf16[192,768]{1,0:T(8,128)(2,1)S(1)}, bf16[192,768]{1,0:T(8,128)(2,1)}, u32[]{:S(2)}, u32[]{:S(2)}) %collective-permute-start.12) | collective-permute-done | bytes 294944 | tf_op jit(solution)/shard_map/ppermute | solution.py:25
  102.3 1.3 pad_maximum_fusion.3.refs_5_
  105.0 4.9 %collective-permute-start.16 = (bf16[192,768]{1,0:T(8,128)(2,1)}, bf16[192,768]{1,0:T(8,128)(2,1)}, u32[]{:S(2)}, u32[]{:S(2)}) collective-permute-start(bf16[192,768]{1,0:T(8,128)(2,1)} %slice_select_fusion.refs_9_), channel_id=1, source_target_pairs={{0,8},{4,12},{8,0},{12,4},{16,24},{20,28},{24,16},{28,20},{1,9},{5... | collective-permute-start | bytes 884744 | tf_op jit(solution)/shard_map/ppermute | solution.py:25
  112.5 1.5 collective-permute-start.19
  117.7 15.6 %shard_map.374 = (f32[256,768]{1,0:T(8,128)}, bf16[256,768]{1,0:T(8,128)(2,1)}, bf16[256,768]{1,0:T(8,128)(2,1)}, bf16[8,256,1536]{2,1,0:T(8,128)(2,1)}, bf16[8,...) custom-call(s32[4]{0:T(128)} %pad_add_fusion.1.refs_0_, s32[32]{0:T(128)} %refs_1_.4, ...), custom_call_target="tpu_custom_call" | custom-call | tf_op jit(solution)/shard_map/pallas_call | solution.py:470
  133.8 1.6 pad_maximum_fusion.6.refs_7_
  135.6 1.2 collective-permute-start.25
  136.9 1.5 collective-permute-done.22.refs_14_
  138.5 1.7 collective-permute-done.21.refs_13_
  142.3 13.5 %shard_map.375 = (bf16[256,768]{1,0:T(8,128)(2,1)}, bf16[256,3072]{1,0:T(8,128)(2,1)}, bf16[256,3072]{1,0:T(8,128)(2,1)}, bf16[4,2,96,768]{3,2,1,0:T(8,128)(2,1)...) custom-call(s32[4]{0:T(128)} %pad_add_fusion.1.refs_0_, ...), custom_call_target="tpu_custom_call" | custom-call | tf_op jit(solution)/shard_map/pallas_call | solution.py:470
  155.9 1.7 collective-permute-done.25.refs_8_
  158.1 1.7 collective-permute-done.26
  160.7 1.6 fusion.3
  162.3 1.3 collective-permute-start.29
  164.5 11.8 %shard_map.376 = (bf16[8,32,768]{2,1,0:T(8,128)(2,1)}, bf16[256,3072]{1,0:T(8,128)(2,1)}, f32[1,768]{1,0:T(1,128)}, f32[1,3072]{1,0:T(1,128)}, bf16[4,2,96,768]{...) custom-call(s32[4]{0:T(128)} %pad_add_fusion.1.refs_0_, ...), custom_call_target="tpu_custom_call" | custom-call | tf_op jit(solution)/shard_map/pallas_call | solution.py:470
  176.3 19.8 %shard_map.377 = (f32[256,768]{1,0:T(8,128)}, f32[2,768]{1,0:T(2,128)}) custom-call(s32[4]{0:T(128)} %pad_add_fusion.1.refs_0_, f32[256,768]{1,0:T(8,128)} %get-tuple-element.185.refs_1_, f32[16,768]{1,0:T(8,128)} %get-tuple-element.159.refs_3_.refs_2_, bf16[256,3072]{1,0:T(8,128)(2,1)} %get-tuple-element.189.refs_3_, bf16[32,32,768]{2,1,0:T(8,128)(2,1)} %refs_4_.3, ...), custom_call_target="tpu_custom_call" | custom-call | tf_op jit(solution)/shard_map/pallas_call | solution.py:470
  196.8 1.5 collective-permute-done.30
  199.6 1.5 add_convert_fusion.3
  201.0 8.2 %all-to-all-start.1 = ((bf16[4,192,768]{2,1,0:T(8,128)(2,1)}), bf16[4,192,768]{2,1,0:T(8,128)(2,1)S(1)}, u32[]{:S(2)}, u32[]{:S(2)}) async-start(bf16[4,192,768]{2,1,0:T(8,128)(2,1)} %bitcast.34), calls=%async_computation.1 | async-start | bytes 2359296 | tf_op jit(solution)/shard_map/all_to_all | solution.py:491
  210.0 17.7 %shard_map.378 = (f32[256,768]{1,0:T(8,128)}, f32[2,768]{1,0:T(2,128)}, bf16[8,256,1536]{2,1,0:T(8,128)(2,1)}, bf16[256,768]{1,0:T(8,128)(2,1)}, bf16[8,64,768]{...) custom-call(s32[4]{0:T(128)} %pad_add_fusion.1.refs_0_, ...), custom_call_target="tpu_custom_call" | custom-call | bytes 60000000 | tf_op jit(solution)/shard_map/pallas_call | solution.py:470
  228.2 8.9 %collective-permute-done.33 = bf16[4,2,96,768]{3,2,1,0:T(8,128)(2,1)S(1)} collective-permute-done((bf16[4,2,96,768]{3,2,1,0:T(8,128)(2,1)S(1)}, bf16[4,2,96,768]{3,2,1,0:T(8,128)(2,1)S(1)}, u32[]{:S(2)}, u32[]{:S(2)}) %collective-permute-start.33) | collective-permute-done | bytes 1179680 | tf_op jit(solution)/shard_map/ppermute | solution.py:25
  238.5 3.1 add_convert_fusion.2
  241.6 4.9 %all-to-all-start.2 = ((bf16[4,192,768]{2,1,0:T(8,128)(2,1)}), bf16[4,192,768]{2,1,0:T(8,128)(2,1)S(1)}, u32[]{:S(2)}, u32[]{:S(2)}) async-start(bf16[4,192,768]{2,1,0:T(8,128)(2,1)} %bitcast.35), calls=%async_computation.2 | async-start | bytes 2359296 | tf_op jit(solution)/shard_map/all_to_all | solution.py:491
  247.2 1.4 collective-permute-start.36
  248.6 12.2 %shard_map.379 = (bf16[4,2,96,768]{3,2,1,0:T(8,128)(2,1)}, bf16[1,4,2,96,768]{4,3,2,1,0:T(8,128)(2,1)}, bf16[4,2,96,768]{3,2,1,0:T(8,128)(2,1)}, bf16[2,2,96,768]{3,2,1,0:T(8,128)(2,1)}, bf16[2,2,96,768]{3,2,1,0:T(8,128)(2,1)}) custom-call(s32[4]{0:T(128)} %pad_add_fusion.1.refs_0_, f32[256,768]{1,0:T(8,128)} %get-tuple-element.212.refs_3_.refs_1_, ...), custom_call_target="tpu_custom_call" | custom-call | tf_op jit(solution)/shard_map/pallas_call | solution.py:470
  264.0 1.6 fusion.1
  265.6 1.7 collective-permute-start.49
  267.3 11.7 %shard_map.380 = (bf16[8,32,768]{2,1,0:T(8,128)(2,1)}, bf16[16,768]{1,0:T(8,128)(2,1)}, bf16[4,2,96,768]{3,2,1,0:T(8,128)(2,1)}, bf16[1,4,2,96,768]{4,3,2,1,0:T(...) custom-call(s32[4]{0:T(128)} %pad_add_fusion.1.refs_0_, ...), custom_call_target="tpu_custom_call" | custom-call | tf_op jit(solution)/shard_map/pallas_call | solution.py:470
  279.2 2.1 collective-permute-done.39.refs_5_
  281.8 1.7 collective-permute-done.40
  284.4 1.3 fusion
  286.5 8.0 %collective-permute-done.49 = bf16[4,2,96,768]{3,2,1,0:T(8,128)(2,1)} collective-permute-done((bf16[4,2,96,768]{3,2,1,0:T(8,128)(2,1)S(1)}, bf16[4,2,96,768]{3,2,1,0:T(8,128)(2,1)}, u32[]{:S(2)}, u32[]{:S(2)}) %collective-permute-start.49) | collective-permute-done | bytes 1179680 | tf_op jit(solution)/shard_map/ppermute | solution.py:25
  294.6 3.1 add_convert_fusion
  297.6 5.2 %all-to-all-start.4 = ((bf16[4,192,768]{2,1,0:T(8,128)(2,1)}), bf16[4,192,768]{2,1,0:T(8,128)(2,1)S(1)}, u32[]{:S(2)}, u32[]{:S(2)}) async-start(bf16[4,192,768]{2,1,0:T(8,128)(2,1)} %bitcast.41), calls=%async_computation.4 | async-start | bytes 2359296 | tf_op jit(solution)/shard_map/all_to_all | solution.py:491
  305.8 1.7 collective-permute-start.45
  308.7 11.5 %collective-permute-done.42 = bf16[384,768]{1,0:T(8,128)(2,1)} collective-permute-done((bf16[384,768]{1,0:T(8,128)(2,1)}, bf16[384,768]{1,0:T(8,128)(2,1)}, u32[]{:S(2)}, u32[]{:S(2)}) %collective-permute-start.42) | collective-permute-done | bytes 589856 | tf_op jit(solution)/shard_map/ppermute | solution.py:25
  320.2 1.8 add_convert_fusion.1
  324.3 5.8 %all-to-all-done.4 = bf16[4,192,768]{2,1,0:T(8,128)(2,1)S(1)} async-done(((bf16[4,192,768]{2,1,0:T(8,128)(2,1)}), bf16[4,192,768]{2,1,0:T(8,128)(2,1)S(1)}, u32[]{:S(2)}, u32[]{:S(2)}) %all-to-all-start.4) | async-done | bytes 1179680 | tf_op jit(solution)/shard_map/all_to_all | solution.py:491
  330.1 3.8 all-to-all-start.3
  334.6 3.5 shard_map.381
  338.1 2.1 pad_maximum_fusion.8
  340.2 4.7 %collective-permute-done.47.refs_2_ = bf16[8,32,768]{2,1,0:T(8,128)(2,1)S(1)} collective-permute-done((bf16[8,32,768]{2,1,0:T(8,128)(2,1)S(1)}, bf16[8,32,768]{2,1,0:T(8,128)(2,1)S(1)}, u32[]{:S(2)}, u32[]{:S(2)}) %collective-permute-start.47) | collective-permute-done | bytes 393248 | tf_op jit(solution)/shard_map/ppermute | solution.py:25
  346.0 1.7 fusion.5
  350.8 2.2 pad_maximum_fusion.4
  353.0 5.2 %collective-permute-done.50 = bf16[192,768]{1,0:T(8,128)(2,1)S(1)} collective-permute-done((bf16[192,768]{1,0:T(8,128)(2,1)S(1)}, bf16[192,768]{1,0:T(8,128)(2,1)S(1)}, u32[]{:S(2)}, u32[]{:S(2)}) %collective-permute-start.50) | collective-permute-done | bytes 294944 | tf_op jit(solution)/shard_map/ppermute | solution.py:25
  358.2 5.7 %all-to-all-done.3 = bf16[4,208,768]{2,1,0:T(8,128)(2,1)S(1)} async-done(((bf16[4,208,768]{2,1,0:T(8,128)(2,1)}), bf16[4,208,768]{2,1,0:T(8,128)(2,1)S(1)}, u32[]{:S(2)}, u32[]{:S(2)}) %all-to-all-start.3) | async-done | bytes 1277984 | tf_op jit(solution)/shard_map/all_to_all | solution.py:491
  370.3 3.4 shard_map.382
  (226 shorter events, 56.6 us)
Async XLA Ops:
  3.6 66.5 %all-to-all-start = ((bf16[4,8,64,768]{3,2,1,0:T(8,128)(2,1)}), bf16[4,8,64,768]{3,2,1,0:T(8,128)(2,1)S(1)}, u32[]{:S(2)}, u32[]{:S(2)}) async-start(bf16[4,8,64,768]{3,2,1,0:T(8,128)(2,1)} %bitcast.72), calls=%async_computation | async-start | bytes 6291456 | tf_op jit(solution)/shard_map/all_to_all | solution.py:702
  7.8 17.1 %collective-permute-start = (bf16[208,768]{1,0:T(8,128)(2,1)S(1)}, bf16[208,768]{1,0:T(8,128)(2,1)S(1)}, u32[]{:S(2)}, u32[]{:S(2)}) collective-permute-start(bf16[208,768]{1,0:T(8,128)(2,1)S(1)} %pad_maximum_fusion.10), channel_id=1, source_target_pairs={{0,8},{4,12},{8,0},{12,4},{16,24},{20,28},{24,16},{28,20},{1,9},{5... | collective-permute-start | bytes 958472 | tf_op jit(solution)/shard_map/ppermute | solution.py:25
  10.4 25.0 %collective-permute-start.1 = (bf16[208,768]{1,0:T(8,128)(2,1)S(1)}, bf16[208,768]{1,0:T(8,128)(2,1)S(1)}, u32[]{:S(2)}, u32[]{:S(2)}) collective-permute-start(bf16[208,768]{1,0:T(8,128)(2,1)S(1)} %pad_maximum_fusion.10), channel_id=1, source_target_pairs={{0,16},{4,20},{8,24},{12,28},{16,0},{20,4},{24,8},{28,12},{1,17},{... | collective-permute-start | bytes 958472 | tf_op jit(solution)/shard_map/ppermute | solution.py:25
  13.0 22.4 %collective-permute-start.2 = (bf16[208,768]{1,0:T(8,128)(2,1)S(1)}, bf16[208,768]{1,0:T(8,128)(2,1)S(1)}, u32[]{:S(2)}, u32[]{:S(2)}) collective-permute-start(bf16[208,768]{1,0:T(8,128)(2,1)S(1)} %pad_maximum_fusion.10), channel_id=1, source_target_pairs={{0,24},{4,28},{8,16},{12,20},{16,8},{20,12},{24,0},{28,4},{1,25},{... | collective-permute-start | bytes 958472 | tf_op jit(solution)/shard_map/ppermute | solution.py:25
  14.8 9.0 %collective-permute-start.3 = (bf16[192,768]{1,0:T(8,128)(2,1)}, bf16[192,768]{1,0:T(8,128)(2,1)S(1)}, u32[]{:S(2)}, u32[]{:S(2)}) collective-permute-start(bf16[192,768]{1,0:T(8,128)(2,1)} %slice_select_fusion.refs_9_), channel_id=1, source_target_pairs={{0,4},{4,0},{8,12},{12,8},{16,20},{20,16},{24,28},{28,24},{1,5},{5... | collective-permute-start | bytes 884744 | tf_op jit(solution)/shard_map/ppermute | solution.py:25
  36.7 33.4 %collective-permute-start.4 = (bf16[4,208,768]{2,1,0:T(8,128)(2,1)}, bf16[4,208,768]{2,1,0:T(8,128)(2,1)}, u32[]{:S(2)}, u32[]{:S(2)}) collective-permute-start(bf16[4,208,768]{2,1,0:T(8,128)(2,1)} %pad_maximum_fusion.refs_2_.refs_12_), channel_id=1, source_target_pairs={{0,4},{4,0},{8,12},{12,8},{16,20},{20,16},{24,28},{28,24},{1,5},{5... | collective-permute-start | bytes 3833864 | tf_op jit(solution)/shard_map/ppermute | solution.py:25
  38.5 18.0 %collective-permute-start.5 = (bf16[192,768]{1,0:T(8,128)(2,1)S(1)}, bf16[192,768]{1,0:T(8,128)(2,1)S(1)}, u32[]{:S(2)}, u32[]{:S(2)}) collective-permute-start(bf16[192,768]{1,0:T(8,128)(2,1)S(1)} %get-tuple-element.160), channel_id=1, source_target_pairs={{0,8},{4,12},{8,0},{12,4},{16,24},{20,28},{24,16},{28,20},{1,9},{5... | collective-permute-start | bytes 884744 | tf_op jit(solution)/shard_map/ppermute | solution.py:25
  45.2 23.5 %collective-permute-start.6 = (bf16[192,768]{1,0:T(8,128)(2,1)S(1)}, bf16[192,768]{1,0:T(8,128)(2,1)S(1)}, u32[]{:S(2)}, u32[]{:S(2)}) collective-permute-start(bf16[192,768]{1,0:T(8,128)(2,1)S(1)} %get-tuple-element.160), channel_id=1, source_target_pairs={{0,16},{4,20},{8,24},{12,28},{16,0},{20,4},{24,8},{28,12},{1,17},{... | collective-permute-start | bytes 884744 | tf_op jit(solution)/shard_map/ppermute | solution.py:25
  46.3 22.4 %collective-permute-start.7 = (bf16[192,768]{1,0:T(8,128)(2,1)S(1)}, bf16[192,768]{1,0:T(8,128)(2,1)S(1)}, u32[]{:S(2)}, u32[]{:S(2)}) collective-permute-start(bf16[192,768]{1,0:T(8,128)(2,1)S(1)} %get-tuple-element.160), channel_id=1, source_target_pairs={{0,24},{4,28},{8,16},{12,20},{16,8},{20,12},{24,0},{28,4},{1,25},{... | collective-permute-start | bytes 884744 | tf_op jit(solution)/shard_map/ppermute | solution.py:25
  47.7 32.0 %collective-permute-start.8 = (bf16[4,208,768]{2,1,0:T(8,128)(2,1)}, bf16[4,208,768]{2,1,0:T(8,128)(2,1)}, u32[]{:S(2)}, u32[]{:S(2)}) collective-permute-start(bf16[4,208,768]{2,1,0:T(8,128)(2,1)} %pad_maximum_fusion.refs_2_.refs_12_), channel_id=1, source_target_pairs={{0,1},{1,0},{2,3},{3,2},{4,5},{5,4},{6,7},{7,6},{8,9},{9,8},{10,11... | collective-permute-start | bytes 3833864 | tf_op jit(solution)/shard_map/ppermute | solution.py:25
  70.1 11.1 %collective-permute-start.9 = (bf16[4,208,768]{2,1,0:T(8,128)(2,1)}, bf16[4,208,768]{2,1,0:T(8,128)(2,1)}, u32[]{:S(2)}, u32[]{:S(2)}) collective-permute-start(bf16[4,208,768]{2,1,0:T(8,128)(2,1)} %collective-permute-done.4.refs_3_.refs_13_), channel_id=1, source_target_pairs={{0,1},{1,0},{2,3},{3,2},{4,5},{5,4},{6,7},{7,6},{8,9},{9,8},{10,11... | collective-permute-start | bytes 3833864 | tf_op jit(solution)/shard_map/ppermute | solution.py:25
  73.5 28.8 %collective-permute-start.10 = (bf16[4,192,768]{2,1,0:T(8,128)(2,1)}, bf16[4,192,768]{2,1,0:T(8,128)(2,1)}, u32[]{:S(2)}, u32[]{:S(2)}) collective-permute-start(bf16[4,192,768]{2,1,0:T(8,128)(2,1)} %pad_maximum_fusion.2.refs_5_.refs_7_), channel_id=1, source_target_pairs={{0,4},{4,0},{8,12},{12,8},{16,20},{20,16},{24,28},{28,24},{1,5},{5... | collective-permute-start | bytes 3538952 | tf_op jit(solution)/shard_map/ppermute | solution.py:25
  74.5 16.1 %collective-permute-start.11 = (bf16[192,768]{1,0:T(8,128)(2,1)S(1)}, bf16[192,768]{1,0:T(8,128)(2,1)}, u32[]{:S(2)}, u32[]{:S(2)}) collective-permute-start(bf16[192,768]{1,0:T(8,128)(2,1)S(1)} %get-tuple-element.168), channel_id=1, source_target_pairs={{0,8},{4,12},{8,0},{12,4},{16,24},{20,28},{24,16},{28,20},{1,9},{5... | collective-permute-start | bytes 884744 | tf_op jit(solution)/shard_map/ppermute | solution.py:25
  78.7 23.6 %collective-permute-start.12 = (bf16[192,768]{1,0:T(8,128)(2,1)S(1)}, bf16[192,768]{1,0:T(8,128)(2,1)}, u32[]{:S(2)}, u32[]{:S(2)}) collective-permute-start(bf16[192,768]{1,0:T(8,128)(2,1)S(1)} %get-tuple-element.168), channel_id=1, source_target_pairs={{0,16},{4,20},{8,24},{12,28},{16,0},{20,4},{24,8},{28,12},{1,17},{... | collective-permute-start | bytes 884744 | tf_op jit(solution)/shard_map/ppermute | solution.py:25
  79.7 22.6 %collective-permute-start.13 = (bf16[192,768]{1,0:T(8,128)(2,1)S(1)}, bf16[192,768]{1,0:T(8,128)(2,1)}, u32[]{:S(2)}, u32[]{:S(2)}) collective-permute-start(bf16[192,768]{1,0:T(8,128)(2,1)S(1)} %get-tuple-element.168), channel_id=1, source_target_pairs={{0,24},{4,28},{8,16},{12,20},{16,8},{20,12},{24,0},{28,4},{1,25},{... | collective-permute-start | bytes 884744 | tf_op jit(solution)/shard_map/ppermute | solution.py:25
  81.2 31.2 %collective-permute-start.14 = (bf16[4,192,768]{2,1,0:T(8,128)(2,1)}, bf16[4,192,768]{2,1,0:T(8,128)(2,1)}, u32[]{:S(2)}, u32[]{:S(2)}) collective-permute-start(bf16[4,192,768]{2,1,0:T(8,128)(2,1)} %pad_maximum_fusion.2.refs_5_.refs_7_), channel_id=1, source_target_pairs={{0,1},{1,0},{2,3},{3,2},{4,5},{5,4},{6,7},{7,6},{8,9},{9,8},{10,11... | collective-permute-start | bytes 3538952 | tf_op jit(solution)/shard_map/ppermute | solution.py:25
  102.3 14.3 %collective-permute-start.15 = (bf16[4,192,768]{2,1,0:T(8,128)(2,1)}, bf16[4,192,768]{2,1,0:T(8,128)(2,1)S(1)}, u32[]{:S(2)}, u32[]{:S(2)}) collective-permute-start(bf16[4,192,768]{2,1,0:T(8,128)(2,1)} %collective-permute-done.10.refs_6_.refs_8_), channel_id=1, source_target_pairs={{0,1},{1,0},{2,3},{3,2},{4,5},{5,4},{6,7},{7,6},{8,9},{9,8},{10,11... | collective-permute-start | bytes 3538952 | tf_op jit(solution)/shard_map/ppermute | solution.py:25
  103.6 30.1 %collective-permute-start.17 = (bf16[4,192,768]{2,1,0:T(8,128)(2,1)S(1)}, bf16[4,192,768]{2,1,0:T(8,128)(2,1)S(1)}, u32[]{:S(2)}, u32[]{:S(2)}) collective-permute-start(bf16[4,192,768]{2,1,0:T(8,128)(2,1)S(1)} %pad_maximum_fusion.3.refs_5_), channel_id=1, source_target_pairs={{0,4},{4,0},{8,12},{12,8},{16,20},{20,16},{24,28},{28,24},{1,5},{5... | collective-permute-start | bytes 3538952 | tf_op jit(solution)/shard_map/ppermute | solution.py:25
  105.0 28.3 %collective-permute-start.16 = (bf16[192,768]{1,0:T(8,128)(2,1)}, bf16[192,768]{1,0:T(8,128)(2,1)}, u32[]{:S(2)}, u32[]{:S(2)}) collective-permute-start(bf16[192,768]{1,0:T(8,128)(2,1)} %slice_select_fusion.refs_9_), channel_id=1, source_target_pairs={{0,8},{4,12},{8,0},{12,4},{16,24},{20,28},{24,16},{28,20},{1,9},{5... | collective-permute-start | bytes 884744 | tf_op jit(solution)/shard_map/ppermute | solution.py:25
  109.9 23.7 %collective-permute-start.18 = (bf16[192,768]{1,0:T(8,128)(2,1)}, bf16[192,768]{1,0:T(8,128)(2,1)}, u32[]{:S(2)}, u32[]{:S(2)}) collective-permute-start(bf16[192,768]{1,0:T(8,128)(2,1)} %slice_select_fusion.refs_9_), channel_id=1, source_target_pairs={{0,16},{4,20},{8,24},{12,28},{16,0},{20,4},{24,8},{28,12},{1,17},{... | collective-permute-start | bytes 884744 | tf_op jit(solution)/shard_map/ppermute | solution.py:25
  112.5 21.2 %collective-permute-start.19 = (bf16[192,768]{1,0:T(8,128)(2,1)}, bf16[192,768]{1,0:T(8,128)(2,1)}, u32[]{:S(2)}, u32[]{:S(2)}) collective-permute-start(bf16[192,768]{1,0:T(8,128)(2,1)} %slice_select_fusion.refs_9_), channel_id=1, source_target_pairs={{0,24},{4,28},{8,16},{12,20},{16,8},{20,12},{24,0},{28,4},{1,25},{... | collective-permute-start | bytes 884744 | tf_op jit(solution)/shard_map/ppermute | solution.py:25
  116.6 23.6 %collective-permute-start.23 = (bf16[4,192,768]{2,1,0:T(8,128)(2,1)S(1)}, bf16[4,192,768]{2,1,0:T(8,128)(2,1)S(1)}, u32[]{:S(2)}, u32[]{:S(2)}) collective-permute-start(bf16[4,192,768]{2,1,0:T(8,128)(2,1)S(1)} %pad_maximum_fusion.3.refs_5_), channel_id=1, source_target_pairs={{0,1},{1,0},{2,3},{3,2},{4,5},{5,4},{6,7},{7,6},{8,9},{9,8},{10,11... | collective-permute-start | bytes 3538952 | tf_op jit(solution)/shard_map/ppermute | solution.py:25
  133.7 6.5 %collective-permute-start.24 = (bf16[4,192,768]{2,1,0:T(8,128)(2,1)S(1)}, bf16[4,192,768]{2,1,0:T(8,128)(2,1)S(1)}, u32[]{:S(2)}, u32[]{:S(2)}) collective-permute-start(bf16[4,192,768]{2,1,0:T(8,128)(2,1)S(1)} %collective-permute-done.17.refs_6_), channel_id=1, source_target_pairs={{0,1},{1,0},{2,3},{3,2},{4,5},{5,4},{6,7},{7,6},{8,9},{9,8},{10,11... | collective-permute-start | bytes 3538952 | tf_op jit(solution)/shard_map/ppermute | solution.py:25
  135.4 4.8 %collective-permute-start.20 = (bf16[3,192,768]{2,1,0:T(8,128)(2,1)S(1)}, bf16[3,192,768]{2,1,0:T(8,128)(2,1)S(1)}, u32[]{:S(2)}, u32[]{:S(2)}) collective-permute-start(bf16[3,192,768]{2,1,0:T(8,128)(2,1)S(1)} %pad_maximum_fusion.6.refs_7_), channel_id=1, source_target_pairs={{0,1},{1,0},{2,3},{3,2},{4,5},{5,4},{6,7},{7,6},{8,9},{9,8},{10,11... | collective-permute-start | bytes 2654216 | tf_op jit(solution)/shard_map/ppermute | solution.py:25
  135.6 22.0 %collective-permute-start.25 = (bf16[3,192,768]{2,1,0:T(8,128)(2,1)S(1)}, bf16[3,192,768]{2,1,0:T(8,128)(2,1)}, u32[]{:S(2)}, u32[]{:S(2)}) collective-permute-start(bf16[3,192,768]{2,1,0:T(8,128)(2,1)S(1)} %pad_maximum_fusion.6.refs_7_), channel_id=1, source_target_pairs={{0,4},{4,0},{8,12},{12,8},{16,20},{20,16},{24,28},{28,24},{1,5},{5... | collective-permute-start | bytes 2654216 | tf_op jit(solution)/shard_map/ppermute | solution.py:25
  138.4 1.8 collective-permute-start.21
  157.6 2.2 collective-permute-start.26
  157.6 3.1 collective-permute-start.27
  158.1 5.5 %collective-permute-start.28 = (bf16[3,192,768]{2,1,0:T(8,128)(2,1)}, bf16[3,192,768]{2,1,0:T(8,128)(2,1)S(1)}, u32[]{:S(2)}, u32[]{:S(2)}) collective-permute-start(bf16[3,192,768]{2,1,0:T(8,128)(2,1)} %collective-permute-done.25.refs_8_), channel_id=1, source_target_pairs={{0,1},{1,0},{2,3},{3,2},{4,5},{5,4},{6,7},{7,6},{8,9},{9,8},{10,11... | collective-permute-start | bytes 2654216 | tf_op jit(solution)/shard_map/ppermute | solution.py:25
  162.3 34.5 %collective-permute-start.29 = (bf16[4,2,96,768]{3,2,1,0:T(8,128)(2,1)S(1)}, bf16[4,2,96,768]{3,2,1,0:T(8,128)(2,1)S(1)}, u32[]{:S(2)}, u32[]{:S(2)}) collective-permute-start(bf16[4,2,96,768]{3,2,1,0:T(8,128)(2,1)S(1)} %fusion.3), channel_id=1, source_target_pairs={{0,4},{4,0},{8,12},{12,8},{16,20},{20,16},{24,28},{28,24},{1,5},{5... | collective-permute-start | bytes 3538952 | tf_op jit(solution)/shard_map/ppermute | solution.py:25
  163.6 35.9 %collective-permute-start.32 = (bf16[4,2,96,768]{3,2,1,0:T(8,128)(2,1)S(1)}, bf16[4,2,96,768]{3,2,1,0:T(8,128)(2,1)S(1)}, u32[]{:S(2)}, u32[]{:S(2)}) collective-permute-start(bf16[4,2,96,768]{3,2,1,0:T(8,128)(2,1)S(1)} %copy-done.39), channel_id=1, source_target_pairs={{0,1},{1,0},{2,3},{3,2},{4,5},{5,4},{6,7},{7,6},{8,9},{9,8},{10,11... | collective-permute-start | bytes 3538952 | tf_op jit(solution)/shard_map/ppermute | solution.py:25
  196.2 2.2 collective-permute-start.30
  196.8 2.5 collective-permute-start.31
  201.0 37.3 %all-to-all-start.1 = ((bf16[4,192,768]{2,1,0:T(8,128)(2,1)}), bf16[4,192,768]{2,1,0:T(8,128)(2,1)S(1)}, u32[]{:S(2)}, u32[]{:S(2)}) async-start(bf16[4,192,768]{2,1,0:T(8,128)(2,1)} %bitcast.34), calls=%async_computation.1 | async-start | bytes 2359296 | tf_op jit(solution)/shard_map/all_to_all | solution.py:491
  209.2 28.0 %collective-permute-start.33 = (bf16[4,2,96,768]{3,2,1,0:T(8,128)(2,1)S(1)}, bf16[4,2,96,768]{3,2,1,0:T(8,128)(2,1)S(1)}, u32[]{:S(2)}, u32[]{:S(2)}) collective-permute-start(bf16[4,2,96,768]{3,2,1,0:T(8,128)(2,1)S(1)} %fusion.2), channel_id=1, source_target_pairs={{0,4},{4,0},{8,12},{12,8},{16,20},{20,16},{24,28},{28,24},{1,5},{5... | collective-permute-start | bytes 3538952 | tf_op jit(solution)/shard_map/ppermute | solution.py:25
  210.0 28.4 %collective-permute-start.34 = (bf16[4,2,96,768]{3,2,1,0:T(8,128)(2,1)}, bf16[4,2,96,768]{3,2,1,0:T(8,128)(2,1)}, u32[]{:S(2)}, u32[]{:S(2)}) collective-permute-start(bf16[4,2,96,768]{3,2,1,0:T(8,128)(2,1)} %get-tuple-element.211), channel_id=1, source_target_pairs={{0,1},{1,0},{2,3},{3,2},{4,5},{5,4},{6,7},{7,6},{8,9},{9,8},{10,11... | collective-permute-start | bytes 3538952 | tf_op jit(solution)/shard_map/ppermute | solution.py:25
  227.7 33.2 %collective-permute-start.35 = (bf16[8,64,768]{2,1,0:T(8,128)(2,1)}, bf16[8,64,768]{2,1,0:T(8,128)(2,1)}, u32[]{:S(2)}, u32[]{:S(2)}) collective-permute-start(bf16[8,64,768]{2,1,0:T(8,128)(2,1)} %get-tuple-element.220), channel_id=1, source_target_pairs={{0,1},{1,0},{2,3},{3,2},{4,5},{5,4},{6,7},{7,6},{8,9},{9,8},{10,11... | collective-permute-start | bytes 2359304 | tf_op jit(solution)/shard_map/ppermute | solution.py:25
  241.6 37.4 %all-to-all-start.2 = ((bf16[4,192,768]{2,1,0:T(8,128)(2,1)}), bf16[4,192,768]{2,1,0:T(8,128)(2,1)S(1)}, u32[]{:S(2)}, u32[]{:S(2)}) async-start(bf16[4,192,768]{2,1,0:T(8,128)(2,1)} %bitcast.35), calls=%async_computation.2 | async-start | bytes 2359296 | tf_op jit(solution)/shard_map/all_to_all | solution.py:491
  247.2 13.6 %collective-permute-start.36 = (bf16[4,64,768]{2,1,0:T(8,128)(2,1)S(1)}, bf16[4,64,768]{2,1,0:T(8,128)(2,1)S(1)}, u32[]{:S(2)}, u32[]{:S(2)}) collective-permute-start(bf16[4,64,768]{2,1,0:T(8,128)(2,1)S(1)} %get-tuple-element.286), channel_id=1, source_target_pairs={{0,2},{1,3},{2,0},{3,1},{4,6},{5,7},{6,4},{7,5},{8,10},{9,11},{10,... | collective-permute-start | bytes 1179656 | tf_op jit(solution)/shard_map/ppermute | solution.py:25
  260.9 2.3 collective-permute-start.37
  260.9 3.0 collective-permute-start.38
  261.4 19.9 %collective-permute-start.39 = (bf16[8,64,768]{2,1,0:T(8,128)(2,1)}, bf16[8,64,768]{2,1,0:T(8,128)(2,1)}, u32[]{:S(2)}, u32[]{:S(2)}) collective-permute-start(bf16[8,64,768]{2,1,0:T(8,128)(2,1)} %get-tuple-element.239), channel_id=1, source_target_pairs={{0,3},{1,2},{2,1},{3,0},{4,7},{5,6},{6,5},{7,4},{8,11},{9,10},{10,... | collective-permute-start | bytes 2359304 | tf_op jit(solution)/shard_map/ppermute | solution.py:25
  261.8 24.8 %collective-permute-start.48 = (bf16[4,2,96,768]{3,2,1,0:T(8,128)(2,1)}, bf16[4,2,96,768]{3,2,1,0:T(8,128)(2,1)}, u32[]{:S(2)}, u32[]{:S(2)}) collective-permute-start(bf16[4,2,96,768]{3,2,1,0:T(8,128)(2,1)} %get-tuple-element.255), channel_id=1, source_target_pairs={{0,1},{1,0},{2,3},{3,2},{4,5},{5,4},{6,7},{7,6},{8,9},{9,8},{10,11... | collective-permute-start | bytes 3538952 | tf_op jit(solution)/shard_map/ppermute | solution.py:25
  265.6 29.0 %collective-permute-start.49 = (bf16[4,2,96,768]{3,2,1,0:T(8,128)(2,1)S(1)}, bf16[4,2,96,768]{3,2,1,0:T(8,128)(2,1)}, u32[]{:S(2)}, u32[]{:S(2)}) collective-permute-start(bf16[4,2,96,768]{3,2,1,0:T(8,128)(2,1)S(1)} %fusion.1), channel_id=1, source_target_pairs={{0,4},{4,0},{8,12},{12,8},{16,20},{20,16},{24,28},{28,24},{1,5},{5... | collective-permute-start | bytes 3538952 | tf_op jit(solution)/shard_map/ppermute | solution.py:25
  281.3 2.2 collective-permute-start.40
  281.7 2.7 collective-permute-start.41
  285.7 34.5 %collective-permute-start.46 = (bf16[4,2,96,768]{3,2,1,0:T(8,128)(2,1)}, bf16[4,2,96,768]{3,2,1,0:T(8,128)(2,1)}, u32[]{:S(2)}, u32[]{:S(2)}) collective-permute-start(bf16[4,2,96,768]{3,2,1,0:T(8,128)(2,1)} %fusion), channel_id=1, source_target_pairs={{0,4},{4,0},{8,12},{12,8},{16,20},{20,16},{24,28},{28,24},{1,5},{5... | collective-permute-start | bytes 3538952 | tf_op jit(solution)/shard_map/ppermute | solution.py:25
  297.6 32.4 %all-to-all-start.4 = ((bf16[4,192,768]{2,1,0:T(8,128)(2,1)}), bf16[4,192,768]{2,1,0:T(8,128)(2,1)S(1)}, u32[]{:S(2)}, u32[]{:S(2)}) async-start(bf16[4,192,768]{2,1,0:T(8,128)(2,1)} %bitcast.41), calls=%async_computation.4 | async-start | bytes 2359296 | tf_op jit(solution)/shard_map/all_to_all | solution.py:491
  302.9 17.3 %collective-permute-start.43 = (bf16[4,2,96,768]{3,2,1,0:T(8,128)(2,1)S(1)}, bf16[4,2,96,768]{3,2,1,0:T(8,128)(2,1)S(1)}, u32[]{:S(2)}, u32[]{:S(2)}) collective-permute-start(bf16[4,2,96,768]{3,2,1,0:T(8,128)(2,1)S(1)} %copy-done.38), channel_id=1, source_target_pairs={{0,1},{1,0},{2,3},{3,2},{4,5},{5,4},{6,7},{7,6},{8,9},{9,8},{10,11... | collective-permute-start | bytes 3538952 | tf_op jit(solution)/shard_map/ppermute | solution.py:25
  303.7 16.4 %collective-permute-start.42 = (bf16[384,768]{1,0:T(8,128)(2,1)}, bf16[384,768]{1,0:T(8,128)(2,1)}, u32[]{:S(2)}, u32[]{:S(2)}) collective-permute-start(bf16[384,768]{1,0:T(8,128)(2,1)} %pad_maximum_fusion.9), channel_id=1, source_target_pairs={{0,2},{1,3},{2,0},{3,1},{4,6},{5,7},{6,4},{7,5},{8,10},{9,11},{10,... | collective-permute-start | bytes 1769480 | tf_op jit(solution)/shard_map/ppermute | solution.py:25
  305.8 14.4 %collective-permute-start.45 = (bf16[16,768]{1,0:T(8,128)(2,1)S(1)}, bf16[16,768]{1,0:T(8,128)(2,1)S(1)}, u32[]{:S(2)}, u32[]{:S(2)}) collective-permute-start(bf16[16,768]{1,0:T(8,128)(2,1)S(1)} %add_convert_fusion.5), channel_id=1, source_target_pairs={{0,4},{4,0},{8,12},{12,8},{16,20},{20,16},{24,28},{28,24},{1,5},{5... | collective-permute-start | bytes 73736 | tf_op jit(solution)/shard_map/ppermute | solution.py:25
  307.5 27.1 %collective-permute-start.54 = (bf16[4,64,768]{2,1,0:T(8,128)(2,1)}, bf16[4,64,768]{2,1,0:T(8,128)(2,1)}, u32[]{:S(2)}, u32[]{:S(2)}) collective-permute-start(bf16[4,64,768]{2,1,0:T(8,128)(2,1)} %get-tuple-element.285), channel_id=1, source_target_pairs={{0,2},{1,3},{2,0},{3,1},{4,6},{5,7},{6,4},{7,5},{8,10},{9,11},{10,... | collective-permute-start | bytes 1179656 | tf_op jit(solution)/shard_map/ppermute | solution.py:25
  323.1 15.0 %collective-permute-start.51 = (bf16[8,32,768]{2,1,0:T(8,128)(2,1)}, bf16[8,32,768]{2,1,0:T(8,128)(2,1)}, u32[]{:S(2)}, u32[]{:S(2)}) collective-permute-start(bf16[8,32,768]{2,1,0:T(8,128)(2,1)} %get-tuple-element.257.refs_4_), channel_id=1, source_target_pairs={{0,2},{1,3},{2,0},{3,1},{4,6},{5,7},{6,4},{7,5},{8,10},{9,11},{10,... | collective-permute-start | bytes 1179656 | tf_op jit(solution)/shard_map/ppermute | solution.py:25
  323.8 22.2 %collective-permute-start.52 = (bf16[384,768]{1,0:T(8,128)(2,1)}, bf16[384,768]{1,0:T(8,128)(2,1)}, u32[]{:S(2)}, u32[]{:S(2)}) collective-permute-start(bf16[384,768]{1,0:T(8,128)(2,1)} %pad_maximum_fusion.9), channel_id=1, source_target_pairs={{0,1},{1,0},{2,3},{3,2},{4,5},{5,4},{6,7},{7,6},{8,9},{9,8},{10,11... | collective-permute-start | bytes 1769480 | tf_op jit(solution)/shard_map/ppermute | solution.py:25
  323.8 22.2 %collective-permute-start.53 = (bf16[384,768]{1,0:T(8,128)(2,1)}, bf16[384,768]{1,0:T(8,128)(2,1)}, u32[]{:S(2)}, u32[]{:S(2)}) collective-permute-start(bf16[384,768]{1,0:T(8,128)(2,1)} %collective-permute-done.42), channel_id=1, source_target_pairs={{0,1},{1,0},{2,3},{3,2},{4,5},{5,4},{6,7},{7,6},{8,9},{9,8},{10,11... | collective-permute-start | bytes 1769480 | tf_op jit(solution)/shard_map/ppermute | solution.py:25
  330.1 33.8 %all-to-all-start.3 = ((bf16[4,208,768]{2,1,0:T(8,128)(2,1)}), bf16[4,208,768]{2,1,0:T(8,128)(2,1)S(1)}, u32[]{:S(2)}, u32[]{:S(2)}) async-start(bf16[4,208,768]{2,1,0:T(8,128)(2,1)} %pad_maximum_fusion.1), calls=%async_computation.3 | async-start | bytes 2555904 | tf_op jit(solution)/shard_map/all_to_all | solution.py:491
  333.8 11.1 %collective-permute-start.47 = (bf16[8,32,768]{2,1,0:T(8,128)(2,1)S(1)}, bf16[8,32,768]{2,1,0:T(8,128)(2,1)S(1)}, u32[]{:S(2)}, u32[]{:S(2)}) collective-permute-start(bf16[8,32,768]{2,1,0:T(8,128)(2,1)S(1)} %copy-done.7), channel_id=1, source_target_pairs={{0,2},{1,3},{2,0},{3,1},{4,6},{5,7},{6,4},{7,5},{8,10},{9,11},{10,... | collective-permute-start | bytes 1179656 | tf_op jit(solution)/shard_map/ppermute | solution.py:25
  350.1 8.1 %collective-permute-start.50 = (bf16[192,768]{1,0:T(8,128)(2,1)S(1)}, bf16[192,768]{1,0:T(8,128)(2,1)S(1)}, u32[]{:S(2)}, u32[]{:S(2)}) collective-permute-start(bf16[192,768]{1,0:T(8,128)(2,1)S(1)} %reduce_sum.44), channel_id=1, source_target_pairs={{0,2},{1,3},{2,0},{3,1},{4,6},{5,7},{6,4},{7,5},{8,10},{9,11},{10,... | collective-permute-start | bytes 884744 | tf_op jit(solution)/shard_map/ppermute | solution.py:25
  364.3 2.1 collective-permute-start.61
  364.8 4.5 %collective-permute-start.56 = (bf16[2,8,32,768]{3,2,1,0:T(8,128)(2,1)}, bf16[2,8,32,768]{3,2,1,0:T(8,128)(2,1)S(1)}, u32[]{:S(2)}, u32[]{:S(2)}) collective-permute-start(bf16[2,8,32,768]{3,2,1,0:T(8,128)(2,1)} %pad_maximum_fusion.8), channel_id=1, source_target_pairs={{0,1},{1,0},{2,3},{3,2},{4,5},{5,4},{6,7},{7,6},{8,9},{9,8},{10,11... | collective-permute-start | bytes 2359304 | tf_op jit(solution)/shard_map/ppermute | solution.py:25
  364.9 4.5 %collective-permute-start.55 = (bf16[2,8,32,768]{3,2,1,0:T(8,128)(2,1)}, bf16[2,8,32,768]{3,2,1,0:T(8,128)(2,1)}, u32[]{:S(2)}, u32[]{:S(2)}) collective-permute-start(bf16[2,8,32,768]{3,2,1,0:T(8,128)(2,1)} %pad_maximum_fusion.7), channel_id=1, source_target_pairs={{0,1},{1,0},{2,3},{3,2},{4,5},{5,4},{6,7},{7,6},{8,9},{9,8},{10,11... | collective-permute-start | bytes 2359304 | tf_op jit(solution)/shard_map/ppermute | solution.py:25
  365.3 9.5 %collective-permute-start.57 = (bf16[208,768]{1,0:T(8,128)(2,1)S(1)}, bf16[208,768]{1,0:T(8,128)(2,1)S(1)}, u32[]{:S(2)}, u32[]{:S(2)}) collective-permute-start(bf16[208,768]{1,0:T(8,128)(2,1)S(1)} %reduce_sum.45), channel_id=1, source_target_pairs={{0,2},{1,3},{2,0},{3,1},{4,6},{5,7},{6,4},{7,5},{8,10},{9,11},{10,... | collective-permute-start | bytes 958472 | tf_op jit(solution)/shard_map/ppermute | solution.py:25
  374.9 2.1 collective-permute-start.58
  375.0 2.0 collective-permute-start.59
  (45 other events, 421.3 us)
